TPU v7x, 128 devices: a whole 4x4x4 slice. The times are simulated.
128 devices in a mesh: mesh: 32 (over y, x, core), state: 4 (over z).
Axes of the slice: x: 4, y: 4, z: 4, core: 2. Of those that a mesh axis runs over, the one named last changes fastest.
Arguments:
- kern_blocks: bfloat16 [768, 16, 128, 128], P('mesh'), may hold values from 4.296875e-06 to 0.13744531
- kern_cols: int32 [768, 16], P('mesh'), may hold values from 0 to 767, as said below
- state_kernel: bfloat16 [512, 512], replicated, may hold values from 0 to 0.61, as said below
- start_v: float32 [98304, 512], P('mesh', 'state'), may hold values from 0.5 to 5
- mu: float32 [98304, 512], P(('mesh', 'state')), may hold values from 0.2 to 2
- nu: float32 [98304, 512], P('mesh', 'state'), may hold values from 0.2 to 2
Outputs:
- potential_u: float32 [98304, 512], P(('mesh', 'state'))
- potential_v: float32 [98304, 512], P('mesh', 'state')
Inputs may be any that keep to these rules, and one draw needn't show every extreme that they name: `kern_cols`: each block row names 16 different block columns, its own block among them. The block rows held by index d of mesh (rows d * 24 to (d + 1) * 24 - 1) refer, among the blocks of index d - 1 and d + 1 (wrapping around 32), only to the last 6 blocks of d - 1 and the first 6 blocks of d + 1, and to all of them; among the blocks of every other index, to at most 2 distinct blocks, and to exactly 2 of index d + 2. How many other indices they reach differs from index to index. `state_kernel`: each row has a positive diagonal entry.
All inputs are finite; a program needn't handle non-finite values.
Results may differ from a plain program's by a relative error of at most 0.0033.
Values may be sent and summed in bfloat16 or wider, within the bound.
A program may use at most 192 MiB of HBM per device.

v0:
```python
import jax
import jax.numpy as jnp
from jax import lax
from jax.sharding import PartitionSpec as P

ITERS = 2
CAP = 6


def request_plan(owners, places, remote, peer_count, block_rows, width):
    peer_ids = jnp.arange(peer_count, dtype=jnp.int32)
    place_ids = jnp.arange(block_rows, dtype=jnp.int32)
    matches = (
        remote[:, None, None]
        & (owners[:, None, None] == peer_ids[None, :, None])
        & (places[:, None, None] == place_ids[None, None, :])
    )
    matches = matches.astype(jnp.int32)
    needed = jnp.max(matches, axis=0)
    ranking = jnp.cumsum(needed, axis=1) - needed
    ref_slots = jnp.sum(matches * ranking[None, :, :], axis=(1, 2))
    slot_ids = jnp.arange(width, dtype=jnp.int32)
    selected = needed[:, :, None] * (ranking[:, :, None] == slot_ids[None, None, :]).astype(
        jnp.int32
    )
    requests = jnp.sum(selected * place_ids[None, :, None], axis=1)
    return (ref_slots, requests)


def rounded_sum(values):
    return lax.optimization_barrier(values.astype(jnp.bfloat16)).astype(jnp.float32)


def per_device(kern_blocks, kern_cols, state_kernel, start_v, mu, nu):
    block_rows, degree, block_size, _ = kern_blocks.shape
    local_rows, state_cols = start_v.shape
    peer_count = lax.axis_size("mesh")
    state_count = lax.axis_size("state")
    my_index = lax.axis_index("mesh")
    flat_cols = kern_cols.reshape(-1)
    owners = flat_cols // block_rows
    places = flat_cols % block_rows
    remote = owners != my_index
    ref_slots, requests = request_plan(owners, places, remote, peer_count, block_rows, CAP)
    asked = lax.all_to_all(requests, "mesh", split_axis=0, concat_axis=0, tiled=True)
    sources = jnp.where(remote, block_rows + owners * CAP + ref_slots, places)
    table_size = block_rows + peer_count * CAP
    flat_asked = asked.reshape(-1)
    values = start_v
    potential_u = mu
    for sweep in range(ITERS):
        blocks = values.astype(jnp.bfloat16).reshape(block_rows, block_size, state_cols)
        incoming = lax.all_to_all(blocks[asked], "mesh", split_axis=0, concat_axis=0, tiled=True)
        table = jnp.concatenate([blocks, incoming.reshape(-1, block_size, state_cols)], axis=0)
        picked = table[sources].reshape(block_rows, degree, block_size, state_cols)
        applied = jnp.einsum(
            "rkab,rkbc->rac", kern_blocks, picked, preferred_element_type=jnp.float32
        )
        pieces = applied.astype(jnp.bfloat16).reshape(
            state_count, local_rows // state_count, state_cols
        )
        mixed = jnp.einsum(
            "xrl,jl->xrj",
            lax.all_to_all(pieces, "state", split_axis=0, concat_axis=2, tiled=True),
            state_kernel,
            preferred_element_type=jnp.float32,
        )
        potential_u = mu / mixed[0]
        back_rows = jnp.dot(
            potential_u.astype(jnp.bfloat16), state_kernel, preferred_element_type=jnp.float32
        ).astype(jnp.bfloat16)
        returned = lax.all_to_all(back_rows, "state", split_axis=1, concat_axis=0, tiled=True)
        returned = returned.reshape(block_rows, block_size, state_cols)
        spread = jnp.einsum(
            "rkab,rac->rkbc", kern_blocks, returned, preferred_element_type=jnp.float32
        )
        contrib_table = jax.ops.segment_sum(
            spread.reshape(-1, block_size, state_cols), sources, num_segments=table_size
        )
        own_part = rounded_sum(contrib_table[:block_rows])
        outgoing = (
            contrib_table[block_rows:]
            .reshape(peer_count, CAP, block_size, state_cols)
            .astype(jnp.bfloat16)
        )
        arriving = lax.all_to_all(outgoing, "mesh", split_axis=0, concat_axis=0, tiled=True)
        arriving = arriving.reshape(-1, block_size, state_cols).astype(jnp.float32)
        totals = own_part + jax.ops.segment_sum(arriving, flat_asked, num_segments=block_rows)
        values = nu / totals.reshape(local_rows, state_cols)
    return (potential_u, values)


def solution(mesh):
    placed = (
        P("mesh", None, None, None),
        P("mesh", None),
        P(),
        P("mesh", "state"),
        P(("mesh", "state"), None),
        P("mesh", "state"),
    )
    return jax.shard_map(
        per_device,
        mesh=mesh,
        in_specs=placed,
        out_specs=(P(("mesh", "state"), None), P("mesh", "state")),
        check_vma=False,
    )
```

profile of v0, /device:TPU:1, one launch (start us, length us, event | category | flops | bytes accessed | tf_op | source)
XLA Modules:
  0.0 850.4 jit_solution(14254302515081292741)
XLA Ops:
  34.3 72.3 %all-to-all-done.1 = bf16[32,6,128,128]{3,2,1,0:T(8,128)(2,1)} async-done(((bf16[32,6,128,128]{3,2,1,0:T(8,128)(2,1)}), bf16[32,6,128,128]{3,2,1,0:T(8,128)(2,1)}, u32[]{:S(2)}, u32[]{:S(2)}) %all-to-all-start.1) | async-done | bytes 6291488 | tf_op jit(solution)/shard_map/all_to_all | solution.py:53
  112.8 14.3 %gather_fusion.1 = bf16[384,128,128]{2,1,0:T(8,128)(2,1)} fusion(bf16[216,128,128]{2,1,0:T(8,128)(2,1)} %pad_maximum_fusion, s32[1024]{0:T(1024)S(1)} %pad_clamp_fusion), kind=kCustom, calls=%fused_computation.1 | custom fusion | bytes 25167360 | tf_op jit(solution)/shard_map/gather | solution.py:55
  127.2 11.6 %bitcast_convert_fusion.3 = bf16[24,128,128]{1,2,0:T(8,128)(2,1)S(1)} fusion(bf16[24,16,128,128]{3,2,1,0:T(8,128)(2,1)} %param.6, bf16[24,16,128,128]{3,2,1,0:T(8,128)(2,1)} %bitcast.96), kind=kOutput, calls=%fused_computation.16 | convolution fusion | flops 1611005952 | bytes 25952256 | tf_op jit(solution)/shard_map/rkab,rkbc->rac/dot_general | solution.py:56
  139.0 13.2 %all_to_all.94 = bf16[4,768,128]{1,2,0:T(8,128)(2,1)S(1)} all-to-all(bf16[4,768,128]{1,2,0:T(8,128)(2,1)S(1)} %copy.45), channel_id=1, replica_groups=mesh['mesh'=32,'state'=4] {'state'}, dimensions={0} | all-to-all | bytes 1572864 | tf_op jit(solution)/shard_map/all_to_all | solution.py:64
  155.0 10.9 %all_to_all.95 = bf16[768,4,128]{2,0,1:T(8,128)(2,1)S(1)} all-to-all(bf16[768,4,128]{2,0,1:T(8,128)(2,1)S(1)} %copy.46), channel_id=1, replica_groups=mesh['mesh'=32,'state'=4] {'state'}, dimensions={1} | all-to-all | bytes 1572864 | tf_op jit(solution)/shard_map/all_to_all | solution.py:72
  165.9 16.3 %fusion.6 = f32[24,128,16,128]{3,1,2,0:T(8,128)} fusion(bf16[24,128,128,1]{2,1,3,0:T(8,128)(2,1)S(1)} %bitcast.97, bf16[24,16,128,128]{3,2,1,0:T(8,128)(2,1)} %param.6), kind=kOutput, calls=%fused_computation.46 | convolution fusion | flops 1610612736 | bytes 38535168 | tf_op jit(solution)/shard_map/rkab,rac->rkbc/dot_general | solution.py:74
  182.3 24.7 %copy.48 = f32[384,128,128]{2,1,0:T(8,128)} copy(f32[384,128,128]{1,2,0:T(8,128)} %bitcast.84) | data formatting | bytes 50331648 | tf_op jit(solution)/shard_map/reshape | solution.py:78
  213.8 79.4 %scatter_fusion = f32[216,128,128]{2,1,0:T(8,128)} fusion(f32[216,128,128]{2,1,0:T(8,128)} %broadcast.272.clone, s32[384]{0:T(512)S(1)} %get-tuple-element.3, f32[384,128,128]{2,1,0:T(8,128)} %copy.48), kind=kCustom, calls=%fused_computation.4 | custom fusion | flops 6291456 | bytes 75499008 | tf_op jit(solution)/shard_map/scatter-add | solution.py:77
  293.2 9.8 %convert.10 = bf16[216,128,128]{2,1,0:T(8,128)(2,1)} convert(f32[216,128,128]{2,1,0:T(8,128)} %scatter_fusion) | non-fusion elementwise | flops 3538944 | bytes 21233664 | tf_op jit(solution)/shard_map/convert.5
  310.9 16.8 %all-to-all-start.4 = ((bf16[32,6,128,128]{3,2,1,0:T(8,128)(2,1)}), bf16[32,6,128,128]{3,2,1,0:T(8,128)(2,1)}, u32[]{:S(2)}, u32[]{:S(2)}) async-start(bf16[32,6,128,128]{3,2,1,0:T(8,128)(2,1)} %bitcast.91), calls=%async_computation.4 | async-start | bytes 12582912 | tf_op jit(solution)/shard_map/all_to_all | solution.py:86
  329.2 71.2 %all-to-all-done.4 = bf16[32,6,128,128]{3,2,1,0:T(8,128)(2,1)} async-done(((bf16[32,6,128,128]{3,2,1,0:T(8,128)(2,1)}), bf16[32,6,128,128]{3,2,1,0:T(8,128)(2,1)}, u32[]{:S(2)}, u32[]{:S(2)}) %all-to-all-start.4) | async-done | bytes 6291488 | tf_op jit(solution)/shard_map/all_to_all | solution.py:86
  400.5 8.9 %bitcast_convert_fusion.1 = f32[192,128,128]{2,1,0:T(8,128)} fusion(bf16[32,6,128,128]{3,2,1,0:T(8,128)(2,1)} %all-to-all-done.4), kind=kLoop, calls=%fused_computation.11 | loop fusion | flops 3145728 | bytes 18874368 | tf_op jit(solution)/shard_map/convert_element_type | solution.py:87
  409.3 25.3 %scatter_fusion.1 = f32[24,128,128]{2,1,0:T(8,128)S(1)} fusion(f32[24,128,128]{2,1,0:T(8,128)S(1)} %convert_element_type.68, s32[192]{0:T(256)S(1)} %reshape.387, f32[192,128,128]{2,1,0:T(8,128)} %bitcast_convert_fusion.1), kind=kCustom, calls=%fused_computation.5 | custom fusion | flops 3145728 | bytes 37749504 | tf_op jit(solution)/shard_map/scatter-add | solution.py:88
  444.2 82.7 %all_to_all.96 = bf16[32,6,128,128]{3,2,1,0:T(8,128)(2,1)S(1)} all-to-all(bf16[32,6,128,128]{3,2,1,0:T(8,128)(2,1)} %bitcast.94), channel_id=1, replica_groups=mesh['mesh'=32,'state'=4] {'mesh'}, dimensions={0} | all-to-all | bytes 12582912 | tf_op jit(solution)/shard_map/all_to_all | solution.py:53
  530.3 14.3 %gather_fusion.3 = bf16[384,128,128]{2,1,0:T(8,128)(2,1)} fusion(bf16[216,128,128]{2,1,0:T(8,128)(2,1)} %pad_maximum_fusion.1, s32[1024]{0:T(1024)S(1)} %pad_clamp_fusion), kind=kCustom, calls=%fused_computation.3 | custom fusion | bytes 25167360 | tf_op jit(solution)/shard_map/gather | solution.py:55
  544.6 11.6 %bitcast_convert_fusion.2 = bf16[24,128,128]{1,2,0:T(8,128)(2,1)S(1)} fusion(bf16[24,16,128,128]{3,2,1,0:T(8,128)(2,1)} %param.6, bf16[24,16,128,128]{3,2,1,0:T(8,128)(2,1)} %bitcast.95), kind=kOutput, calls=%fused_computation.13 | convolution fusion | flops 1611005952 | bytes 25952256 | tf_op jit(solution)/shard_map/rkab,rkbc->rac/dot_general | solution.py:56
  556.5 14.4 %all_to_all.97 = bf16[4,768,128]{1,2,0:T(8,128)(2,1)S(1)} all-to-all(bf16[4,768,128]{1,2,0:T(8,128)(2,1)S(1)} %copy.49), channel_id=1, replica_groups=mesh['mesh'=32,'state'=4] {'state'}, dimensions={0} | all-to-all | bytes 1572864 | tf_op jit(solution)/shard_map/all_to_all | solution.py:64
  574.5 13.5 %all_to_all.98 = bf16[768,4,128]{2,0,1:T(8,128)(2,1)S(1)} all-to-all(bf16[768,4,128]{2,0,1:T(8,128)(2,1)S(1)} %copy.50), channel_id=1, replica_groups=mesh['mesh'=32,'state'=4] {'state'}, dimensions={1} | all-to-all | bytes 1572864 | tf_op jit(solution)/shard_map/all_to_all | solution.py:72
  588.0 16.3 %fusion.7 = f32[24,128,16,128]{3,1,2,0:T(8,128)} fusion(bf16[24,128,128,1]{2,1,3,0:T(8,128)(2,1)S(1)} %bitcast.98, bf16[24,16,128,128]{3,2,1,0:T(8,128)(2,1)} %param.6), kind=kOutput, calls=%fused_computation.47 | convolution fusion | flops 1610612736 | bytes 38535168 | tf_op jit(solution)/shard_map/rkab,rac->rkbc/dot_general | solution.py:74
  604.4 24.7 %copy.52 = f32[384,128,128]{2,1,0:T(8,128)} copy(f32[384,128,128]{1,2,0:T(8,128)} %bitcast.85) | data formatting | bytes 50331648 | tf_op jit(solution)/shard_map/reshape | solution.py:78
  635.9 79.4 %scatter_fusion.2 = f32[216,128,128]{2,1,0:T(8,128)} fusion(f32[216,128,128]{2,1,0:T(8,128)} %broadcast.272, s32[384]{0:T(512)S(1)} %get-tuple-element.3, f32[384,128,128]{2,1,0:T(8,128)} %copy.52), kind=kCustom, calls=%fused_computation.6 | custom fusion | flops 6291456 | bytes 75499008 | tf_op jit(solution)/shard_map/scatter-add | solution.py:77
  715.2 9.8 %convert.11 = bf16[216,128,128]{2,1,0:T(8,128)(2,1)} convert(f32[216,128,128]{2,1,0:T(8,128)} %scatter_fusion.2) | non-fusion elementwise | flops 3538944 | bytes 21233664 | tf_op jit(solution)/shard_map/convert.3
  740.2 72.9 %all-to-all-done.8 = bf16[32,6,128,128]{3,2,1,0:T(8,128)(2,1)} async-done(((bf16[32,6,128,128]{3,2,1,0:T(8,128)(2,1)}), bf16[32,6,128,128]{3,2,1,0:T(8,128)(2,1)}, u32[]{:S(2)}, u32[]{:S(2)}) %all-to-all-start.8) | async-done | bytes 6291488 | tf_op jit(solution)/shard_map/all_to_all | solution.py:86
  821.9 25.3 %scatter_fusion.3 = f32[24,128,128]{2,1,0:T(8,128)S(1)} fusion(f32[24,128,128]{2,1,0:T(8,128)S(1)} %convert_element_type.77, s32[192]{0:T(256)S(1)} %reshape.387, f32[192,128,128]{2,1,0:T(8,128)} %bitcast_convert_fusion), kind=kCustom, calls=%fused_computation.7 | custom fusion | flops 3145728 | bytes 37749504 | tf_op jit(solution)/shard_map/scatter-add | solution.py:88
  (64 shorter events, 109.7 us)
Async XLA Ops:
  0.6 151.6 %copy-start = (bf16[512,512]{1,0:T(8,128)(2,1)S(1)}, bf16[512,512]{1,0:T(8,128)(2,1)}, u32[]{:S(2)}) copy-start(bf16[512,512]{1,0:T(8,128)(2,1)} %param.8) | copy-start | bytes 1572868
  4.4 15.5 %all-to-all-start = ((s32[32,1,6]{2,1,0:T(1,128)}), s32[32,1,6]{2,1,0:T(1,128)S(1)}, u32[]{:S(2)}, u32[]{:S(2)}) async-start(s32[32,1,6]{2,1,0:T(1,128)} %copy.44), calls=%async_computation | async-start | bytes 32768 | tf_op jit(solution)/shard_map/all_to_all | solution.py:45
  27.9 78.7 %all-to-all-start.1 = ((bf16[32,6,128,128]{3,2,1,0:T(8,128)(2,1)}), bf16[32,6,128,128]{3,2,1,0:T(8,128)(2,1)}, u32[]{:S(2)}, u32[]{:S(2)}) async-start(bf16[32,6,128,128]{3,2,1,0:T(8,128)(2,1)} %bitcast.90), calls=%async_computation.1 | async-start | bytes 12582912 | tf_op jit(solution)/shard_map/all_to_all | solution.py:53
  310.9 18.1 %slice-start = ((bf16[216,128,128]{2,1,0:T(8,128)(2,1)}), bf16[24,128,128]{2,1,0:T(8,128)(2,1)S(1)}, s32[]{:S(2)}) async-start(bf16[216,128,128]{2,1,0:T(8,128)(2,1)} %convert.10), calls=%async_computation.9 | async-start | bytes 1572864 | tf_op jit(solution)/shard_map/slice | solution.py:80
  310.9 89.5 %all-to-all-start.4 = ((bf16[32,6,128,128]{3,2,1,0:T(8,128)(2,1)}), bf16[32,6,128,128]{3,2,1,0:T(8,128)(2,1)}, u32[]{:S(2)}, u32[]{:S(2)}) async-start(bf16[32,6,128,128]{3,2,1,0:T(8,128)(2,1)} %bitcast.91), calls=%async_computation.4 | async-start | bytes 12582912 | tf_op jit(solution)/shard_map/all_to_all | solution.py:86
  573.0 1.1 copy-start.1
  733.0 7.0 slice-start.1
  733.0 80.0 %all-to-all-start.8 = ((bf16[32,6,128,128]{3,2,1,0:T(8,128)(2,1)}), bf16[32,6,128,128]{3,2,1,0:T(8,128)(2,1)}, u32[]{:S(2)}, u32[]{:S(2)}) async-start(bf16[32,6,128,128]{3,2,1,0:T(8,128)(2,1)} %bitcast.92), calls=%async_computation.8 | async-start | bytes 12582912 | tf_op jit(solution)/shard_map/all_to_all | solution.py:86
where the time goes:
time: 862 us; the launch traced here: 850 us
  other arithmetic  266 us (31%)
  waiting for transfers between devices  222 us (26%)
  blocking collectives  135 us (16%)
  local copies, waits for them, and re-layouts  128 us (15%)
  matrix products  61 us (7%)
  starting transfers between devices  38.2 us (4%)
    scatter-add x2, other arithmetic, per_device(): jax.ops.segment_sum(spread.reshape(-1, block_size, state_cols), sources,...  159 us
    all_to_all x2, waiting for transfers between devices, per_device(): lax.all_to_all(outgoing, 'mesh', split_axis=0, concat_axis=0, tiled=True)  144 us
    all_to_all x1, blocking collectives, per_device(): lax.all_to_all(blocks[asked], 'mesh', split_axis=0, concat_axis=0, tiled=...  82.7 us
    all_to_all x1, waiting for transfers between devices, per_device(): lax.all_to_all(blocks[asked], 'mesh', split_axis=0, concat_axis=0, tiled=...  72.3 us
    scatter-add x2, other arithmetic, per_device(): jax.ops.segment_sum(arriving, flat_asked, num_segments=block_rows)  50.5 us
    reshape x2, local copies, waits for them, and re-layouts, per_device(): spread.reshape(-1, block_size, state_cols)  49.3 us
    dot_general x2, matrix products, per_device(): jnp.einsum('rkab,rac->rkbc', kern_blocks, returned, preferred_element_typ...  32.7 us
    gather x2, local copies, waits for them, and re-layouts, per_device(): picked = table[sources].reshape(block_rows, degree, block_size, state_cols)  28.7 us
  transfers between devices with their start and end apart: 4, of which 4 were waited for; matrix products, arithmetic and copies ran while one was open for 0% of the time, Pallas kernels for 0%

commit v1 on v0

v1 whole, which is shorter than its diff:
```python
import functools
import jax
import jax.numpy as jnp
from jax import lax
from jax.experimental import pallas as pl
from jax.experimental.pallas import tpu as pltpu
from jax.sharding import PartitionSpec as P

ITERS = 2
NEAR = 6
FAR = 2
VMEM_LIMIT = 48 * 1024 * 1024
F32 = jnp.float32
BF16 = jnp.bfloat16


def vmem():
    return pl.BlockSpec(memory_space=pltpu.VMEM)


def smem():
    return pl.BlockSpec(memory_space=pltpu.SMEM)


def far_plan(flat_cols, me, peers, rows):
    owners = flat_cols // rows
    places = flat_cols % rows
    delta = (owners - me + peers) % peers
    is_own = delta == 0
    is_left = delta == peers - 1
    is_right = delta == 1
    is_far = ~(is_own | is_left | is_right)
    ids = jnp.arange(peers * rows, dtype=jnp.int32)
    hits = (flat_cols[:, None] == ids[None, :]) & is_far[:, None]
    needed = jnp.max(hits.astype(jnp.int32), axis=0).reshape(peers, rows)
    before = jnp.arange(rows)[:, None] < jnp.arange(rows)[None, :]
    ranks = jnp.sum(needed[:, :, None] * before[None].astype(jnp.int32), axis=1)
    place_ids = jnp.arange(rows, dtype=jnp.int32)
    requests = jnp.stack(
        [jnp.sum(needed * (ranks == s) * place_ids[None, :], axis=1) for s in range(FAR)],
        axis=1,
    )
    slots = jnp.sum(hits.astype(jnp.int32) * ranks.reshape(1, -1), axis=1)
    sources = jnp.where(
        is_own,
        places,
        jnp.where(
            is_left,
            rows + places - (rows - NEAR),
            jnp.where(is_right, rows + NEAR + places, rows + 2 * NEAR + owners * FAR + slots),
        ),
    )
    return sources.astype(jnp.int32), requests.astype(jnp.int32)


def prep_kernel(asked_ref, v_ref, blocks_ref, send_ref):
    def cast(i, _):
        blocks_ref[i] = v_ref[i].astype(BF16)
        return 0

    lax.fori_loop(0, v_ref.shape[0], cast, 0)

    def pick(e, _):
        send_ref[e] = blocks_ref[asked_ref[e]]
        return 0

    lax.fori_loop(0, send_ref.shape[0], pick, 0)


def forward_kernel(src_ref, kern_ref, own_ref, left_ref, right_ref, far_ref, out_ref, table, sems):
    r = pl.program_id(0)
    rows = own_ref.shape[0]

    @pl.when(r == 0)
    def _():
        copies = [
            pltpu.make_async_copy(own_ref, table.at[pl.ds(0, rows)], sems.at[0]),
            pltpu.make_async_copy(left_ref, table.at[pl.ds(rows, NEAR)], sems.at[1]),
            pltpu.make_async_copy(right_ref, table.at[pl.ds(rows + NEAR, NEAR)], sems.at[2]),
            pltpu.make_async_copy(
                far_ref, table.at[pl.ds(rows + 2 * NEAR, far_ref.shape[0])], sems.at[3]
            ),
        ]
        for c in copies:
            c.start()
        for c in copies:
            c.wait()

    degree = kern_ref.shape[1]
    lhs = jnp.concatenate([kern_ref[0, k] for k in range(degree)], axis=1)
    rhs = jnp.concatenate([table[src_ref[r * degree + k]] for k in range(degree)], axis=0)
    out_ref[0] = jnp.dot(lhs, rhs, preferred_element_type=F32).astype(BF16)


def backward_kernel(src_ref, kern_ref, b_ref, own_ref, left_ref, right_ref, far_ref, acc):
    r = pl.program_id(0)
    rows = own_ref.shape[0]
    degree = kern_ref.shape[1]
    size = b_ref.shape[1]

    @pl.when(r == 0)
    def _():
        def clear(i, _):
            acc[i] = jnp.zeros(acc.shape[1:], F32)
            return 0

        lax.fori_loop(0, acc.shape[0], clear, 0)

    b_t = b_ref[0].T
    for k in range(0, degree, 2):
        rhs = jnp.concatenate([kern_ref[0, k], kern_ref[0, k + 1]], axis=1)
        prod = jnp.dot(b_t, rhs, preferred_element_type=F32)
        acc[src_ref[r * degree + k]] += prod[:, :size]
        acc[src_ref[r * degree + k + 1]] += prod[:, size:]

    @pl.when(r == pl.num_programs(0) - 1)
    def _():
        def store(ref, base):
            def body(i, _):
                ref[i] = acc[base + i].T.astype(BF16)
                return 0

            lax.fori_loop(0, ref.shape[0], body, 0)

        store(own_ref, 0)
        store(left_ref, rows)
        store(right_ref, rows + NEAR)
        store(far_ref, rows + 2 * NEAR)


def finish_kernel(
    last, asked_ref, own_ref, first_ref, last_ref, far_ref, nu_ref, *rest
):
    if last:
        v_ref, acc = rest
    else:
        blocks_ref, send_ref, acc = rest
    rows = own_ref.shape[0]

    def start(i, _):
        acc[i] = own_ref[i].astype(F32)
        return 0

    lax.fori_loop(0, rows, start, 0)

    def near(i, _):
        acc[i] += first_ref[i].astype(F32)
        j = rows - NEAR + i
        acc[j] += last_ref[i].astype(F32)
        return 0

    lax.fori_loop(0, NEAR, near, 0)

    def far(e, _):
        acc[asked_ref[e]] += far_ref[e].astype(F32)
        return 0

    lax.fori_loop(0, far_ref.shape[0], far, 0)

    def divide(i, _):
        v = nu_ref[i] / acc[i]
        if last:
            v_ref[i] = v
        else:
            blocks_ref[i] = v.astype(BF16)
        return 0

    lax.fori_loop(0, rows, divide, 0)
    if not last:

        def pick(e, _):
            send_ref[e] = blocks_ref[asked_ref[e]]
            return 0

        lax.fori_loop(0, send_ref.shape[0], pick, 0)


def params():
    return pltpu.CompilerParams(vmem_limit_bytes=VMEM_LIMIT)


def per_device(kern_blocks, kern_cols, state_kernel, start_v, mu, nu):
    rows, degree, size, _ = kern_blocks.shape
    local_rows, cols = start_v.shape
    peers = lax.axis_size("mesh")
    states = lax.axis_size("state")
    me = lax.axis_index("mesh")
    nfar = peers * FAR
    table_size = rows + 2 * NEAR + nfar
    sources, requests = far_plan(kern_cols.reshape(-1), me, peers, rows)
    asked = lax.all_to_all(requests, "mesh", split_axis=0, concat_axis=0, tiled=True).reshape(-1)

    def blk(n, dtype=BF16):
        return jax.ShapeDtypeStruct((n, size, cols), dtype)

    up = [(i, (i + 1) % peers) for i in range(peers)]
    down = [(i, (i + peers - 1) % peers) for i in range(peers)]

    def swap_far(x):
        return lax.all_to_all(x, "mesh", split_axis=0, concat_axis=0, tiled=True)

    blocks, send = pl.pallas_call(
        prep_kernel,
        out_shape=(blk(rows), blk(nfar)),
        in_specs=[smem(), vmem()],
        out_specs=(vmem(), vmem()),
        compiler_params=params(),
        name="prep",
    )(asked, start_v.reshape(rows, size, cols))

    nu_blocks = nu.reshape(rows, size, cols)
    kern_spec = pl.BlockSpec((1, degree, size, size), lambda r, s: (r, 0, 0, 0))
    row_spec = pl.BlockSpec((1, size, cols), lambda r, s: (r, 0, 0))
    any_spec = pl.BlockSpec(memory_space=pl.ANY)

    def whole(n):
        return pl.BlockSpec((n, size, cols), lambda r, s: (0, 0, 0))

    potential_u = mu
    values = None
    for sweep in range(ITERS):
        from_left = lax.ppermute(blocks[rows - NEAR :], "mesh", up)
        from_right = lax.ppermute(blocks[:NEAR], "mesh", down)
        far = swap_far(send)
        applied = pl.pallas_call(
            forward_kernel,
            grid_spec=pltpu.PrefetchScalarGridSpec(
                num_scalar_prefetch=1,
                grid=(rows,),
                in_specs=[kern_spec, any_spec, any_spec, any_spec, any_spec],
                out_specs=row_spec,
                scratch_shapes=[
                    pltpu.VMEM((table_size, size, cols), BF16),
                    pltpu.SemaphoreType.DMA((4,)),
                ],
            ),
            out_shape=blk(rows),
            compiler_params=params(),
            name="forward",
        )(sources, kern_blocks, blocks, from_left, from_right, far)
        pieces = applied.reshape(states, local_rows // states, cols)
        mixed = jnp.einsum(
            "xrl,jl->xrj",
            lax.all_to_all(pieces, "state", split_axis=0, concat_axis=2, tiled=True),
            state_kernel,
            preferred_element_type=F32,
        )
        potential_u = mu / mixed[0]
        back_rows = jnp.dot(
            potential_u.astype(BF16), state_kernel, preferred_element_type=F32
        ).astype(BF16)
        returned = lax.all_to_all(back_rows, "state", split_axis=1, concat_axis=0, tiled=True)
        returned = returned.reshape(rows, size, cols)
        own, to_left, to_right, to_far = pl.pallas_call(
            backward_kernel,
            grid_spec=pltpu.PrefetchScalarGridSpec(
                num_scalar_prefetch=1,
                grid=(rows,),
                in_specs=[kern_spec, row_spec],
                out_specs=(whole(rows), whole(NEAR), whole(NEAR), whole(nfar)),
                scratch_shapes=[pltpu.VMEM((table_size, size, cols), F32)],
            ),
            out_shape=(blk(rows), blk(NEAR), blk(NEAR), blk(nfar)),
            compiler_params=params(),
            name="backward",
        )(sources, kern_blocks, returned)
        part_last = lax.ppermute(to_left, "mesh", down)
        part_first = lax.ppermute(to_right, "mesh", up)
        part_far = swap_far(to_far)
        last = sweep == ITERS - 1
        result = pl.pallas_call(
            functools.partial(finish_kernel, last),
            out_shape=(blk(rows, F32),) if last else (blk(rows), blk(nfar)),
            in_specs=[smem()] + [vmem()] * 5,
            out_specs=(vmem(),) if last else (vmem(), vmem()),
            scratch_shapes=[pltpu.VMEM((rows, size, cols), F32)],
            compiler_params=params(),
            name="finish",
        )(asked, own, part_first, part_last, part_far, nu_blocks)
        if last:
            values = result[0]
        else:
            blocks, send = result
    return (potential_u, values.reshape(local_rows, cols))


def solution(mesh):
    placed = (
        P("mesh", None, None, None),
        P("mesh", None),
        P(),
        P("mesh", "state"),
        P(("mesh", "state"), None),
        P("mesh", "state"),
    )
    return jax.shard_map(
        per_device,
        mesh=mesh,
        in_specs=placed,
        out_specs=(P(("mesh", "state"), None), P("mesh", "state")),
        check_vma=False,
    )
```

time: 862 us -> 353 us (0.41)
  other arithmetic: 266 us -> 1.63 us
  waiting for transfers between devices: 222 us -> 102 us
  Pallas kernels: 0 us -> 101 us
  local copies, waits for them, and re-layouts: 128 us -> 27.2 us
  blocking collectives: 135 us -> 62.5 us
  matrix products: 61 us -> 3.74 us
  starting transfers between devices: 38.2 us -> 47.7 us
    all_to_all x4, waiting for transfers between devices: 222 us -> 0.55 us  [swap_far(): return lax.all_to_all(x, 'mesh', split_axis=0, concat_axis=0, tiled=True)]
    scatter-add x4 -> x0, other arithmetic: 209 us -> none  [the longest x2 159 us: per_device(): jax.ops.segment_sum(spread.reshape(-1, block_size, state_cols), sources,...]
    ppermute x0 -> x8, waiting for transfers between devices: none -> 102 us  [the longest x2 50.9 us: per_device(): from_right = lax.ppermute(blocks[:NEAR], 'mesh', down)]
    pallas_call x0 -> x7, Pallas kernels: none -> 101 us  [the longest x2 57.3 us: per_device(): pl.pallas_call(backward_kernel, grid_spec=pltpu.PrefetchScalarGridSpec(nu...]
    all_to_all x1, blocking collectives: 82.7 us -> 15.3 us  [per_device(): lax.all_to_all(requests, 'mesh', split_axis=0, concat_axis=0, tiled=True)]
    dot_general x6 -> x2, matrix products: 58.9 us -> 3.09 us  [per_device(): jnp.dot(potential_u.astype(BF16), state_kernel, preferred_element_type=F32)]
    reshape x4, local copies, waits for them, and re-layouts: 49.9 us -> 0.74 us  [the longest x2 0.56 us: per_device(): pieces = applied.reshape(states, local_rows // states, cols)]
    gather x4 -> x0, local copies, waits for them, and re-layouts: 44.5 us -> none  [the longest x2 28.7 us: per_device(): picked = table[sources].reshape(block_rows, degree, block_size, state_cols)]
  transfers between devices with their start and end apart: 4 -> 12, of which waited for: 4 -> 7; matrix products, arithmetic and copies ran while one was open for 0% -> 0% of each run, Pallas kernels for 0% -> 0%
where the time goes in v1:
time: 353 us; the launch traced here: 347 us
  waiting for transfers between devices  102 us (29%)
  Pallas kernels  101 us (29%)
  blocking collectives  62.5 us (18%)
  starting transfers between devices  47.7 us (14%)
  local copies, waits for them, and re-layouts  27.2 us (8%)
  matrix products  3.74 us (1%)
    pallas_call x2, Pallas kernels, per_device(): pl.pallas_call(backward_kernel, grid_spec=pltpu.PrefetchScalarGridSpec(nu...  57.3 us
    ppermute x2, waiting for transfers between devices, per_device(): from_right = lax.ppermute(blocks[:NEAR], 'mesh', down)  50.9 us
    ppermute x2, waiting for transfers between devices, per_device(): part_first = lax.ppermute(to_right, 'mesh', up)  47.1 us
    all_to_all x4, starting transfers between devices, swap_far(): return lax.all_to_all(x, 'mesh', split_axis=0, concat_axis=0, tiled=True)  40.7 us
    pallas_call x2, Pallas kernels, per_device(): pl.pallas_call(forward_kernel, grid_spec=pltpu.PrefetchScalarGridSpec(num...  36.2 us
    all_to_all x2, blocking collectives, per_device(): lax.all_to_all(pieces, 'state', split_axis=0, concat_axis=2, tiled=True)  25.7 us
    unnamed x61, local copies, waits for them, and re-layouts  24.8 us
    all_to_all x2, blocking collectives, per_device(): lax.all_to_all(back_rows, 'state', split_axis=1, concat_axis=0, tiled=True)  21.5 us
  transfers between devices with their start and end apart: 12, of which 7 were waited for; matrix products, arithmetic and copies ran while one was open for 0% of the time, Pallas kernels for 0%

profile of v1, /device:TPU:1, one launch (start us, length us, event | category | flops | bytes accessed | tf_op | source)
XLA Modules:
  0.0 347.5 jit_solution(16274431381791191010)
XLA Ops:
  2.3 15.3 %all_to_all.91 = s32[32,1,2]{2,1,0:T(1,128)S(1)} all-to-all(s32[32,1,2]{2,1,0:T(1,128)S(1)} %copy.28), channel_id=1, replica_groups=mesh['mesh'=32,'state'=4] {'mesh'}, dimensions={0} | all-to-all | bytes 512 | tf_op jit(solution)/shard_map/all_to_all | solution.py:191
  22.9 4.3 %all-to-all-start.1 = ((bf16[64,128,128]{2,1,0:T(8,128)(2,1)}), bf16[64,128,128]{2,1,0:T(8,128)(2,1)S(1)}, u32[]{:S(2)}, u32[]{:S(2)}) async-start(bf16[64,128,128]{2,1,0:T(8,128)(2,1)} %copy-done.3), calls=%async_computation.1 | async-start | bytes 4194304 | tf_op jit(solution)/shard_map/all_to_all | solution.py:200
  29.7 25.1 %collective-permute-done.1.right_ref = bf16[6,128,128]{2,1,0:T(8,128)(2,1)S(1)} collective-permute-done((bf16[6,128,128]{2,1,0:T(8,128)(2,1)S(1)}, bf16[6,128,128]{2,1,0:T(8,128)(2,1)S(1)}, u32[]{:S(2)}, u32[]{:S(2)}) %collective-permute-start.1) | collective-permute-done | bytes 196640 | tf_op jit(solution)/shard_map/ppermute | solution.py:223
  59.2 18.1 %forward.2 = bf16[24,128,128]{2,1,0:T(8,128)(2,1)S(1)} custom-call(s32[384]{0:T(512)S(1)} %select_select_fusion.src_ref, bf16[24,16,128,128]{3,2,1,0:T(8,128)(2,1)} %kern_ref.7, bf16[24,128,128]{2,1,0:T(8,128)(2,1)S(1)} %copy-done.8, bf16[6,128,128]{2,1,0:T(8,128)(2,1)S(1)} %copy-done.17, bf16[6,128,128]{2,1,0:T(8,128)(2,1)S(1)} %copy-done.15, ...), custom_call_target="tpu_custom_call" | custom-call | tf_op jit(solution)/shard_map/forward/pallas_call | solution.py:225
  77.5 14.0 %all_to_all.92 = bf16[4,768,128]{1,2,0:T(8,128)(2,1)S(1)} all-to-all(bf16[4,768,128]{1,2,0:T(8,128)(2,1)S(1)} %copy.29), channel_id=1, replica_groups=mesh['mesh'=32,'state'=4] {'state'}, dimensions={0} | all-to-all | bytes 1572864 | tf_op jit(solution)/shard_map/all_to_all | solution.py:244
  91.5 2.5 convolution_convert_fusion.1
  94.3 10.7 %all_to_all.93 = bf16[768,4,128]{2,0,1:T(8,128)(2,1)S(1)} all-to-all(bf16[768,4,128]{2,0,1:T(8,128)(2,1)S(1)} %copy.30), channel_id=1, replica_groups=mesh['mesh'=32,'state'=4] {'state'}, dimensions={1} | all-to-all | bytes 1572864 | tf_op jit(solution)/shard_map/all_to_all | solution.py:252
  105.1 28.7 %backward.2 = (bf16[24,128,128]{2,1,0:T(8,128)(2,1)S(1)}, bf16[6,128,128]{2,1,0:T(8,128)(2,1)S(1)}, bf16[6,128,128]{2,1,0:T(8,128)(2,1)S(1)}, bf16[64,128,128]{2,1,0:T(8,128)(2,1)S(1)}) custom-call(s32[384]{0:T(512)S(1)} %select_select_fusion.src_ref, bf16[24,16,128,128]{3,2,1,0:T(8,128)(2,1)} %kern_ref.7, bf16[24,128,128]{2,1,0:T(8,128)(2,1)S(1)} %bitcast.38), custom_call_target="tpu_custom_call" | custom-call | tf_op jit(solution)/shard_map/backward/pallas_call | solution.py:254
  136.0 14.7 %all-to-all-start.4 = ((bf16[64,128,128]{2,1,0:T(8,128)(2,1)}), bf16[64,128,128]{2,1,0:T(8,128)(2,1)}, u32[]{:S(2)}, u32[]{:S(2)}) async-start(bf16[64,128,128]{2,1,0:T(8,128)(2,1)} %copy-done.6), calls=%async_computation.4 | async-start | bytes 4194304 | tf_op jit(solution)/shard_map/all_to_all | solution.py:200
  150.7 1.7 collective-permute-start.2
  152.4 23.5 %collective-permute-done.2.first_ref = bf16[6,128,128]{2,1,0:T(8,128)(2,1)S(1)} collective-permute-done((bf16[6,128,128]{2,1,0:T(8,128)(2,1)S(1)}, bf16[6,128,128]{2,1,0:T(8,128)(2,1)S(1)}, u32[]{:S(2)}, u32[]{:S(2)}) %collective-permute-start.2) | collective-permute-done | bytes 196640 | tf_op jit(solution)/shard_map/ppermute | solution.py:268
  175.9 2.4 collective-permute-done.3.last_ref
  179.9 3.5 finish.2
  184.7 6.7 %all-to-all-start.5 = ((bf16[64,128,128]{2,1,0:T(8,128)(2,1)}), bf16[64,128,128]{2,1,0:T(8,128)(2,1)S(1)}, u32[]{:S(2)}, u32[]{:S(2)}) async-start(bf16[64,128,128]{2,1,0:T(8,128)(2,1)} %copy-done.4), calls=%async_computation.5 | async-start | bytes 4194304 | tf_op jit(solution)/shard_map/all_to_all | solution.py:200
  193.3 25.7 %collective-permute-done.5.right_ref = bf16[6,128,128]{2,1,0:T(8,128)(2,1)S(1)} collective-permute-done((bf16[6,128,128]{2,1,0:T(8,128)(2,1)S(1)}, bf16[6,128,128]{2,1,0:T(8,128)(2,1)S(1)}, u32[]{:S(2)}, u32[]{:S(2)}) %collective-permute-start.5) | collective-permute-done | bytes 196640 | tf_op jit(solution)/shard_map/ppermute | solution.py:223
  223.4 18.1 %forward.3 = bf16[24,128,128]{2,1,0:T(8,128)(2,1)S(1)} custom-call(s32[384]{0:T(512)S(1)} %select_select_fusion.src_ref, bf16[24,16,128,128]{3,2,1,0:T(8,128)(2,1)} %kern_ref.7, bf16[24,128,128]{2,1,0:T(8,128)(2,1)S(1)} %copy-done.10, bf16[6,128,128]{2,1,0:T(8,128)(2,1)S(1)} %copy-done.21, bf16[6,128,128]{2,1,0:T(8,128)(2,1)S(1)} %copy-done.19, ...), custom_call_target="tpu_custom_call" | custom-call | tf_op jit(solution)/shard_map/forward/pallas_call | solution.py:225
  241.8 11.8 %all_to_all.94 = bf16[4,768,128]{1,2,0:T(8,128)(2,1)S(1)} all-to-all(bf16[4,768,128]{1,2,0:T(8,128)(2,1)S(1)} %copy.31), channel_id=1, replica_groups=mesh['mesh'=32,'state'=4] {'state'}, dimensions={0} | all-to-all | bytes 1572864 | tf_op jit(solution)/shard_map/all_to_all | solution.py:244
  255.8 10.7 %all_to_all.95 = bf16[768,4,128]{2,0,1:T(8,128)(2,1)S(1)} all-to-all(bf16[768,4,128]{2,0,1:T(8,128)(2,1)S(1)} %copy.32), channel_id=1, replica_groups=mesh['mesh'=32,'state'=4] {'state'}, dimensions={1} | all-to-all | bytes 1572864 | tf_op jit(solution)/shard_map/all_to_all | solution.py:252
  266.5 28.7 %backward.3 = (bf16[24,128,128]{2,1,0:T(8,128)(2,1)S(1)}, bf16[6,128,128]{2,1,0:T(8,128)(2,1)S(1)}, bf16[6,128,128]{2,1,0:T(8,128)(2,1)S(1)}, bf16[64,128,128]{2,1,0:T(8,128)(2,1)S(1)}) custom-call(s32[384]{0:T(512)S(1)} %select_select_fusion.src_ref, bf16[24,16,128,128]{3,2,1,0:T(8,128)(2,1)} %kern_ref.7, bf16[24,128,128]{2,1,0:T(8,128)(2,1)S(1)} %bitcast.37), custom_call_target="tpu_custom_call" | custom-call | tf_op jit(solution)/shard_map/backward/pallas_call | solution.py:254
  297.9 14.9 %all-to-all-start.8 = ((bf16[64,128,128]{2,1,0:T(8,128)(2,1)}), bf16[64,128,128]{2,1,0:T(8,128)(2,1)S(1)}, u32[]{:S(2)}, u32[]{:S(2)}) async-start(bf16[64,128,128]{2,1,0:T(8,128)(2,1)} %copy-done.5), calls=%async_computation.8 | async-start | bytes 4194304 | tf_op jit(solution)/shard_map/all_to_all | solution.py:200
  312.8 1.7 collective-permute-start.6
  314.5 23.6 %collective-permute-done.6.first_ref = bf16[6,128,128]{2,1,0:T(8,128)(2,1)S(1)} collective-permute-done((bf16[6,128,128]{2,1,0:T(8,128)(2,1)}, bf16[6,128,128]{2,1,0:T(8,128)(2,1)S(1)}, u32[]{:S(2)}, u32[]{:S(2)}) %collective-permute-start.6) | collective-permute-done | bytes 196640 | tf_op jit(solution)/shard_map/ppermute | solution.py:268
  338.8 1.6 collective-permute-done.7.last_ref
  344.4 3.1 finish.3
  (99 shorter events, 35.5 us)
Async XLA Ops:
  0.6 90.9 %copy-start = (bf16[512,512]{1,0:T(8,128)(2,1)S(1)}, bf16[512,512]{1,0:T(8,128)(2,1)}, u32[]{:S(2)}) copy-start(bf16[512,512]{1,0:T(8,128)(2,1)} %param.8) | copy-start | bytes 1572868
  18.9 1.4 copy-start.11
  21.5 1.3 copy-start.3
  22.9 4.9 %copy-start.7 = (bf16[24,128,128]{2,1,0:T(8,128)(2,1)}, bf16[24,128,128]{2,1,0:T(8,128)(2,1)S(1)}, u32[]{:S(2)}) copy-start(bf16[24,128,128]{2,1,0:T(8,128)(2,1)S(1)} %get-tuple-element.14.own_ref) | copy-start | bytes 2359300
  22.9 33.3 %all-to-all-start.1 = ((bf16[64,128,128]{2,1,0:T(8,128)(2,1)}), bf16[64,128,128]{2,1,0:T(8,128)(2,1)S(1)}, u32[]{:S(2)}, u32[]{:S(2)}) async-start(bf16[64,128,128]{2,1,0:T(8,128)(2,1)} %copy-done.3), calls=%async_computation.1 | async-start | bytes 4194304 | tf_op jit(solution)/shard_map/all_to_all | solution.py:200
  27.8 27.0 %collective-permute-start.1 = (bf16[6,128,128]{2,1,0:T(8,128)(2,1)S(1)}, bf16[6,128,128]{2,1,0:T(8,128)(2,1)S(1)}, u32[]{:S(2)}, u32[]{:S(2)}) collective-permute-start(bf16[6,128,128]{2,1,0:T(8,128)(2,1)S(1)} %get-tuple-element.34), channel_id=1, source_target_pairs={{0,124},{4,0},{8,4},{12,8},{16,12},{20,16},{24,20},{28,24},{32,28}... | collective-permute-start | bytes 589832 | tf_op jit(solution)/shard_map/ppermute | solution.py:223
  28.2 27.2 %collective-permute-start = (bf16[6,128,128]{2,1,0:T(8,128)(2,1)S(1)}, bf16[6,128,128]{2,1,0:T(8,128)(2,1)S(1)}, u32[]{:S(2)}, u32[]{:S(2)}) collective-permute-start(bf16[6,128,128]{2,1,0:T(8,128)(2,1)S(1)} %get-tuple-element.35), channel_id=1, source_target_pairs={{0,4},{4,8},{8,12},{12,16},{16,20},{20,24},{24,28},{28,32},{32,36}... | collective-permute-start | bytes 589832 | tf_op jit(solution)/shard_map/ppermute | solution.py:222
  133.7 1.3 copy-start.6
  136.0 42.8 %copy-start.1 = (f32[3072,128]{1,0:T(8,128)S(1)}, f32[3072,128]{1,0:T(8,128)}, u32[]{:S(2)}) copy-start(f32[3072,128]{1,0:T(8,128)} %param.11) | copy-start | bytes 4718596
  136.0 42.8 %all-to-all-start.4 = ((bf16[64,128,128]{2,1,0:T(8,128)(2,1)}), bf16[64,128,128]{2,1,0:T(8,128)(2,1)}, u32[]{:S(2)}, u32[]{:S(2)}) async-start(bf16[64,128,128]{2,1,0:T(8,128)(2,1)} %copy-done.6), calls=%async_computation.4 | async-start | bytes 4194304 | tf_op jit(solution)/shard_map/all_to_all | solution.py:200
  150.7 25.2 %collective-permute-start.2 = (bf16[6,128,128]{2,1,0:T(8,128)(2,1)S(1)}, bf16[6,128,128]{2,1,0:T(8,128)(2,1)S(1)}, u32[]{:S(2)}, u32[]{:S(2)}) collective-permute-start(bf16[6,128,128]{2,1,0:T(8,128)(2,1)S(1)} %get-tuple-element.17), channel_id=1, source_target_pairs={{0,4},{4,8},{8,12},{12,16},{16,20},{20,24},{24,28},{28,32},{32,36}... | collective-permute-start | bytes 589832 | tf_op jit(solution)/shard_map/ppermute | solution.py:268
  152.4 25.8 %collective-permute-start.3 = (bf16[6,128,128]{2,1,0:T(8,128)(2,1)S(1)}, bf16[6,128,128]{2,1,0:T(8,128)(2,1)S(1)}, u32[]{:S(2)}, u32[]{:S(2)}) collective-permute-start(bf16[6,128,128]{2,1,0:T(8,128)(2,1)S(1)} %get-tuple-element.18), channel_id=1, source_target_pairs={{0,124},{4,0},{8,4},{12,8},{16,12},{20,16},{24,20},{28,24},{32,28}... | collective-permute-start | bytes 589832 | tf_op jit(solution)/shard_map/ppermute | solution.py:267
  183.4 1.3 copy-start.4
  184.7 6.7 %copy-start.9 = (bf16[24,128,128]{2,1,0:T(8,128)(2,1)}, bf16[24,128,128]{2,1,0:T(8,128)(2,1)S(1)}, u32[]{:S(2)}) copy-start(bf16[24,128,128]{2,1,0:T(8,128)(2,1)S(1)} %get-tuple-element.20.own_ref) | copy-start | bytes 2359300
  184.7 35.7 %all-to-all-start.5 = ((bf16[64,128,128]{2,1,0:T(8,128)(2,1)}), bf16[64,128,128]{2,1,0:T(8,128)(2,1)S(1)}, u32[]{:S(2)}, u32[]{:S(2)}) async-start(bf16[64,128,128]{2,1,0:T(8,128)(2,1)} %copy-done.4), calls=%async_computation.5 | async-start | bytes 4194304 | tf_op jit(solution)/shard_map/all_to_all | solution.py:200
  191.5 27.5 %collective-permute-start.5 = (bf16[6,128,128]{2,1,0:T(8,128)(2,1)S(1)}, bf16[6,128,128]{2,1,0:T(8,128)(2,1)S(1)}, u32[]{:S(2)}, u32[]{:S(2)}) collective-permute-start(bf16[6,128,128]{2,1,0:T(8,128)(2,1)S(1)} %get-tuple-element.32), channel_id=1, source_target_pairs={{0,124},{4,0},{8,4},{12,8},{16,12},{20,16},{24,20},{28,24},{32,28}... | collective-permute-start | bytes 589832 | tf_op jit(solution)/shard_map/ppermute | solution.py:223
  191.9 27.9 %collective-permute-start.4 = (bf16[6,128,128]{2,1,0:T(8,128)(2,1)S(1)}, bf16[6,128,128]{2,1,0:T(8,128)(2,1)S(1)}, u32[]{:S(2)}, u32[]{:S(2)}) collective-permute-start(bf16[6,128,128]{2,1,0:T(8,128)(2,1)S(1)} %get-tuple-element.33), channel_id=1, source_target_pairs={{0,4},{4,8},{8,12},{12,16},{16,20},{20,24},{24,28},{28,32},{32,36}... | collective-permute-start | bytes 589832 | tf_op jit(solution)/shard_map/ppermute | solution.py:222
  241.8 11.8 %copy-start.29 = (f32[768,512]{1,0:T(8,128)S(1)}, f32[768,512]{1,0:T(8,128)}, u32[]{:S(2)}) copy-start(f32[768,512]{1,0:T(8,128)} %param.10) | copy-start | bytes 4718596
  254.2 1.1 copy-start.28
  295.2 1.3 copy-start.5
  297.9 43.2 %all-to-all-start.8 = ((bf16[64,128,128]{2,1,0:T(8,128)(2,1)}), bf16[64,128,128]{2,1,0:T(8,128)(2,1)S(1)}, u32[]{:S(2)}, u32[]{:S(2)}) async-start(bf16[64,128,128]{2,1,0:T(8,128)(2,1)} %copy-done.5), calls=%async_computation.8 | async-start | bytes 4194304 | tf_op jit(solution)/shard_map/all_to_all | solution.py:200
  312.8 25.3 %collective-permute-start.6 = (bf16[6,128,128]{2,1,0:T(8,128)(2,1)}, bf16[6,128,128]{2,1,0:T(8,128)(2,1)S(1)}, u32[]{:S(2)}, u32[]{:S(2)}) collective-permute-start(bf16[6,128,128]{2,1,0:T(8,128)(2,1)} %copy-done.27), channel_id=1, source_target_pairs={{0,4},{4,8},{8,12},{12,16},{16,20},{20,24},{24,28},{28,32},{32,36}... | collective-permute-start | bytes 589832 | tf_op jit(solution)/shard_map/ppermute | solution.py:268
  314.5 25.9 %collective-permute-start.7 = (bf16[6,128,128]{2,1,0:T(8,128)(2,1)}, bf16[6,128,128]{2,1,0:T(8,128)(2,1)S(1)}, u32[]{:S(2)}, u32[]{:S(2)}) collective-permute-start(bf16[6,128,128]{2,1,0:T(8,128)(2,1)} %copy-done.26), channel_id=1, source_target_pairs={{0,124},{4,0},{8,4},{12,8},{16,12},{20,16},{24,20},{28,24},{32,28}... | collective-permute-start | bytes 589832 | tf_op jit(solution)/shard_map/ppermute | solution.py:267
  341.1 1.4 copy-start.2
  (18 other events, 15.3 us)

commit v2 on v0

v2 whole, which is shorter than its diff:
```python
import functools
import jax
import jax.numpy as jnp
from jax import lax
from jax.experimental import pallas as pl
from jax.experimental.pallas import tpu as pltpu
from jax.sharding import PartitionSpec as P

ITERS = 2
NEAR = 6
FAR = 2
LAG = 2
VMEM_LIMIT = 52 * 1024 * 1024
F32 = jnp.float32
BF16 = jnp.bfloat16


def vmem():
    return pl.BlockSpec(memory_space=pltpu.VMEM)


def smem():
    return pl.BlockSpec(memory_space=pltpu.SMEM)


def hbm():
    return pl.BlockSpec(memory_space=pl.ANY)


def far_plan(flat_cols, me, peers, rows):
    owners = flat_cols // rows
    places = flat_cols % rows
    delta = (owners - me + peers) % peers
    is_own = delta == 0
    is_left = delta == peers - 1
    is_right = delta == 1
    is_far = ~(is_own | is_left | is_right)
    ids = jnp.arange(peers * rows, dtype=jnp.int32)
    hits = (flat_cols[:, None] == ids[None, :]) & is_far[:, None]
    needed = jnp.max(hits.astype(jnp.int32), axis=0).reshape(peers, rows)
    before = jnp.arange(rows)[:, None] < jnp.arange(rows)[None, :]
    ranks = jnp.sum(needed[:, :, None] * before[None].astype(jnp.int32), axis=1)
    place_ids = jnp.arange(rows, dtype=jnp.int32)
    requests = jnp.stack(
        [jnp.sum(needed * (ranks == s) * place_ids[None, :], axis=1) for s in range(FAR)],
        axis=1,
    )
    slots = jnp.sum(hits.astype(jnp.int32) * ranks.reshape(1, -1), axis=1)
    far_at = rows + 2 * NEAR + (delta - 2) * FAR + slots
    sources = jnp.where(
        is_own,
        places,
        jnp.where(
            is_left,
            rows + places - (rows - NEAR),
            jnp.where(is_right, rows + NEAR + places, far_at),
        ),
    )
    return sources.astype(jnp.int32), requests.astype(jnp.int32)


def arrival_order(asked, me, peers, rows):
    deltas = (me + jnp.arange(2, peers - 1, dtype=jnp.int32)) % peers
    places = asked.reshape(peers, FAR)[deltas].reshape(-1)
    count = places.shape[0]
    ids = jnp.arange(count, dtype=jnp.int32)
    keys = places * count + ids
    rank = jnp.sum((keys[None, :] < keys[:, None]).astype(jnp.int32), axis=1)
    here = (rank[:, None] == ids[None, :]).astype(jnp.int32)
    perm = jnp.sum(here * ids[:, None], axis=0)
    ordered = jnp.sum(here * places[:, None], axis=0)
    keep = jnp.concatenate([jnp.zeros((1,), jnp.int32), (ordered[1:] == ordered[:-1]).astype(jnp.int32)])
    same = ordered[None, :] == jnp.arange(rows, dtype=jnp.int32)[:, None]
    last = jnp.max(jnp.where(same, ids[None, :], -1), axis=1)
    return perm, keep, last


def exchange_kernel(mode, with_u, peers, states, *refs):
    with_back = mode != "first"
    with_forward = mode != "last"
    refs = list(refs)

    def take(n):
        out = refs[:n]
        del refs[:n]
        return out

    if with_back:
        perm_ref, keep_ref, last_ref, parts_ref, nu_hbm = take(5)
    else:
        (start_ref,) = take(1)
    if with_forward:
        asked_ref, src_ref, kern_hbm, mix_hbm, mu_hbm = take(5)
        (back_ref,) = take(1)
        if with_u:
            (u_ref,) = take(1)
    else:
        (v_ref,) = take(1)
    if with_back:
        own_part, arrived, running, nu_ref, back_send, back_recv, local_sem = take(7)
    if with_forward:
        (
            table, blocks, outbox, kern, mix, mu_ref, a_out, a_in, b_out, b_in,
            kern_sem, mix_sem, mu_sem, near_send, near_recv, far_send, far_recv,
            a_send, a_recv, b_send, b_recv,
        ) = take(21)

    me = lax.axis_index("mesh")
    mz = lax.axis_index("state")
    nfar = peers - 3

    if with_back:
        rows = own_part.shape[0]
    else:
        rows = start_ref.shape[0]
    far0 = rows + 2 * NEAR
    per = rows // states

    local = []
    if with_back:
        local.append(pltpu.make_async_copy(parts_ref.at[pl.ds(0, rows)], own_part, local_sem.at[0]))
        local.append(pltpu.make_async_copy(nu_hbm, nu_ref, local_sem.at[1]))
    for c in local:
        c.start()
    if with_forward:
        kern_copy = pltpu.make_async_copy(kern_hbm, kern, kern_sem)
        mix_copy = pltpu.make_async_copy(mix_hbm, mix, mix_sem)
        mu_copy = pltpu.make_async_copy(mu_hbm, mu_ref, mu_sem)
        kern_copy.start()
        mix_copy.start()
        mu_copy.start()

    barrier = pltpu.get_barrier_semaphore()

    def greet(o, _):
        pl.semaphore_signal(barrier, inc=1, device_id={"mesh": lax.rem(me + o, peers)})
        return 0

    lax.fori_loop(1, peers, greet, 0)
    greeted = peers - 1
    if with_forward:
        for j in range(1, states):
            pl.semaphore_signal(barrier, inc=1, device_id={"state": lax.rem(mz + j, states)})
        greeted += states - 1
    pl.semaphore_wait(barrier, greeted)

    right = lax.rem(me + 1, peers)
    left = lax.rem(me + peers - 1, peers)

    if with_back:

        def back_far(d):
            at = peers - d
            return pltpu.make_async_remote_copy(
                src_ref=parts_ref.at[pl.ds(far0 + (d - 2) * FAR, FAR)],
                dst_ref=arrived.at[pl.ds(2 * NEAR + (at - 2) * FAR, FAR)],
                send_sem=back_send.at[d],
                recv_sem=back_recv.at[at],
                device_id={"mesh": lax.rem(me + d, peers)},
            )

        def back_near(k):
            return pltpu.make_async_remote_copy(
                src_ref=parts_ref.at[pl.ds(rows + k * NEAR, NEAR)],
                dst_ref=arrived.at[pl.ds(k * NEAR, NEAR)],
                send_sem=back_send.at[k],
                recv_sem=back_recv.at[k],
                device_id={"mesh": (left, right)[k]},
            )

        def go(d, _):
            back_far(d).start()
            return 0

        lax.fori_loop(2, peers - 1, go, 0)
        for k in range(2):
            back_near(k).start()
        for c in local:
            c.wait()

        def got(d, _):
            back_far(peers - d).wait_recv()
            return 0

        for k in range(2):
            back_near(k).wait_recv()
        lax.fori_loop(2, peers - 1, got, 0)

        def add(i, acc):
            kept = jnp.where(keep_ref[i] > 0, acc, jnp.zeros_like(acc))
            acc = kept + arrived[2 * NEAR + perm_ref[i]].astype(F32)
            running[i] = acc
            return acc

        lax.fori_loop(0, nfar * FAR, add, jnp.zeros(running.shape[1:], F32))

        def finish(p, near):
            at = last_ref[p]
            total = own_part[p].astype(F32)
            if near is not None:
                total = total + arrived[near].astype(F32)
            far = running[jnp.maximum(at, 0)]
            total = total + jnp.where(at >= 0, far, jnp.zeros_like(far))
            v = nu_ref[p] / total
            if with_forward:
                table[p] = v.astype(BF16)
                blocks[p] = v.astype(BF16)
            else:
                v_ref[p] = v
            return 0

        lax.fori_loop(0, NEAR, lambda p, _: finish(p, NEAR + p), 0)
        lax.fori_loop(NEAR, rows - NEAR, lambda p, _: finish(p, None), 0)
        lax.fori_loop(rows - NEAR, rows, lambda p, _: finish(p, p - (rows - NEAR)), 0)
    else:

        def cast(p, _):
            v = start_ref[p].astype(BF16)
            table[p] = v
            blocks[p] = v
            return 0

        lax.fori_loop(0, rows, cast, 0)

    if with_forward:

        def fwd_near(k):
            return pltpu.make_async_remote_copy(
                src_ref=blocks.at[pl.ds((rows - NEAR, 0)[k], NEAR)],
                dst_ref=table.at[pl.ds(rows + k * NEAR, NEAR)],
                send_sem=near_send.at[k],
                recv_sem=near_recv.at[k],
                device_id={"mesh": (right, left)[k]},
            )

        def fwd_far(o):
            at = peers - o
            return pltpu.make_async_remote_copy(
                src_ref=outbox.at[pl.ds(o * FAR, FAR)],
                dst_ref=table.at[pl.ds(far0 + (at - 2) * FAR, FAR)],
                send_sem=far_send.at[o],
                recv_sem=far_recv.at[at],
                device_id={"mesh": lax.rem(me + o, peers)},
            )

        def send(o, _):
            q = lax.rem(me + o, peers)
            for s in range(FAR):
                outbox[o * FAR + s] = blocks[asked_ref[q * FAR + s]]
            fwd_far(o).start()
            return 0

        lax.fori_loop(2, peers - 1, send, 0)
        for k in range(2):
            fwd_near(k).start()
        for k in range(2):
            fwd_near(k).wait_recv()

        def got_far(d, _):
            fwd_far(peers - d).wait_recv()
            return 0

        lax.fori_loop(2, peers - 1, got_far, 0)
        kern_copy.wait()
        mix_copy.wait()
        mu_copy.wait()
        degree = kern.shape[1]
        size, cols = table.shape[1:]

        def a_copy(j, sub):
            to = lax.rem(mz + j, states)
            return pltpu.make_async_remote_copy(
                src_ref=a_out.at[to, sub],
                dst_ref=a_in.at[mz, sub],
                send_sem=a_send.at[j, sub],
                recv_sem=a_recv.at[j, sub],
                device_id={"state": to},
            )

        def b_copy(j, sub):
            to = lax.rem(mz + j, states)
            return pltpu.make_async_remote_copy(
                src_ref=b_out.at[to, sub],
                dst_ref=b_in.at[mz, sub],
                send_sem=b_send.at[j, sub],
                recv_sem=b_recv.at[j, sub],
                device_id={"state": to},
            )

        def apply_rows(sub):
            for j in list(range(1, states)) + [0]:
                to = lax.rem(mz + j, states)
                r = to * per + sub
                lhs = jnp.concatenate([kern[r, k] for k in range(degree)], axis=1)
                rhs = jnp.concatenate(
                    [table[src_ref[r * degree + k]] for k in range(degree)], axis=0
                )
                out = jnp.dot(lhs, rhs, preferred_element_type=F32).astype(BF16)
                if j == 0:
                    a_in[mz, sub] = out
                else:
                    a_out[to, sub] = out
                    a_copy(j, sub).start()

        def mix_rows(sub):
            for j in range(1, states):
                a_copy(j, sub).wait_recv()
            a = jnp.concatenate([a_in[z, sub] for z in range(states)], axis=1)
            kv = lax.dot_general(
                a, mix[...], (((1,), (1,)), ((), ())), preferred_element_type=F32
            )
            at = pl.ds(pl.multiple_of(sub * size, size), size)
            u = mu_ref[at, :] / kv
            if with_u:
                u_ref[at, :] = u
            b = jnp.dot(u.astype(BF16), mix[...], preferred_element_type=F32).astype(BF16)
            for z in range(states):
                b_out[z, sub] = b[:, z * cols : (z + 1) * cols]
            for j in range(1, states):
                b_copy(j, sub).start()

        def step(sub, _):
            apply_rows(sub)

            @pl.when(sub >= LAG)
            def _():
                mix_rows(sub - LAG)

            return 0

        lax.fori_loop(0, per, step, 0)
        lax.fori_loop(per - LAG, per, lambda sub, _: (mix_rows(sub), 0)[1], 0)

        def collect(sub, _):
            for j in range(1, states):
                b_copy(j, sub).wait_recv()
                z = lax.rem(mz + states - j, states)
                back_ref[z * per + sub] = b_in[z, sub]
            back_ref[mz * per + sub] = b_out[mz, sub]
            for j in range(1, states):
                a_copy(j, sub).wait_send()
                b_copy(j, sub).wait_send()
            return 0

        lax.fori_loop(0, per, collect, 0)
        for k in range(2):
            fwd_near(k).wait_send()

        def sent(o, _):
            fwd_far(o).wait_send()
            return 0

        lax.fori_loop(2, peers - 1, sent, 0)

    if with_back:
        for k in range(2):
            back_near(k).wait_send()

        def back_sent(d, _):
            back_far(d).wait_send()
            return 0

        lax.fori_loop(2, peers - 1, back_sent, 0)


def backward_kernel(src_ref, kern_ref, b_ref, part_ref, acc):
    r = pl.program_id(0)
    degree = kern_ref.shape[1]

    @pl.when(r == 0)
    def _():
        def clear(i, _):
            acc[i] = jnp.zeros(acc.shape[1:], F32)
            return 0

        lax.fori_loop(0, acc.shape[0], clear, 0)

    b = b_ref[r]
    for k in range(degree):
        prod = lax.dot_general(
            kern_ref[0, k], b, (((0,), (0,)), ((), ())), preferred_element_type=F32
        )
        acc[src_ref[r * degree + k]] += prod

    @pl.when(r == pl.num_programs(0) - 1)
    def _():
        def store(i, _):
            part_ref[i] = acc[i].astype(BF16)
            return 0

        lax.fori_loop(0, acc.shape[0], store, 0)


def per_device(kern_blocks, kern_cols, state_kernel, start_v, mu, nu):
    rows, degree, size, _ = kern_blocks.shape
    local_rows, cols = start_v.shape
    peers = lax.axis_size("mesh")
    states = lax.axis_size("state")
    me = lax.axis_index("mesh")
    per = rows // states
    nfar = (peers - 3) * FAR
    table_size = rows + 2 * NEAR + nfar
    nodes = states * cols
    sources, requests = far_plan(kern_cols.reshape(-1), me, peers, rows)
    asked = lax.all_to_all(requests, "mesh", split_axis=0, concat_axis=0, tiled=True).reshape(-1)
    perm, keep, last = arrival_order(asked, me, peers, rows)
    nu_blocks = nu.reshape(rows, size, cols)
    dma = pltpu.SemaphoreType.DMA

    def blk(*dims, dtype=BF16):
        return jax.ShapeDtypeStruct(dims + (size, cols), dtype)

    def scratch(*dims, dtype=BF16):
        return pltpu.VMEM(dims + (size, cols), dtype)

    def exchange(mode, with_u, ident, parts):
        ins, specs, outs, scr = [], [], [], []
        if mode == "first":
            ins += [start_v.reshape(rows, size, cols)]
            specs += [vmem()]
        else:
            ins += [perm, keep, last, parts, nu_blocks]
            specs += [smem(), smem(), smem(), hbm(), hbm()]
            scr += [
                scratch(rows), scratch(2 * NEAR + nfar), scratch(nfar, dtype=F32),
                scratch(rows, dtype=F32), dma((peers,)), dma((peers,)), dma((2,)),
            ]
        if mode == "last":
            outs += [blk(rows, dtype=F32)]
        else:
            ins += [asked, sources, kern_blocks, state_kernel, mu]
            specs += [smem(), smem(), hbm(), hbm(), hbm()]
            outs += [blk(rows)]
            if with_u:
                outs += [jax.ShapeDtypeStruct((local_rows // states, nodes), F32)]
            scr += [
                scratch(table_size), scratch(rows), scratch(peers * FAR),
                pltpu.VMEM((rows, degree, size, size), BF16),
                pltpu.VMEM((nodes, nodes), BF16),
                pltpu.VMEM((local_rows // states, nodes), F32),
                scratch(states, per), scratch(states, per), scratch(states, per), scratch(states, per),
                dma, dma, dma, dma((2,)), dma((2,)), dma((peers,)), dma((peers,)),
                dma((states, per)), dma((states, per)), dma((states, per)), dma((states, per)),
            ]
        return pl.pallas_call(
            functools.partial(exchange_kernel, mode, with_u, peers, states),
            out_shape=tuple(outs),
            in_specs=specs,
            out_specs=tuple(vmem() for _ in outs),
            scratch_shapes=scr,
            compiler_params=pltpu.CompilerParams(
                vmem_limit_bytes=VMEM_LIMIT, collective_id=ident, has_side_effects=True
            ),
            name="exchange_" + mode,
        )(*ins)

    def backward(b):
        return pl.pallas_call(
            backward_kernel,
            grid_spec=pltpu.PrefetchScalarGridSpec(
                num_scalar_prefetch=1,
                grid=(rows,),
                in_specs=[
                    pl.BlockSpec((1, degree, size, size), lambda r, s: (r, 0, 0, 0)),
                    pl.BlockSpec((rows, size, cols), lambda r, s: (0, 0, 0)),
                ],
                out_specs=pl.BlockSpec((table_size, size, cols), lambda r, s: (0, 0, 0)),
                scratch_shapes=[scratch(table_size, dtype=F32)],
            ),
            out_shape=blk(table_size),
            compiler_params=pltpu.CompilerParams(vmem_limit_bytes=VMEM_LIMIT),
            name="backward",
        )(sources, kern_blocks, b)

    result = exchange("first", ITERS == 1, 0, None)
    for sweep in range(1, ITERS):
        result = exchange("mid", sweep == ITERS - 1, sweep, backward(result[0]))
    potential_u = result[1]
    (values,) = exchange("last", False, ITERS, backward(result[0]))
    return (potential_u, values.reshape(local_rows, cols))


def solution(mesh):
    placed = (
        P("mesh", None, None, None),
        P("mesh", None),
        P(),
        P("mesh", "state"),
        P(("mesh", "state"), None),
        P("mesh", "state"),
    )
    return jax.shard_map(
        per_device,
        mesh=mesh,
        in_specs=placed,
        out_specs=(P(("mesh", "state"), None), P("mesh", "state")),
        check_vma=False,
    )
```

time: 862 us -> 261 us (0.30); the launches traced: 850 us -> 260 us
  other arithmetic: 266 us -> 2.21 us
  Pallas kernels: 0 us -> 236 us
  waiting for transfers between devices: 222 us -> 6.21 us
  blocking collectives: 135 us -> 0 us
  local copies, waits for them, and re-layouts: 128 us -> 6.47 us
  matrix products: 61 us -> 0 us
  starting transfers between devices: 38.2 us -> 8.59 us
    pallas_call x0 -> x5, Pallas kernels: none -> 236 us  [the longest x3 194 us: exchange(): pl.pallas_call(functools.partial(exchange_kernel, mode, with_u, peers, st...]
    all_to_all x3 -> x0, waiting for transfers between devices: 216 us -> none  [the longest x2 144 us: per_device(): lax.all_to_all(outgoing, 'mesh', split_axis=0, concat_axis=0, tiled=True)]
    scatter-add x4 -> x0, other arithmetic: 209 us -> none  [the longest x2 159 us: per_device(): jax.ops.segment_sum(spread.reshape(-1, block_size, state_cols), sources,...]
    all_to_all x5 -> x0, blocking collectives: 135 us -> none  [the longest x1 82.7 us: per_device(): lax.all_to_all(blocks[asked], 'mesh', split_axis=0, concat_axis=0, tiled=...]
    dot_general x7 -> x0, matrix products: 61 us -> none  [the longest x2 32.7 us: per_device(): jnp.einsum('rkab,rac->rkbc', kern_blocks, returned, preferred_element_typ...]
    reshape x4 -> x2, local copies, waits for them, and re-layouts: 49.9 us -> 0.2 us  [the longest x1 0.1 us: per_device(): lax.all_to_all(requests, 'mesh', split_axis=0, concat_axis=0, tiled=True)]
    gather x4 -> x1, local copies, waits for them, and re-layouts: 44.5 us -> 0.57 us  [arrival_order(): places = asked.reshape(peers, FAR)[deltas].reshape(-1)]
    all_to_all x3 -> x0, starting transfers between devices: 29.6 us -> none  [the longest x2 23.7 us: per_device(): lax.all_to_all(outgoing, 'mesh', split_axis=0, concat_axis=0, tiled=True)]
  transfers between devices with their start and end apart: 4 -> 1, of which waited for: 4 -> 1; matrix products, arithmetic and copies ran while one was open for 0% -> 0% of each run, Pallas kernels for 0% -> 0%
where the time goes in v2:
time: 261 us; the launch traced here: 260 us
  Pallas kernels  236 us (90%)
  starting transfers between devices  8.59 us (3%)
  local copies, waits for them, and re-layouts  6.47 us (2%)
  waiting for transfers between devices  6.21 us (2%)
    pallas_call x3, Pallas kernels, exchange(): pl.pallas_call(functools.partial(exchange_kernel, mode, with_u, peers, st...  194 us
    pallas_call x2, Pallas kernels, backward(): pl.pallas_call(backward_kernel, grid_spec=pltpu.PrefetchScalarGridSpec(nu...  41.9 us
    all_to_all x1, starting transfers between devices, per_device(): lax.all_to_all(requests, 'mesh', split_axis=0, concat_axis=0, tiled=True)  8.59 us
    all_to_all x1, waiting for transfers between devices, per_device(): lax.all_to_all(requests, 'mesh', split_axis=0, concat_axis=0, tiled=True)  6.21 us
  transfers between devices with their start and end apart: 1, of which 1 were waited for; matrix products, arithmetic and copies ran while one was open for 0% of the time, Pallas kernels for 0%

profile of v2, /device:TPU:1, one launch (start us, length us, event | category | flops | bytes accessed | tf_op | source)
XLA Modules:
  0.0 259.8 jit_solution(12519606213870986700)
XLA Ops:
  0.6 0.8 copy.17
  1.5 0.3 convert_reduce_fusion
  2.0 0.1 multiply_reduce_fusion
  2.2 0.7 copy.21
  2.9 8.6 %all-to-all-start = ((s32[32,1,2]{2,1,0:T(1,128)}), s32[32,1,2]{2,1,0:T(1,128)S(1)}, u32[]{:S(2)}, u32[]{:S(2)}) async-start(s32[32,1,2]{2,1,0:T(1,128)} %copy.21), calls=%async_computation | async-start | bytes 32768 | tf_op jit(solution)/shard_map/all_to_all | solution.py:405
  11.5 0.1 mul.97
  11.6 0.4 select_reduce_fusion
  12.1 6.2 %all-to-all-done = s32[32,1,2]{2,1,0:T(1,128)S(1)} async-done(((s32[32,1,2]{2,1,0:T(1,128)}), s32[32,1,2]{2,1,0:T(1,128)S(1)}, u32[]{:S(2)}, u32[]{:S(2)}) %all-to-all-start) | async-done | bytes 288 | tf_op jit(solution)/shard_map/all_to_all | solution.py:405
  18.3 0.6 gather_fusion
  18.9 0.1 reshape.152
  19.0 0.2 convert_reduce_fusion.1
  19.2 0.1 select_reduce_fusion.1
  19.3 0.1 select_reduce_fusion.3.refs_2_
  19.5 0.5 broadcast.196
  20.0 0.7 reduce.3
  20.7 0.1 reshape.154.refs_1_.refs_5_
  20.8 1.0 copy-done
  21.8 60.5 %exchange_first.1.b_ref = bf16[24,128,128]{2,1,0:T(8,128)(2,1)S(1)} custom-call(f32[24,128,128]{2,1,0:T(8,128)} %bitcast.14, s32[64]{0:T(128)S(1)} %reshape.154.refs_1_.refs_5_, s32[384]{0:T(512)S(1)} %select_select_fusion.refs_2_.src_ref.refs_6_, bf16[24,16,128,128]{3,2,1,0:T(8,128)(2,1)} %kern_ref.3, bf16[512,512]{1,0:T(8,128)(2,1)S(1)} %copy-done, ...), custom_call_target="tpu_custom_call" | custom-call | tf_op jit(solution)/shard_map/exchange_first/pallas_call | solution.py:445
  82.4 20.9 %backward.2.refs_3_ = bf16[94,128,128]{2,1,0:T(8,128)(2,1)} custom-call(s32[384]{0:T(512)S(1)} %select_select_fusion.refs_2_.src_ref.refs_6_, bf16[24,16,128,128]{3,2,1,0:T(8,128)(2,1)} %kern_ref.3, bf16[24,128,128]{2,1,0:T(8,128)(2,1)S(1)} %exchange_first.1.b_ref), custom_call_target="tpu_custom_call" | custom-call | tf_op jit(solution)/shard_map/backward/pallas_call | solution.py:458
  103.4 92.0 %exchange_mid.1 = (bf16[24,128,128]{2,1,0:T(8,128)(2,1)S(1)}, f32[768,512]{1,0:T(8,128)}) custom-call(s32[58]{0:T(128)S(1)} %get-tuple-element.9.refs_0_, s32[58]{0:T(128)S(1)} %add_convert_fusion.refs_1_, s32[24]{0:T(128)S(1)} %select_reduce_fusion.3.refs_2_, bf16[94,128,128]{2,1,0:T(8,128)(2,1)} %backward.2.refs_3_, f32[24,128,128]{2,1,0:T(8,128)} %bitcast.11, ...), custom_call_target="tpu_custom_call" | custom-call | tf_op jit(solution)/shard_map/exchange_mid/pallas_call | solution.py:445
  195.4 20.9 %backward.3.refs_3_ = bf16[94,128,128]{2,1,0:T(8,128)(2,1)} custom-call(s32[384]{0:T(512)S(1)} %select_select_fusion.refs_2_.src_ref.refs_6_, bf16[24,16,128,128]{3,2,1,0:T(8,128)(2,1)} %kern_ref.3, bf16[24,128,128]{2,1,0:T(8,128)(2,1)S(1)} %get-tuple-element.5.b_ref), custom_call_target="tpu_custom_call" | custom-call | tf_op jit(solution)/shard_map/backward/pallas_call | solution.py:458
  216.3 41.2 %exchange_last.1 = f32[24,128,128]{2,1,0:T(8,128)S(1)} custom-call(s32[58]{0:T(128)S(1)} %get-tuple-element.9.refs_0_, s32[58]{0:T(128)S(1)} %add_convert_fusion.refs_1_, s32[24]{0:T(128)S(1)} %select_reduce_fusion.3.refs_2_, bf16[94,128,128]{2,1,0:T(8,128)(2,1)} %backward.3.refs_3_, f32[24,128,128]{2,1,0:T(8,128)} %bitcast.12), custom_call_target="tpu_custom_call" | custom-call | tf_op jit(solution)/shard_map/exchange_last/pallas_call | solution.py:445
  257.5 1.1 copy.28
  258.7 1.1 copy.29
  (17 shorter events, 0.6 us)
Async XLA Ops:
  2.9 15.5 %all-to-all-start = ((s32[32,1,2]{2,1,0:T(1,128)}), s32[32,1,2]{2,1,0:T(1,128)S(1)}, u32[]{:S(2)}, u32[]{:S(2)}) async-start(s32[32,1,2]{2,1,0:T(1,128)} %copy.21), calls=%async_computation | async-start | bytes 32768 | tf_op jit(solution)/shard_map/all_to_all | solution.py:405
  20.8 1.0 copy-start
  216.3 41.2 %copy-start.1 = (f32[768,512]{1,0:T(8,128)S(1)}, f32[768,512]{1,0:T(8,128)}, u32[]{:S(2)}) copy-start(f32[768,512]{1,0:T(8,128)} %get-tuple-element.14) | copy-start | bytes 4718596

commit v3 on v0

v3 whole, which is shorter than its diff:
```python
import functools
import jax
import jax.numpy as jnp
from jax import lax
from jax.experimental import pallas as pl
from jax.experimental.pallas import tpu as pltpu
from jax.sharding import PartitionSpec as P

ITERS = 2
NEAR = 6
FAR = 2
LAG = 2
VMEM_LIMIT = 60 * 1024 * 1024
F32 = jnp.float32
BF16 = jnp.bfloat16


def vmem():
    return pl.BlockSpec(memory_space=pltpu.VMEM)


def smem():
    return pl.BlockSpec(memory_space=pltpu.SMEM)


def hbm():
    return pl.BlockSpec(memory_space=pl.ANY)


def far_plan(flat_cols, me, peers, rows):
    owners = flat_cols // rows
    places = flat_cols % rows
    delta = (owners - me + peers) % peers
    is_own = delta == 0
    is_left = delta == peers - 1
    is_right = delta == 1
    is_far = ~(is_own | is_left | is_right)
    ids = jnp.arange(peers * rows, dtype=jnp.int32)
    hits = (flat_cols[:, None] == ids[None, :]) & is_far[:, None]
    needed = jnp.max(hits.astype(jnp.int32), axis=0).reshape(peers, rows)
    before = jnp.arange(rows)[:, None] < jnp.arange(rows)[None, :]
    ranks = jnp.sum(needed[:, :, None] * before[None].astype(jnp.int32), axis=1)
    place_ids = jnp.arange(rows, dtype=jnp.int32)
    requests = jnp.stack(
        [jnp.sum(needed * (ranks == s) * place_ids[None, :], axis=1) for s in range(FAR)],
        axis=1,
    )
    slots = jnp.sum(hits.astype(jnp.int32) * ranks.reshape(1, -1), axis=1)
    far_at = rows + 2 * NEAR + (delta - 2) * FAR + slots
    sources = jnp.where(
        is_own,
        places,
        jnp.where(
            is_left,
            rows + places - (rows - NEAR),
            jnp.where(is_right, rows + NEAR + places, far_at),
        ),
    )
    return sources.astype(jnp.int32), requests.astype(jnp.int32)


def ordered_sums(keys, bins):
    count = keys.shape[0]
    ids = jnp.arange(count, dtype=jnp.int32)
    full = keys * count + ids
    rank = jnp.sum((full[None, :] < full[:, None]).astype(jnp.int32), axis=1)
    here = (rank[:, None] == ids[None, :]).astype(jnp.int32)
    perm = jnp.sum(here * ids[:, None], axis=0)
    bin_ids = jnp.arange(bins, dtype=jnp.int32)[:, None]
    upto = jnp.sum((keys[None, :] <= bin_ids).astype(jnp.int32), axis=1)
    some = jnp.any(keys[None, :] == bin_ids, axis=1)
    return perm, jnp.where(some, upto - 1, -1)


def ask_kernel(peers, want_ref, got_ref, inbox, send_sem, recv_sem):
    me = lax.axis_index("mesh")
    barrier = pltpu.get_barrier_semaphore()

    def greet(o, _):
        pl.semaphore_signal(barrier, inc=1, device_id={"mesh": lax.rem(me + o, peers)})
        return 0

    lax.fori_loop(1, peers, greet, 0)
    pl.semaphore_wait(barrier, peers - 1)

    def ask(o):
        q = lax.rem(me + o, peers)
        return pltpu.make_async_remote_copy(
            src_ref=want_ref.at[q],
            dst_ref=inbox.at[me],
            send_sem=send_sem.at[o],
            recv_sem=recv_sem.at[o],
            device_id={"mesh": q},
        )

    def start(o, _):
        ask(o).start()
        return 0

    def wait(o, _):
        ask(o).wait_recv()
        ask(o).wait_send()
        return 0

    inbox[me] = want_ref[me]
    lax.fori_loop(1, peers, start, 0)
    lax.fori_loop(1, peers, wait, 0)
    got_ref[...] = inbox[...]


def solve_kernel(
    sweeps, peers, states,
    asked_ref, arr_perm, arr_last, arr_place, src_ref, pair_perm, pair_last,
    start_hbm, kern_hbm, mix_hbm, mu_hbm, nu_hbm,
    u_hbm, v_hbm,
    kern, mix, u_ref, v_ref, table, blocks, outbox, products, sums, arrived, running,
    a_out, a_in, b_out, b_in,
    local_sem, near_send, near_recv, far_send, far_recv,
    back_near_send, back_near_recv, back_far_send, back_far_recv,
    a_send, a_recv, b_send, b_recv,
):
    me = lax.axis_index("mesh")
    mz = lax.axis_index("state")
    rows, degree, size, _ = kern.shape
    cols = table.shape[2]
    per = rows // states
    far0 = rows + 2 * NEAR
    others = peers - 3
    right = lax.rem(me + 1, peers)
    left = lax.rem(me + peers - 1, peers)

    kern_copy = pltpu.make_async_copy(kern_hbm, kern, local_sem.at[0])
    mix_copy = pltpu.make_async_copy(mix_hbm, mix, local_sem.at[1])
    mu_copy = pltpu.make_async_copy(mu_hbm, u_ref, local_sem.at[2])
    nu_copy = pltpu.make_async_copy(nu_hbm, v_ref, local_sem.at[3])
    u_copy = pltpu.make_async_copy(u_ref, u_hbm, local_sem.at[4])
    v_copy = pltpu.make_async_copy(v_ref, v_hbm, local_sem.at[5])
    start_copy = pltpu.make_async_copy(start_hbm, v_ref, local_sem.at[6])
    start_copy.start()

    barrier = pltpu.get_barrier_semaphore()

    def greet(o, _):
        pl.semaphore_signal(barrier, inc=1, device_id={"mesh": lax.rem(me + o, peers)})
        return 0

    lax.fori_loop(1, peers, greet, 0)
    for j in range(1, states):
        pl.semaphore_signal(barrier, inc=1, device_id={"state": lax.rem(mz + j, states)})

    start_copy.wait()
    kern_copy.start()
    mix_copy.start()

    def cast(p, _):
        v = v_ref[p].astype(BF16)
        table[p] = v
        blocks[p] = v
        return 0

    lax.fori_loop(0, rows, cast, 0)
    pl.semaphore_wait(barrier, peers - 1 + states - 1)

    def every(body):
        def one(i, _):
            body(2 + lax.rem(i * 12, others))
            return 0

        lax.fori_loop(0, others, one, 0)

    def fwd_near(k):
        return pltpu.make_async_remote_copy(
            src_ref=blocks.at[pl.ds((rows - NEAR, 0)[k], NEAR)],
            dst_ref=table.at[pl.ds(rows + k * NEAR, NEAR)],
            send_sem=near_send.at[k],
            recv_sem=near_recv.at[k],
            device_id={"mesh": (right, left)[k]},
        )

    def fwd_far(o):
        at = peers - o
        return pltpu.make_async_remote_copy(
            src_ref=outbox.at[pl.ds(2 * NEAR + (o - 2) * FAR, FAR)],
            dst_ref=table.at[pl.ds(far0 + (at - 2) * FAR, FAR)],
            send_sem=far_send.at[o],
            recv_sem=far_recv.at[at],
            device_id={"mesh": lax.rem(me + o, peers)},
        )

    def back_near(k):
        return pltpu.make_async_remote_copy(
            src_ref=outbox.at[pl.ds(k * NEAR, NEAR)],
            dst_ref=arrived.at[pl.ds(k * NEAR, NEAR)],
            send_sem=back_near_send.at[k],
            recv_sem=back_near_recv.at[k],
            device_id={"mesh": (left, right)[k]},
        )

    def back_far(o):
        at = peers - o
        return pltpu.make_async_remote_copy(
            src_ref=outbox.at[pl.ds(2 * NEAR + (o - 2) * FAR, FAR)],
            dst_ref=arrived.at[pl.ds(2 * NEAR + (at - 2) * FAR, FAR)],
            send_sem=back_far_send.at[o],
            recv_sem=back_far_recv.at[at],
            device_id={"mesh": lax.rem(me + o, peers)},
        )

    def a_copy(j, sub):
        to = lax.rem(mz + j, states)
        return pltpu.make_async_remote_copy(
            src_ref=a_out.at[to, sub],
            dst_ref=a_in.at[mz, sub],
            send_sem=a_send.at[j, sub],
            recv_sem=a_recv.at[j, sub],
            device_id={"state": to},
        )

    def b_copy(j, sub):
        to = lax.rem(mz + j, states)
        return pltpu.make_async_remote_copy(
            src_ref=b_out.at[to, sub],
            dst_ref=b_in.at[mz, sub],
            send_sem=b_send.at[j, sub],
            recv_sem=b_recv.at[j, sub],
            device_id={"state": to},
        )

    def apply_rows(sub):
        for j in list(range(1, states)) + [0]:
            to = lax.rem(mz + j, states)
            r = to * per + sub
            lhs = jnp.concatenate([kern[r, k] for k in range(degree)], axis=1)
            rhs = jnp.concatenate(
                [table[src_ref[r * degree + k]] for k in range(degree)], axis=0
            )
            out = jnp.dot(lhs, rhs, preferred_element_type=F32).astype(BF16)
            if j == 0:
                a_in[mz, sub] = out
            else:
                a_out[to, sub] = out
                a_copy(j, sub).start()

    def mix_rows(sub):
        for j in range(1, states):
            a_copy(j, sub).wait_recv()
        a = jnp.concatenate([a_in[z, sub] for z in range(states)], axis=1)
        kv = lax.dot_general(a, mix[...], (((1,), (1,)), ((), ())), preferred_element_type=F32)
        at = pl.ds(pl.multiple_of(sub * size, size), size)
        u = u_ref[at, :] / kv
        u_ref[at, :] = u
        b = jnp.dot(u.astype(BF16), mix[...], preferred_element_type=F32).astype(BF16)
        for z in range(states):
            b_out[z, sub] = b[:, z * cols : (z + 1) * cols]
        for j in range(1, states):
            b_copy(j, sub).start()
        b_in[mz, sub] = b_out[mz, sub]

    def product_rows(sub):
        for j in range(1, states):
            b_copy(j, sub).wait_recv()
        for z in range(states):
            r = z * per + sub
            b = b_in[z, sub]
            for k in range(degree):
                products[r * degree + k] = lax.dot_general(
                    kern[r, k], b, (((0,), (0,)), ((), ())), preferred_element_type=F32
                ).astype(BF16)

    def chain(t, _):
        @pl.when(t < per)
        def _():
            apply_rows(t)

        @pl.when((t >= LAG) & (t < per + LAG))
        def _():
            mix_rows(t - LAG)

        @pl.when(t >= 2 * LAG)
        def _():
            product_rows(t - 2 * LAG)

        return 0

    def pick(ref, at):
        got = ref[jnp.maximum(at, 0)].astype(F32)
        return jnp.where(at >= 0, got, jnp.zeros_like(got))

    def sweep(s, _):
        mu_copy.start()
        nu_copy.start()

        def send(o):
            q = lax.rem(me + o, peers)
            for f in range(FAR):
                outbox[2 * NEAR + (o - 2) * FAR + f] = blocks[asked_ref[q * FAR + f]]
            fwd_far(o).start()

        for k in range(2):
            fwd_near(k).start()
        every(send)

        @pl.when(s == 0)
        def _():
            kern_copy.wait()
            mix_copy.wait()

        mu_copy.wait()
        nu_copy.wait()
        for k in range(2):
            fwd_near(k).wait_recv()
        every(lambda o: fwd_far(o).wait_recv())
        for k in range(2):
            fwd_near(k).wait_send()
        every(lambda o: fwd_far(o).wait_send())

        lax.fori_loop(0, per + 2 * LAG, chain, 0)
        u_copy.start()

        def add_pair(i, carry):
            acc, before = carry
            for h in range(4):
                p = pair_perm[i * 4 + h]
                now = src_ref[p]
                kept = jnp.where(now == before, acc, jnp.zeros_like(acc))
                acc = kept + products[p].astype(F32)
                sums[i * 4 + h] = acc.astype(BF16)
                before = now
            return acc, before

        lax.fori_loop(
            0, rows * degree // 4, add_pair, (jnp.zeros((size, cols), F32), jnp.int32(-1))
        )

        def pack_near(i, _):
            outbox[i] = pick(sums, pair_last[rows + i]).astype(BF16)
            return 0

        lax.fori_loop(0, 2 * NEAR, pack_near, 0)
        for k in range(2):
            back_near(k).start()

        def give(o):
            for f in range(FAR):
                i = 2 * NEAR + (o - 2) * FAR + f
                outbox[i] = pick(sums, pair_last[rows + i]).astype(BF16)
            back_far(o).start()

        every(give)

        def settle(sub, _):
            for j in range(1, states):
                a_copy(j, sub).wait_send()
                b_copy(j, sub).wait_send()
            return 0

        lax.fori_loop(0, per, settle, 0)
        u_copy.wait()
        for k in range(2):
            back_near(k).wait_recv()
        every(lambda o: back_far(o).wait_recv())
        for k in range(2):
            back_near(k).wait_send()
        every(lambda o: back_far(o).wait_send())

        def add_arrived(i, carry):
            acc, before = carry
            e = arr_perm[i]
            now = arr_place[e]
            kept = jnp.where(now == before, acc, jnp.zeros_like(acc))
            acc = kept + arrived[2 * NEAR + e].astype(F32)
            running[i] = acc
            return acc, now

        lax.fori_loop(
            0, others * FAR, add_arrived, (jnp.zeros((size, cols), F32), jnp.int32(-1))
        )

        def finish(p, near):
            total = pick(sums, pair_last[p]) + pick(running, arr_last[p])
            if near is not None:
                total = total + arrived[near].astype(F32)
            v = v_ref[p] / total
            v_ref[p] = v
            rounded = v.astype(BF16)
            table[p] = rounded
            blocks[p] = rounded
            return 0

        lax.fori_loop(0, NEAR, lambda p, _: finish(p, NEAR + p), 0)
        lax.fori_loop(NEAR, rows - NEAR, lambda p, _: finish(p, None), 0)
        lax.fori_loop(rows - NEAR, rows, lambda p, _: finish(p, p - (rows - NEAR)), 0)
        return 0

    lax.fori_loop(0, sweeps, sweep, 0)
    v_copy.start()
    v_copy.wait()


def per_device(kern_blocks, kern_cols, state_kernel, start_v, mu, nu):
    rows, degree, size, _ = kern_blocks.shape
    local_rows, cols = start_v.shape
    peers = lax.axis_size("mesh")
    states = lax.axis_size("state")
    me = lax.axis_index("mesh")
    per = rows // states
    nfar = (peers - 3) * FAR
    table_size = rows + 2 * NEAR + nfar
    nodes = states * cols
    dma = pltpu.SemaphoreType.DMA
    sources, requests = far_plan(kern_cols.reshape(-1), me, peers, rows)
    want = jnp.pad(requests, ((0, 0), (0, cols - FAR))).reshape(peers, 1, cols)
    got = pl.pallas_call(
        functools.partial(ask_kernel, peers),
        out_shape=jax.ShapeDtypeStruct((peers, 1, cols), jnp.int32),
        in_specs=[vmem()],
        out_specs=vmem(),
        scratch_shapes=[pltpu.VMEM((peers, 1, cols), jnp.int32), dma((peers,)), dma((peers,))],
        compiler_params=pltpu.CompilerParams(collective_id=0, has_side_effects=True),
        name="ask",
    )(want)
    asked = got[:, 0, :FAR]
    pair_perm, pair_last = ordered_sums(sources, table_size)
    deltas = (me + jnp.arange(2, peers - 1, dtype=jnp.int32)) % peers
    arr_place = asked[deltas].reshape(-1)
    arr_perm, arr_last = ordered_sums(arr_place, rows)

    def scratch(*dims, dtype=BF16):
        return pltpu.VMEM(dims + (size, cols), dtype)

    potential_u, values = pl.pallas_call(
        functools.partial(solve_kernel, ITERS, peers, states),
        out_shape=(
            jax.ShapeDtypeStruct((local_rows // states, nodes), F32),
            jax.ShapeDtypeStruct((rows, size, cols), F32),
        ),
        in_specs=[smem()] * 7 + [hbm()] * 5,
        out_specs=(hbm(), hbm()),
        scratch_shapes=[
            pltpu.VMEM((rows, degree, size, size), BF16),
            pltpu.VMEM((nodes, nodes), BF16),
            pltpu.VMEM((local_rows // states, nodes), F32),
            scratch(rows, dtype=F32),
            scratch(table_size),
            scratch(rows),
            scratch(2 * NEAR + nfar),
            scratch(rows * degree),
            scratch(rows * degree),
            scratch(2 * NEAR + nfar),
            scratch(nfar, dtype=F32),
            scratch(states, per),
            scratch(states, per),
            scratch(states, per),
            scratch(states, per),
            dma((7,)),
            dma((2,)), dma((2,)), dma((peers,)), dma((peers,)),
            dma((2,)), dma((2,)), dma((peers,)), dma((peers,)),
            dma((states, per)), dma((states, per)), dma((states, per)), dma((states, per)),
        ],
        compiler_params=pltpu.CompilerParams(
            vmem_limit_bytes=VMEM_LIMIT, collective_id=1, has_side_effects=True
        ),
        name="solve",
    )(
        asked.reshape(-1), arr_perm, arr_last, arr_place, sources, pair_perm, pair_last,
        start_v.reshape(rows, size, cols), kern_blocks, state_kernel, mu,
        nu.reshape(rows, size, cols),
    )
    return (potential_u, values.reshape(local_rows, cols))


def solution(mesh):
    placed = (
        P("mesh", None, None, None),
        P("mesh", None),
        P(),
        P("mesh", "state"),
        P(("mesh", "state"), None),
        P("mesh", "state"),
    )
    return jax.shard_map(
        per_device,
        mesh=mesh,
        in_specs=placed,
        out_specs=(P(("mesh", "state"), None), P("mesh", "state")),
        check_vma=False,
    )
```

time: 862 us -> 198 us (0.23); the launches traced: 850 us -> 197 us
  other arithmetic: 266 us -> 4.31 us
  waiting for transfers between devices: 222 us -> 0 us
  Pallas kernels: 0 us -> 185 us
  blocking collectives: 135 us -> 0 us
  local copies, waits for them, and re-layouts: 128 us -> 7.86 us
  matrix products: 61 us -> 0 us
  starting transfers between devices: 38.2 us -> 0 us
    all_to_all x4 -> x0, waiting for transfers between devices: 222 us -> none  [the longest x2 144 us: per_device(): lax.all_to_all(outgoing, 'mesh', split_axis=0, concat_axis=0, tiled=True)]
    scatter-add x4 -> x0, other arithmetic: 209 us -> none  [the longest x2 159 us: per_device(): jax.ops.segment_sum(spread.reshape(-1, block_size, state_cols), sources,...]
    pallas_call x0 -> x2, Pallas kernels: none -> 185 us  [the longest x1 172 us: per_device(): pl.pallas_call(functools.partial(solve_kernel, ITERS, peers, states), out...]
    all_to_all x5 -> x0, blocking collectives: 135 us -> none  [the longest x1 82.7 us: per_device(): lax.all_to_all(blocks[asked], 'mesh', split_axis=0, concat_axis=0, tiled=...]
    dot_general x7 -> x0, matrix products: 61 us -> none  [the longest x2 32.7 us: per_device(): jnp.einsum('rkab,rac->rkbc', kern_blocks, returned, preferred_element_typ...]
    reshape x4 -> x1, local copies, waits for them, and re-layouts: 49.9 us -> 0.1 us  [per_device(): arr_place = asked[deltas].reshape(-1)]
    gather x4 -> x1, local copies, waits for them, and re-layouts: 44.5 us -> 0.57 us  [per_device(): arr_place = asked[deltas].reshape(-1)]
    all_to_all x4 -> x0, starting transfers between devices: 38.2 us -> none  [the longest x2 23.7 us: per_device(): lax.all_to_all(outgoing, 'mesh', split_axis=0, concat_axis=0, tiled=True)]
  transfers between devices with their start and end apart: 4 -> 0, of which waited for: 4 -> 0; matrix products, arithmetic and copies ran while one was open for 0% -> 0% of each run, Pallas kernels for 0% -> 0%
where the time goes in v3:
time: 198 us; the launch traced here: 197 us
  Pallas kernels  185 us (93%)
  local copies, waits for them, and re-layouts  7.86 us (4%)
  other arithmetic  4.31 us (2%)
    pallas_call x1, Pallas kernels, per_device(): pl.pallas_call(functools.partial(solve_kernel, ITERS, peers, states), out...  172 us
    pallas_call x1, Pallas kernels, per_device(): pl.pallas_call(functools.partial(ask_kernel, peers), out_shape=jax.ShapeD...  12.1 us
    unnamed x9, local copies, waits for them, and re-layouts  4.71 us

profile of v3, /device:TPU:1, one launch (start us, length us, event | category | flops | bytes accessed | tf_op | source)
XLA Modules:
  0.0 197.5 jit_solution(11886399950175847133)
XLA Ops:
  0.7 0.8 copy.21
  1.5 0.3 convert_reduce_fusion
  2.0 0.2 multiply_reduce_fusion
  2.3 0.4 select_reduce_fusion
  2.8 0.2 convert_reduce_fusion.1
  3.0 0.7 select_reduce_fusion.1.pair_perm
  3.8 0.1 fusion.1
  3.9 0.1 convert_reduce_fusion.2
  4.0 0.5 add_select_fusion.3.pair_last
  4.5 0.1 copy.25
  4.6 0.6 pad.4
  5.2 12.1 %ask.1 = s32[32,1,128]{2,1,0:T(1,128)} custom-call(s32[32,1,128]{2,1,0:T(1,128)} %bitcast.13), custom_call_target="tpu_custom_call" | custom-call | tf_op jit(solution)/shard_map/ask/pallas_call | solution.py:413
  17.3 0.8 fusion.8
  18.1 0.6 gather_fusion
  18.6 0.1 reshape.240.arr_place
  18.8 0.1 convert_reduce_fusion.4
  18.9 0.1 fusion.3
  19.0 0.5 add_select_fusion.4.arr_last
  19.5 0.2 convert_reduce_fusion.3
  19.7 0.7 select_reduce_fusion.2.arr_perm
  20.4 0.6 reshape_squeeze.3.asked_ref
  21.0 172.5 %solve.1 = (f32[768,512]{1,0:T(8,128)}, f32[24,128,128]{2,1,0:T(8,128)}) custom-call(s32[64]{0:T(128)} %reshape_squeeze.3.asked_ref, s32[58]{0:T(128)} %select_reduce_fusion.2.arr_perm, s32[24]{0:T(128)} %add_select_fusion.4.arr_last, s32[58]{0:T(128)} %copy-done.2, s32[384]{0:T(512)} %copy-done.1, s32[384]{0:T(512)} %select_reduce_fusion.1.pair_perm, ...), custom_call_target="tpu_custom_call" | custom-call | tf_op jit(solution)/shard_map/solve/pallas_call | solution.py:431
  193.5 2.8 %copy.32 = f32[768,512]{1,0:T(8,128)} copy(f32[768,512]{1,0:T(8,128)} %get-tuple-element.16) | data formatting | bytes 3145728
  196.3 1.1 copy.33
  (19 shorter events, 0.5 us)
Async XLA Ops:
  2.8 18.2 %copy-start.1 = (s32[384]{0:T(512)}, s32[384]{0:T(512)S(1)}, u32[]{:S(2)}) copy-start(s32[384]{0:T(512)S(1)} %get-tuple-element.9.src_ref) | copy-start | bytes 4612
  18.8 2.3 %copy-start.2 = (s32[58]{0:T(128)}, s32[58]{0:T(128)S(1)}, u32[]{:S(2)}) copy-start(s32[58]{0:T(128)S(1)} %reshape.240.arr_place) | copy-start | bytes 700
  193.5 2.8 %copy-start = (f32[24,128,128]{2,1,0:T(8,128)S(1)}, f32[24,128,128]{2,1,0:T(8,128)}, u32[]{:S(2)}) copy-start(f32[24,128,128]{2,1,0:T(8,128)} %get-tuple-element.5) | copy-start | bytes 4718596

commit v4 on v3

v4 whole, which is shorter than its diff:
```python
import functools
import jax
import jax.numpy as jnp
from jax import lax
from jax.experimental import pallas as pl
from jax.experimental.pallas import tpu as pltpu
from jax.sharding import PartitionSpec as P

ITERS = 2
NEAR = 6
FAR = 2
LAG = 2
VMEM_LIMIT = 60 * 1024 * 1024
F32 = jnp.float32
BF16 = jnp.bfloat16


def vmem():
    return pl.BlockSpec(memory_space=pltpu.VMEM)


def smem():
    return pl.BlockSpec(memory_space=pltpu.SMEM)


def hbm():
    return pl.BlockSpec(memory_space=pl.ANY)


def far_plan(flat_cols, me, peers, rows):
    owners = flat_cols // rows
    places = flat_cols % rows
    delta = (owners - me + peers) % peers
    is_own = delta == 0
    is_left = delta == peers - 1
    is_right = delta == 1
    is_far = ~(is_own | is_left | is_right)
    ids = jnp.arange(peers * rows, dtype=jnp.int32)
    hits = (flat_cols[:, None] == ids[None, :]) & is_far[:, None]
    needed = jnp.max(hits.astype(jnp.int32), axis=0).reshape(peers, rows)
    before = jnp.arange(rows)[:, None] < jnp.arange(rows)[None, :]
    ranks = jnp.sum(needed[:, :, None] * before[None].astype(jnp.int32), axis=1)
    place_ids = jnp.arange(rows, dtype=jnp.int32)
    requests = jnp.stack(
        [jnp.sum(needed * (ranks == s) * place_ids[None, :], axis=1) for s in range(FAR)],
        axis=1,
    )
    slots = jnp.sum(hits.astype(jnp.int32) * ranks.reshape(1, -1), axis=1)
    far_at = rows + 2 * NEAR + (delta - 2) * FAR + slots
    sources = jnp.where(
        is_own,
        places,
        jnp.where(
            is_left,
            rows + places - (rows - NEAR),
            jnp.where(is_right, rows + NEAR + places, far_at),
        ),
    )
    return sources.astype(jnp.int32), requests.astype(jnp.int32)


def ordered_sums(keys, bins):
    count = keys.shape[0]
    ids = jnp.arange(count, dtype=jnp.int32)
    full = keys * count + ids
    rank = jnp.sum((full[None, :] < full[:, None]).astype(jnp.int32), axis=1)
    here = (rank[:, None] == ids[None, :]).astype(jnp.int32)
    perm = jnp.sum(here * ids[:, None], axis=0)
    bin_ids = jnp.arange(bins, dtype=jnp.int32)[:, None]
    upto = jnp.sum((keys[None, :] <= bin_ids).astype(jnp.int32), axis=1)
    some = jnp.any(keys[None, :] == bin_ids, axis=1)
    return perm, jnp.where(some, upto - 1, -1)


def ask_kernel(peers, want_ref, got_ref, inbox, send_sem, recv_sem):
    me = lax.axis_index("mesh")
    barrier = pltpu.get_barrier_semaphore()

    def greet(o, _):
        pl.semaphore_signal(barrier, inc=1, device_id={"mesh": lax.rem(me + o, peers)})
        return 0

    lax.fori_loop(1, peers, greet, 0)
    pl.semaphore_wait(barrier, peers - 1)

    def ask(o):
        q = lax.rem(me + o, peers)
        return pltpu.make_async_remote_copy(
            src_ref=want_ref.at[q],
            dst_ref=inbox.at[me],
            send_sem=send_sem.at[o],
            recv_sem=recv_sem.at[o],
            device_id={"mesh": q},
        )

    def start(o, _):
        ask(o).start()
        return 0

    def wait(o, _):
        ask(o).wait_recv()
        ask(o).wait_send()
        return 0

    inbox[me] = want_ref[me]
    lax.fori_loop(1, peers, start, 0)
    lax.fori_loop(1, peers, wait, 0)
    got_ref[...] = inbox[...]


def solve_kernel(
    sweeps, peers, states,
    asked_ref, arr_perm, arr_last, arr_place, src_ref, pair_perm, pair_last,
    start_hbm, kern_hbm, mix_hbm, mix_t_hbm, mu_hbm, nu_hbm,
    u_ref, v_ref,
    kern, mix, mix_t, u_t, table_0, table_1, blocks_0, blocks_1, outbox, products, sums,
    arrived_0, arrived_1, running,
    a_out, a_in, b_out, b_in,
    local_sem, near_send, near_recv, far_send, far_recv,
    back_near_send, back_near_recv, back_far_send, back_far_recv,
    a_send, a_recv, b_send, b_recv,
):
    me = lax.axis_index("mesh")
    mz = lax.axis_index("state")
    rows, degree, size, _ = kern.shape
    table, blocks, arrived = (table_0, table_1), (blocks_0, blocks_1), (arrived_0, arrived_1)
    half = table_0.shape[1]
    per = rows // states
    far0 = rows + 2 * NEAR
    others = peers - 3
    right = lax.rem(me + 1, peers)
    left = lax.rem(me + peers - 1, peers)

    kern_copy = pltpu.make_async_copy(kern_hbm, kern, local_sem.at[0])
    mix_copy = pltpu.make_async_copy(mix_hbm, mix, local_sem.at[1])
    mix_t_copy = pltpu.make_async_copy(mix_t_hbm, mix_t, local_sem.at[2])
    mu_copy = pltpu.make_async_copy(mu_hbm, u_ref, local_sem.at[3])
    nu_copy = pltpu.make_async_copy(nu_hbm, v_ref, local_sem.at[4])
    start_copy = pltpu.make_async_copy(start_hbm, v_ref, local_sem.at[5])
    start_copy.start()

    barrier = pltpu.get_barrier_semaphore()

    def greet(o, _):
        pl.semaphore_signal(barrier, inc=1, device_id={"mesh": lax.rem(me + o, peers)})
        return 0

    lax.fori_loop(1, peers, greet, 0)
    for j in range(1, states):
        pl.semaphore_signal(barrier, inc=1, device_id={"state": lax.rem(mz + j, states)})

    start_copy.wait()
    kern_copy.start()
    mix_copy.start()
    mix_t_copy.start()

    def cast(p, _):
        v = v_ref[p].T.astype(BF16)
        for h in range(2):
            table[h][p] = v[h * half : (h + 1) * half]
            blocks[h][p] = v[h * half : (h + 1) * half]
        return 0

    lax.fori_loop(0, rows, cast, 0)
    pl.semaphore_wait(barrier, peers - 1 + states - 1)

    def every(body):
        def one(i, _):
            body(2 + lax.rem(i * 12, others))
            return 0

        lax.fori_loop(0, others, one, 0)

    def fwd_near(h, k):
        return pltpu.make_async_remote_copy(
            src_ref=blocks[h].at[pl.ds((rows - NEAR, 0)[k], NEAR)],
            dst_ref=table[h].at[pl.ds(rows + k * NEAR, NEAR)],
            send_sem=near_send.at[h, k],
            recv_sem=near_recv.at[h, k],
            device_id={"mesh": (right, left)[k]},
        )

    def fwd_far(h, o):
        at = peers - o
        return pltpu.make_async_remote_copy(
            src_ref=outbox.at[h, pl.ds(2 * NEAR + (o - 2) * FAR, FAR)],
            dst_ref=table[h].at[pl.ds(far0 + (at - 2) * FAR, FAR)],
            send_sem=far_send.at[h, o],
            recv_sem=far_recv.at[h, at],
            device_id={"mesh": lax.rem(me + o, peers)},
        )

    def back_near(h, k):
        return pltpu.make_async_remote_copy(
            src_ref=outbox.at[h, pl.ds(k * NEAR, NEAR)],
            dst_ref=arrived[h].at[pl.ds(k * NEAR, NEAR)],
            send_sem=back_near_send.at[h, k],
            recv_sem=back_near_recv.at[h, k],
            device_id={"mesh": (left, right)[k]},
        )

    def back_far(h, o):
        at = peers - o
        return pltpu.make_async_remote_copy(
            src_ref=outbox.at[h, pl.ds(2 * NEAR + (o - 2) * FAR, FAR)],
            dst_ref=arrived[h].at[pl.ds(2 * NEAR + (at - 2) * FAR, FAR)],
            send_sem=back_far_send.at[h, o],
            recv_sem=back_far_recv.at[h, at],
            device_id={"mesh": lax.rem(me + o, peers)},
        )

    def a_copy(h, j, sub):
        to = lax.rem(mz + j, states)
        return pltpu.make_async_remote_copy(
            src_ref=a_out.at[h, to, sub],
            dst_ref=a_in.at[h, mz, sub],
            send_sem=a_send.at[h, j, sub],
            recv_sem=a_recv.at[h, j, sub],
            device_id={"state": to},
        )

    def b_copy(h, j, sub):
        to = lax.rem(mz + j, states)
        return pltpu.make_async_remote_copy(
            src_ref=b_out.at[h, to, sub],
            dst_ref=b_in.at[h, mz, sub],
            send_sem=b_send.at[h, j, sub],
            recv_sem=b_recv.at[h, j, sub],
            device_id={"state": to},
        )

    def send_forward(h):
        for k in range(2):
            fwd_near(h, k).start()

        def send(o):
            q = lax.rem(me + o, peers)
            for f in range(FAR):
                outbox[h, 2 * NEAR + (o - 2) * FAR + f] = blocks[h][asked_ref[q * FAR + f]]
            fwd_far(h, o).start()

        every(send)

    def receive_forward(h):
        for k in range(2):
            fwd_near(h, k).wait_recv()
        every(lambda o: fwd_far(h, o).wait_recv())

    def forward_sent(h):
        for k in range(2):
            fwd_near(h, k).wait_send()
        every(lambda o: fwd_far(h, o).wait_send())

    def apply_rows(h, sub):
        for j in list(range(1, states)) + [0]:
            to = lax.rem(mz + j, states)
            r = to * per + sub
            lhs = jnp.concatenate(
                [table[h][src_ref[r * degree + k]] for k in range(degree)], axis=1
            )
            rhs = jnp.concatenate([kern[r, k] for k in range(degree)], axis=1)
            out = lax.dot_general(
                lhs, rhs, (((1,), (1,)), ((), ())), preferred_element_type=F32
            ).astype(BF16)
            if j == 0:
                a_in[h, mz, sub] = out
            else:
                a_out[h, to, sub] = out
                a_copy(h, j, sub).start()

    def mix_rows(sub):
        for h in range(2):
            for j in range(1, states):
                a_copy(h, j, sub).wait_recv()
        a = jnp.concatenate(
            [a_in[h, z, sub] for z in range(states) for h in range(2)], axis=0
        )
        kv = jnp.dot(mix[...], a, preferred_element_type=F32)
        at = pl.ds(pl.multiple_of(sub * size, size), size)
        u = u_ref[at, :].T / kv
        u_t[sub] = u
        b = jnp.dot(mix_t[...], u.astype(BF16), preferred_element_type=F32).astype(BF16)
        for z in range(states):
            for h in range(2):
                b_out[h, z, sub] = b[(2 * z + h) * half : (2 * z + h + 1) * half]
        for j in range(1, states):
            b_copy(0, j, sub).start()
        for h in range(2):
            b_in[h, mz, sub] = b_out[h, mz, sub]

    def product_rows(h, sub):
        for j in range(1, states):
            b_copy(h, j, sub).wait_recv()
        for z in range(states):
            r = z * per + sub
            b = b_in[h, z, sub]
            for k in range(0, degree, 2):
                rhs = jnp.concatenate([kern[r, k], kern[r, k + 1]], axis=1)
                both = jnp.dot(b, rhs, preferred_element_type=F32)
                products[r * degree + k] = both[:, :size]
                products[r * degree + k + 1] = both[:, size:]

    def chain(t, _):
        @pl.when(t < per)
        def _():
            apply_rows(1, t)

        @pl.when((t >= LAG) & (t < per + LAG))
        def _():
            mix_rows(t - LAG)

        @pl.when(t == per + LAG - 1)
        def _():
            def rest(sub, _):
                for j in range(1, states):
                    b_copy(1, j, sub).start()
                return 0

            lax.fori_loop(0, per, rest, 0)

        @pl.when(t >= 2 * LAG)
        def _():
            product_rows(0, t - 2 * LAG)

        return 0

    def zeros():
        return jnp.zeros((half, size), F32)

    def pick(got, at):
        return jnp.where(at >= 0, got.astype(F32), zeros())

    def sum_products(h):
        def add(i, carry):
            acc, before = carry
            for g in range(8):
                p = pair_perm[i * 8 + g]
                now = src_ref[p]
                acc = jnp.where(now == before, acc, zeros()) + products[p]
                sums[h, i * 8 + g] = acc.astype(BF16)
                before = now
            return acc, before

        lax.fori_loop(0, rows * degree // 8, add, (zeros(), jnp.int32(-1)))

    def send_back(h):
        def load(i):
            at = pair_last[rows + i]
            outbox[h, i] = pick(sums[h, jnp.maximum(at, 0)], at).astype(BF16)

        def pack_near(i, _):
            load(i)
            return 0

        lax.fori_loop(0, 2 * NEAR, pack_near, 0)
        for k in range(2):
            back_near(h, k).start()

        def give(o):
            for f in range(FAR):
                load(2 * NEAR + (o - 2) * FAR + f)
            back_far(h, o).start()

        every(give)

    def receive_back(h):
        for k in range(2):
            back_near(h, k).wait_recv()
        every(lambda o: back_far(h, o).wait_recv())
        for k in range(2):
            back_near(h, k).wait_send()
        every(lambda o: back_far(h, o).wait_send())

    def finish_all(h):
        def add(i, carry):
            acc, before = carry
            e = arr_perm[i]
            now = arr_place[e]
            acc = jnp.where(now == before, acc, zeros()) + arrived[h][2 * NEAR + e].astype(F32)
            running[i] = acc
            return acc, now

        lax.fori_loop(0, others * FAR, add, (zeros(), jnp.int32(-1)))

        def finish(p, near):
            at, far = pair_last[p], arr_last[p]
            total = pick(sums[h, jnp.maximum(at, 0)], at) + pick(running[jnp.maximum(far, 0)], far)
            if near is not None:
                total = total + arrived[h][near].astype(F32)
            v = v_ref[p, h * half : (h + 1) * half] / total
            v_ref[p, h * half : (h + 1) * half] = v
            rounded = v.astype(BF16)
            table[h][p] = rounded
            blocks[h][p] = rounded
            return 0

        lax.fori_loop(0, NEAR, lambda p, _: finish(p, NEAR + p), 0)
        lax.fori_loop(NEAR, rows - NEAR, lambda p, _: finish(p, None), 0)
        lax.fori_loop(rows - NEAR, rows, lambda p, _: finish(p, p - (rows - NEAR)), 0)

    for h in range(2):
        send_forward(h)

    def sweep(s, _):
        mu_copy.start()
        nu_copy.start()

        @pl.when(s == 0)
        def _():
            kern_copy.wait()
            mix_copy.wait()
            mix_t_copy.wait()

        mu_copy.wait()
        nu_copy.wait()

        def turn_nu(p, _):
            v_ref[p] = v_ref[p].T
            return 0

        lax.fori_loop(0, rows, turn_nu, 0)

        receive_forward(0)
        lax.fori_loop(0, per, lambda sub, _: (apply_rows(0, sub), 0)[1], 0)
        receive_forward(1)
        lax.fori_loop(0, per + 2 * LAG, chain, 0)
        for h in range(2):
            forward_sent(h)
        sum_products(0)
        send_back(0)
        lax.fori_loop(0, per, lambda sub, _: (product_rows(1, sub), 0)[1], 0)
        sum_products(1)
        send_back(1)

        def settle(sub, _):
            for h in range(2):
                for j in range(1, states):
                    a_copy(h, j, sub).wait_send()
                    b_copy(h, j, sub).wait_send()
            u_ref[pl.ds(pl.multiple_of(sub * size, size), size), :] = u_t[sub].T
            return 0

        lax.fori_loop(0, per, settle, 0)
        for h in range(2):
            receive_back(h)
            finish_all(h)

            @pl.when(s < sweeps - 1)
            def _():
                send_forward(h)

        return 0

    lax.fori_loop(0, sweeps, sweep, 0)


def per_device(kern_blocks, kern_cols, state_kernel, start_v, mu, nu):
    rows, degree, size, _ = kern_blocks.shape
    local_rows, cols = start_v.shape
    peers = lax.axis_size("mesh")
    states = lax.axis_size("state")
    me = lax.axis_index("mesh")
    per = rows // states
    nfar = (peers - 3) * FAR
    table_size = rows + 2 * NEAR + nfar
    nodes = states * cols
    dma = pltpu.SemaphoreType.DMA
    sources, requests = far_plan(kern_cols.reshape(-1), me, peers, rows)
    want = jnp.pad(requests, ((0, 0), (0, cols - FAR))).reshape(peers, 1, cols)
    got = pl.pallas_call(
        functools.partial(ask_kernel, peers),
        out_shape=jax.ShapeDtypeStruct((peers, 1, cols), jnp.int32),
        in_specs=[vmem()],
        out_specs=vmem(),
        scratch_shapes=[pltpu.VMEM((peers, 1, cols), jnp.int32), dma((peers,)), dma((peers,))],
        compiler_params=pltpu.CompilerParams(collective_id=0, has_side_effects=True),
        name="ask",
    )(want)
    asked = got[:, 0, :FAR]
    pair_perm, pair_last = ordered_sums(sources, table_size)
    deltas = (me + jnp.arange(2, peers - 1, dtype=jnp.int32)) % peers
    arr_place = asked[deltas].reshape(-1)
    arr_perm, arr_last = ordered_sums(arr_place, rows)

    half = cols // 2

    def scratch(*dims, dtype=BF16):
        return pltpu.VMEM(dims + (half, size), dtype)

    potential_u, values = pl.pallas_call(
        functools.partial(solve_kernel, ITERS, peers, states),
        out_shape=(
            jax.ShapeDtypeStruct((local_rows // states, nodes), F32),
            jax.ShapeDtypeStruct((rows, cols, size), F32),
        ),
        in_specs=[smem()] * 7 + [hbm()] * 6,
        out_specs=(vmem(), vmem()),
        scratch_shapes=[
            pltpu.VMEM((rows, degree, size, size), BF16),
            pltpu.VMEM((nodes, nodes), BF16),
            pltpu.VMEM((nodes, nodes), BF16),
            pltpu.VMEM((per, nodes, size), F32),
            scratch(table_size),
            scratch(table_size),
            scratch(rows),
            scratch(rows),
            scratch(2, 2 * NEAR + nfar),
            scratch(rows * degree, dtype=F32),
            scratch(2, rows * degree),
            scratch(2 * NEAR + nfar),
            scratch(2 * NEAR + nfar),
            scratch(nfar, dtype=F32),
            scratch(2, states, per),
            scratch(2, states, per),
            scratch(2, states, per),
            scratch(2, states, per),
            dma((6,)),
            dma((2, 2)), dma((2, 2)), dma((2, peers)), dma((2, peers)),
            dma((2, 2)), dma((2, 2)), dma((2, peers)), dma((2, peers)),
            dma((2, states, per)), dma((2, states, per)),
            dma((2, states, per)), dma((2, states, per)),
        ],
        compiler_params=pltpu.CompilerParams(
            vmem_limit_bytes=VMEM_LIMIT, collective_id=1, has_side_effects=True
        ),
        name="solve",
    )(
        asked.reshape(-1), arr_perm, arr_last, arr_place, sources, pair_perm, pair_last,
        start_v.reshape(rows, size, cols), kern_blocks, state_kernel, state_kernel.T, mu,
        nu.reshape(rows, size, cols),
    )
    return (potential_u, jnp.swapaxes(values, 1, 2).reshape(local_rows, cols))


def solution(mesh):
    placed = (
        P("mesh", None, None, None),
        P("mesh", None),
        P(),
        P("mesh", "state"),
        P(("mesh", "state"), None),
        P("mesh", "state"),
    )
    return jax.shard_map(
        per_device,
        mesh=mesh,
        in_specs=placed,
        out_specs=(P(("mesh", "state"), None), P("mesh", "state")),
        check_vma=False,
    )
```

time: 198 us -> 193 us (0.975)
  Pallas kernels: 185 us -> 177 us
  local copies, waits for them, and re-layouts: 7.86 us -> 10.3 us
    pallas_call x1, Pallas kernels: 172 us -> 165 us  [per_device(): pl.pallas_call(functools.partial(solve_kernel, ITERS, peers, states), out...]
    transpose x0 -> x1, local copies, waits for them, and re-layouts: none -> 3.14 us  [per_device(): return (potential_u, jnp.swapaxes(values, 1, 2).reshape(local_rows, cols))]
where the time goes in v4:
time: 193 us; the launch traced here: 192 us
  Pallas kernels  177 us (92%)
  local copies, waits for them, and re-layouts  10.3 us (5%)
  other arithmetic  4.2 us (2%)
    pallas_call x1, Pallas kernels, per_device(): pl.pallas_call(functools.partial(solve_kernel, ITERS, peers, states), out...  165 us
    pallas_call x1, Pallas kernels, per_device(): pl.pallas_call(functools.partial(ask_kernel, peers), out_shape=jax.ShapeD...  12.1 us
    unnamed x9, local copies, waits for them, and re-layouts  3.97 us

profile of v4, /device:TPU:1, one launch (start us, length us, event | category | flops | bytes accessed | tf_op | source)
XLA Modules:
  0.0 192.3 jit_solution(1735984811732224571)
XLA Ops:
  0.7 0.8 copy.26
  1.5 0.3 convert_reduce_fusion
  2.0 0.2 multiply_reduce_fusion
  2.3 0.4 select_reduce_fusion
  2.8 0.2 convert_reduce_fusion.1
  3.0 0.7 select_reduce_fusion.1.pair_perm
  3.8 0.1 fusion.1
  3.9 0.1 convert_reduce_fusion.2
  4.0 0.5 add_select_fusion.3.pair_last
  4.6 0.6 pad.4
  5.2 12.1 %ask.1 = s32[32,1,128]{2,1,0:T(1,128)} custom-call(s32[32,1,128]{2,1,0:T(1,128)} %bitcast.17), custom_call_target="tpu_custom_call" | custom-call | tf_op jit(solution)/shard_map/ask/pallas_call | solution.py:470
  17.3 0.8 fusion.8
  18.1 0.6 gather_fusion
  18.6 0.1 reshape.240.arr_place
  18.8 0.1 convert_reduce_fusion.4
  18.9 0.1 fusion.3
  19.0 0.5 add_select_fusion.4.arr_last
  19.5 0.2 convert_reduce_fusion.3
  19.7 0.6 select_reduce_fusion.2.arr_perm
  20.3 0.7 reshape_squeeze.3.asked_ref
  21.0 2.0 %copy.34 = bf16[512,512]{0,1:T(8,128)(2,1)} copy(bf16[512,512]{1,0:T(8,128)(2,1)} %mix_hbm.1) | data formatting | bytes 1048576 | tf_op args[2]
  23.0 165.0 %solve.1 = (f32[768,512]{1,0:T(8,128)}, f32[24,128,128]{2,1,0:T(8,128)}) custom-call(s32[64]{0:T(128)} %reshape_squeeze.3.asked_ref, s32[58]{0:T(128)} %select_reduce_fusion.2.arr_perm, s32[24]{0:T(128)} %add_select_fusion.4.arr_last, s32[58]{0:T(128)} %copy-done.2, s32[384]{0:T(512)} %copy-done.1, s32[384]{0:T(512)} %select_reduce_fusion.1.pair_perm, ...), custom_call_target="tpu_custom_call" | custom-call | tf_op jit(solution)/shard_map/solve/pallas_call | solution.py:490
  188.0 3.1 %copy.35 = f32[24,128,128]{2,1,0:T(8,128)} copy(f32[24,128,128]{1,2,0:T(8,128)} %bitcast.14) | data formatting | bytes 3145728 | tf_op jit(solution)/shard_map/transpose | solution.py:532
  191.2 1.1 copy.38
  (20 shorter events, 0.6 us)
Async XLA Ops:
  2.8 20.2 %copy-start.1 = (s32[384]{0:T(512)}, s32[384]{0:T(512)S(1)}, u32[]{:S(2)}) copy-start(s32[384]{0:T(512)S(1)} %get-tuple-element.9.src_ref) | copy-start | bytes 4612
  18.8 4.3 %copy-start.2 = (s32[58]{0:T(128)}, s32[58]{0:T(128)S(1)}, u32[]{:S(2)}) copy-start(s32[58]{0:T(128)S(1)} %reshape.240.arr_place) | copy-start | bytes 700
  188.0 3.2 %copy-start = (f32[768,512]{1,0:T(8,128)S(1)}, f32[768,512]{1,0:T(8,128)}, u32[]{:S(2)}) copy-start(f32[768,512]{1,0:T(8,128)} %get-tuple-element.16) | copy-start | bytes 4718596

commit v5 on v4

--- a/solution.py
+++ b/solution.py
@@ -72,53 +72,17 @@
     return perm, jnp.where(some, upto - 1, -1)
 
 
-def ask_kernel(peers, want_ref, got_ref, inbox, send_sem, recv_sem):
-    me = lax.axis_index("mesh")
-    barrier = pltpu.get_barrier_semaphore()
-
-    def greet(o, _):
-        pl.semaphore_signal(barrier, inc=1, device_id={"mesh": lax.rem(me + o, peers)})
-        return 0
-
-    lax.fori_loop(1, peers, greet, 0)
-    pl.semaphore_wait(barrier, peers - 1)
-
-    def ask(o):
-        q = lax.rem(me + o, peers)
-        return pltpu.make_async_remote_copy(
-            src_ref=want_ref.at[q],
-            dst_ref=inbox.at[me],
-            send_sem=send_sem.at[o],
-            recv_sem=recv_sem.at[o],
-            device_id={"mesh": q},
-        )
-
-    def start(o, _):
-        ask(o).start()
-        return 0
-
-    def wait(o, _):
-        ask(o).wait_recv()
-        ask(o).wait_send()
-        return 0
-
-    inbox[me] = want_ref[me]
-    lax.fori_loop(1, peers, start, 0)
-    lax.fori_loop(1, peers, wait, 0)
-    got_ref[...] = inbox[...]
-
-
 def solve_kernel(
     sweeps, peers, states,
-    asked_ref, arr_perm, arr_last, arr_place, src_ref, pair_perm, pair_last,
+    want_ref, src_ref, pair_perm, pair_last,
     start_hbm, kern_hbm, mix_hbm, mix_t_hbm, mu_hbm, nu_hbm,
     u_ref, v_ref,
     kern, mix, mix_t, u_t, table_0, table_1, blocks_0, blocks_1, outbox, products, sums,
-    arrived_0, arrived_1, running,
+    arrived_0, arrived_1, running, inbox, asked, arr_key, arr_count,
     a_out, a_in, b_out, b_in,
     local_sem, near_send, near_recv, far_send, far_recv,
     back_near_send, back_near_recv, back_far_send, back_far_recv,
-    a_send, a_recv, b_send, b_recv,
+    a_send, a_recv, b_send, b_recv, ask_send, ask_recv,
 ):
     me = lax.axis_index("mesh")
     mz = lax.axis_index("state")
@@ -149,6 +113,28 @@
     for j in range(1, states):
         pl.semaphore_signal(barrier, inc=1, device_id={"state": lax.rem(mz + j, states)})
 
+    def ask(o):
+        q = lax.rem(me + o, peers)
+        return pltpu.make_async_remote_copy(
+            src_ref=want_ref.at[q],
+            dst_ref=inbox.at[me],
+            send_sem=ask_send.at[o],
+            recv_sem=ask_recv.at[o],
+            device_id={"mesh": q},
+        )
+
+    def ask_start(o, _):
+        ask(o).start()
+        return 0
+
+    def ask_wait(o, _):
+        ask(o).wait_recv()
+        ask(o).wait_send()
+        return 0
+
+    inbox[me] = want_ref[me]
+    pl.semaphore_wait(barrier, peers - 1 + states - 1)
+    lax.fori_loop(1, peers, ask_start, 0)
     start_copy.wait()
     kern_copy.start()
     mix_copy.start()
@@ -162,7 +148,10 @@
         return 0
 
     lax.fori_loop(0, rows, cast, 0)
-    pl.semaphore_wait(barrier, peers - 1 + states - 1)
+    lax.fori_loop(1, peers, ask_wait, 0)
+    asked_copy = pltpu.make_async_copy(inbox, asked, local_sem.at[6])
+    asked_copy.start()
+    asked_copy.wait()
 
     def every(body):
         def one(i, _):
@@ -236,7 +225,7 @@
         def send(o):
             q = lax.rem(me + o, peers)
             for f in range(FAR):
-                outbox[h, 2 * NEAR + (o - 2) * FAR + f] = blocks[h][asked_ref[q * FAR + f]]
+                outbox[h, 2 * NEAR + (o - 2) * FAR + f] = blocks[h][asked[q, 0, f]]
             fwd_far(h, o).start()
 
         every(send)
@@ -374,8 +363,8 @@
     def finish_all(h):
         def add(i, carry):
             acc, before = carry
-            e = arr_perm[i]
-            now = arr_place[e]
+            e = lax.rem(arr_key[i], base)
+            now = arr_key[i] // base
             acc = jnp.where(now == before, acc, zeros()) + arrived[h][2 * NEAR + e].astype(F32)
             running[i] = acc
             return acc, now
@@ -383,7 +372,8 @@
         lax.fori_loop(0, others * FAR, add, (zeros(), jnp.int32(-1)))
 
         def finish(p, near):
-            at, far = pair_last[p], arr_last[p]
+            at = pair_last[p]
+            far = jnp.where(arr_count[p + 1] > arr_count[p], arr_count[p + 1] - 1, -1)
             total = pick(sums[h, jnp.maximum(at, 0)], at) + pick(running[jnp.maximum(far, 0)], far)
             if near is not None:
                 total = total + arrived[h][near].astype(F32)
@@ -400,6 +390,27 @@
 
     for h in range(2):
         send_forward(h)
+
+    base = peers * FAR
+    peer_id = lax.broadcasted_iota(jnp.int32, inbox.shape, 0)
+    lane = lax.broadcasted_iota(jnp.int32, inbox.shape, 2)
+    ahead = lax.rem(peer_id - me + peers, peers)
+    real = (lane < FAR) & (ahead >= 2) & (ahead <= peers - 2)
+    beyond = rows * base
+    keys = jnp.where(real, inbox[...] * base + (ahead - 2) * FAR + lane, beyond)
+
+    def next_key(i, last):
+        key = jnp.min(jnp.where(keys > last, keys, beyond))
+        arr_key[i] = key
+        return key
+
+    lax.fori_loop(0, others * FAR, next_key, jnp.int32(-1))
+
+    def count(p, _):
+        arr_count[p] = jnp.sum((keys < p * base).astype(jnp.int32))
+        return 0
+
+    lax.fori_loop(0, rows + 1, count, 0)
 
     def sweep(s, _):
         mu_copy.start()
@@ -452,6 +463,12 @@
         return 0
 
     lax.fori_loop(0, sweeps, sweep, 0)
+
+    def turn_v(p, _):
+        v_ref[p] = v_ref[p].T
+        return 0
+
+    lax.fori_loop(0, rows, turn_v, 0)
 
 
 def per_device(kern_blocks, kern_cols, state_kernel, start_v, mu, nu):
@@ -467,21 +484,7 @@
     dma = pltpu.SemaphoreType.DMA
     sources, requests = far_plan(kern_cols.reshape(-1), me, peers, rows)
     want = jnp.pad(requests, ((0, 0), (0, cols - FAR))).reshape(peers, 1, cols)
-    got = pl.pallas_call(
-        functools.partial(ask_kernel, peers),
-        out_shape=jax.ShapeDtypeStruct((peers, 1, cols), jnp.int32),
-        in_specs=[vmem()],
-        out_specs=vmem(),
-        scratch_shapes=[pltpu.VMEM((peers, 1, cols), jnp.int32), dma((peers,)), dma((peers,))],
-        compiler_params=pltpu.CompilerParams(collective_id=0, has_side_effects=True),
-        name="ask",
-    )(want)
-    asked = got[:, 0, :FAR]
     pair_perm, pair_last = ordered_sums(sources, table_size)
-    deltas = (me + jnp.arange(2, peers - 1, dtype=jnp.int32)) % peers
-    arr_place = asked[deltas].reshape(-1)
-    arr_perm, arr_last = ordered_sums(arr_place, rows)
-
     half = cols // 2
 
     def scratch(*dims, dtype=BF16):
@@ -491,9 +494,9 @@
         functools.partial(solve_kernel, ITERS, peers, states),
         out_shape=(
             jax.ShapeDtypeStruct((local_rows // states, nodes), F32),
-            jax.ShapeDtypeStruct((rows, cols, size), F32),
+            jax.ShapeDtypeStruct((rows, size, cols), F32),
         ),
-        in_specs=[smem()] * 7 + [hbm()] * 6,
+        in_specs=[vmem()] + [smem()] * 3 + [hbm()] * 6,
         out_specs=(vmem(), vmem()),
         scratch_shapes=[
             pltpu.VMEM((rows, degree, size, size), BF16),
@@ -510,26 +513,31 @@
             scratch(2 * NEAR + nfar),
             scratch(2 * NEAR + nfar),
             scratch(nfar, dtype=F32),
+            pltpu.VMEM((peers, 1, cols), jnp.int32),
+            pltpu.SMEM((peers, 1, cols), jnp.int32),
+            pltpu.SMEM((nfar,), jnp.int32),
+            pltpu.SMEM((rows + 1,), jnp.int32),
             scratch(2, states, per),
             scratch(2, states, per),
             scratch(2, states, per),
             scratch(2, states, per),
-            dma((6,)),
+            dma((7,)),
             dma((2, 2)), dma((2, 2)), dma((2, peers)), dma((2, peers)),
             dma((2, 2)), dma((2, 2)), dma((2, peers)), dma((2, peers)),
             dma((2, states, per)), dma((2, states, per)),
             dma((2, states, per)), dma((2, states, per)),
+            dma((peers,)), dma((peers,)),
         ],
         compiler_params=pltpu.CompilerParams(
-            vmem_limit_bytes=VMEM_LIMIT, collective_id=1, has_side_effects=True
+            vmem_limit_bytes=VMEM_LIMIT, collective_id=0, has_side_effects=True
         ),
         name="solve",
     )(
-        asked.reshape(-1), arr_perm, arr_last, arr_place, sources, pair_perm, pair_last,
+        want, sources, pair_perm, pair_last,
         start_v.reshape(rows, size, cols), kern_blocks, state_kernel, state_kernel.T, mu,
         nu.reshape(rows, size, cols),
     )
-    return (potential_u, jnp.swapaxes(values, 1, 2).reshape(local_rows, cols))
+    return (potential_u, values.reshape(local_rows, cols))
 
 
 def solution(mesh):

time: 193 us -> 194 us (level)
  Pallas kernels: 177 us -> 183 us
  local copies, waits for them, and re-layouts: 10.3 us -> 7.84 us
    pallas_call x1, Pallas kernels: 165 us -> 183 us  [per_device(): pl.pallas_call(functools.partial(solve_kernel, ITERS, peers, states), out...]
    pallas_call x1 -> x0, Pallas kernels: 12.1 us -> none  [per_device(): pl.pallas_call(functools.partial(ask_kernel, peers), out_shape=jax.ShapeD...]
    transpose x1 -> x0, local copies, waits for them, and re-layouts: 3.14 us -> none  [per_device(): return (potential_u, jnp.swapaxes(values, 1, 2).reshape(local_rows, cols))]
    unnamed x9 -> x8, local copies, waits for them, and re-layouts: 3.97 us -> 6.75 us
where the time goes in v5:
time: 194 us
  Pallas kernels  183 us (94%)
  local copies, waits for them, and re-layouts  7.84 us (4%)
  other arithmetic  2.73 us (1%)
    pallas_call x1, Pallas kernels, per_device(): pl.pallas_call(functools.partial(solve_kernel, ITERS, peers, states), out...  183 us
    unnamed x8, local copies, waits for them, and re-layouts  6.75 us

profile of v5, /device:TPU:1, one launch (start us, length us, event | category | flops | bytes accessed | tf_op | source)
XLA Modules:
  0.0 193.9 jit_solution(6780241047668131672)
XLA Ops:
  0.6 0.8 copy.18
  1.4 0.1 eq.112
  1.5 0.3 convert_reduce_fusion
  1.8 0.1 mul.83
  1.9 0.1 copy.19
  2.0 0.2 multiply_reduce_fusion
  2.1 0.1 copy.23
  2.2 0.1 mul.94
  2.3 0.4 select_reduce_fusion
  2.8 0.0 copy-start.1
  2.8 0.2 convert_reduce_fusion.1
  3.0 0.7 select_reduce_fusion.1.pair_perm
  3.7 0.1 fusion.1
  3.8 0.1 convert_reduce_fusion.2
  4.0 0.6 add_select_fusion.3.pair_last
  4.6 0.1 copy.22
  4.7 0.6 pad.4
  5.3 2.0 %copy.24 = bf16[512,512]{0,1:T(8,128)(2,1)} copy(bf16[512,512]{1,0:T(8,128)(2,1)} %mix_hbm.1) | data formatting | bytes 1048576 | tf_op args[2]
  7.3 0.0 copy-done.1
  7.3 182.6 %solve.1 = (f32[768,512]{1,0:T(8,128)}, f32[24,128,128]{2,1,0:T(8,128)}) custom-call(s32[32,1,128]{2,1,0:T(1,128)} %bitcast.11, s32[384]{0:T(512)} %copy-done.1, s32[384]{0:T(512)} %select_reduce_fusion.1.pair_perm, s32[94]{0:T(128)} %add_select_fusion.3.pair_last, f32[24,128,128]{2,1,0:T(8,128)} %bitcast.8, bf16[24,16,128,128]{3,2,1,0:T(8,128)(2,1)} %kern_hbm.1, ...), custom_call_target="tpu_custom_call" | custom-call | tf_op jit(solution)/shard_map/solve/pallas_call | solution.py:493
  189.9 0.0 copy-start
  189.9 2.8 %copy.27 = f32[768,512]{1,0:T(8,128)} copy(f32[768,512]{1,0:T(8,128)} %get-tuple-element.14) | data formatting | bytes 3145728
  192.7 0.0 copy-done
  192.7 1.1 copy.28
  (5 shorter events, 0.1 us)
Async XLA Ops:
  2.8 4.5 %copy-start.1 = (s32[384]{0:T(512)}, s32[384]{0:T(512)S(1)}, u32[]{:S(2)}) copy-start(s32[384]{0:T(512)S(1)} %get-tuple-element.9.src_ref) | copy-start | bytes 4612
  189.9 2.8 %copy-start = (f32[24,128,128]{2,1,0:T(8,128)S(1)}, f32[24,128,128]{2,1,0:T(8,128)}, u32[]{:S(2)}) copy-start(f32[24,128,128]{2,1,0:T(8,128)} %get-tuple-element.5) | copy-start | bytes 4718596

commit v6 on v5

--- a/solution.py
+++ b/solution.py
@@ -9,7 +9,7 @@
 ITERS = 2
 NEAR = 6
 FAR = 2
-LAG = 2
+LAG = 1
 VMEM_LIMIT = 60 * 1024 * 1024
 F32 = jnp.float32
 BF16 = jnp.bfloat16
@@ -75,10 +75,10 @@
 def solve_kernel(
     sweeps, peers, states,
     want_ref, src_ref, pair_perm, pair_last,
-    start_hbm, kern_hbm, mix_hbm, mix_t_hbm, mu_hbm, nu_hbm,
+    start_hbm, kern_hbm, mix_hbm, mu_hbm, nu_hbm,
     u_ref, v_ref,
-    kern, mix, mix_t, u_t, table_0, table_1, blocks_0, blocks_1, outbox, products, sums,
-    arrived_0, arrived_1, running, inbox, asked, arr_key, arr_count,
+    kern, mix, mix_t, mu_t, u_t, table_0, table_1, blocks_0, blocks_1, outbox, products, sums,
+    arrived_0, arrived_1, running, inbox, packed, asked, arr_key, arr_count,
     a_out, a_in, b_out, b_in,
     local_sem, near_send, near_recv, far_send, far_recv,
     back_near_send, back_near_recv, back_far_send, back_far_recv,
@@ -97,7 +97,6 @@
 
     kern_copy = pltpu.make_async_copy(kern_hbm, kern, local_sem.at[0])
     mix_copy = pltpu.make_async_copy(mix_hbm, mix, local_sem.at[1])
-    mix_t_copy = pltpu.make_async_copy(mix_t_hbm, mix_t, local_sem.at[2])
     mu_copy = pltpu.make_async_copy(mu_hbm, u_ref, local_sem.at[3])
     nu_copy = pltpu.make_async_copy(nu_hbm, v_ref, local_sem.at[4])
     start_copy = pltpu.make_async_copy(start_hbm, v_ref, local_sem.at[5])
@@ -138,10 +137,10 @@
     start_copy.wait()
     kern_copy.start()
     mix_copy.start()
-    mix_t_copy.start()
+    mu_copy.start()
 
     def cast(p, _):
-        v = v_ref[p].T.astype(BF16)
+        v = v_ref[p].astype(BF16).T
         for h in range(2):
             table[h][p] = v[h * half : (h + 1) * half]
             blocks[h][p] = v[h * half : (h + 1) * half]
@@ -257,25 +256,33 @@
                 a_out[h, to, sub] = out
                 a_copy(h, j, sub).start()
 
-    def mix_rows(sub):
-        for h in range(2):
+    def mix_rows(t):
+        for i in range(2):
+            for h in range(2):
+                for j in range(1, states):
+                    a_copy(h, j, 2 * t + i).wait_recv()
+        a = jnp.concatenate(
+            [
+                jnp.concatenate([a_in[h, z, 2 * t + i] for i in range(2)], axis=1)
+                for z in range(states)
+                for h in range(2)
+            ],
+            axis=0,
+        )
+        kv = jnp.dot(mix[...], a, preferred_element_type=F32)
+        u = mu_t[t] / kv
+        u_t[t] = u
+        b = jnp.dot(mix_t[...], u.astype(BF16), preferred_element_type=F32).astype(BF16)
+        for i in range(2):
+            for z in range(states):
+                for h in range(2):
+                    b_out[h, z, 2 * t + i] = b[
+                        (2 * z + h) * half : (2 * z + h + 1) * half, i * size : (i + 1) * size
+                    ]
             for j in range(1, states):
-                a_copy(h, j, sub).wait_recv()
-        a = jnp.concatenate(
-            [a_in[h, z, sub] for z in range(states) for h in range(2)], axis=0
-        )
-        kv = jnp.dot(mix[...], a, preferred_element_type=F32)
-        at = pl.ds(pl.multiple_of(sub * size, size), size)
-        u = u_ref[at, :].T / kv
-        u_t[sub] = u
-        b = jnp.dot(mix_t[...], u.astype(BF16), preferred_element_type=F32).astype(BF16)
-        for z in range(states):
+                b_copy(0, j, 2 * t + i).start()
             for h in range(2):
-                b_out[h, z, sub] = b[(2 * z + h) * half : (2 * z + h + 1) * half]
-        for j in range(1, states):
-            b_copy(0, j, sub).start()
-        for h in range(2):
-            b_in[h, mz, sub] = b_out[h, mz, sub]
+                b_in[h, mz, 2 * t + i] = b_out[h, mz, 2 * t + i]
 
     def product_rows(h, sub):
         for j in range(1, states):
@@ -290,15 +297,18 @@
                 products[r * degree + k + 1] = both[:, size:]
 
     def chain(t, _):
-        @pl.when(t < per)
+        steps = per // 2
+
+        @pl.when(t < steps)
         def _():
-            apply_rows(1, t)
-
-        @pl.when((t >= LAG) & (t < per + LAG))
+            for i in range(2):
+                apply_rows(1, 2 * t + i)
+
+        @pl.when((t >= LAG) & (t < steps + LAG))
         def _():
             mix_rows(t - LAG)
 
-        @pl.when(t == per + LAG - 1)
+        @pl.when(t == steps + LAG - 1)
         def _():
             def rest(sub, _):
                 for j in range(1, states):
@@ -309,7 +319,8 @@
 
         @pl.when(t >= 2 * LAG)
         def _():
-            product_rows(0, t - 2 * LAG)
+            for i in range(2):
+                product_rows(0, 2 * (t - 2 * LAG) + i)
 
         return 0
 
@@ -392,37 +403,53 @@
         send_forward(h)
 
     base = peers * FAR
-    peer_id = lax.broadcasted_iota(jnp.int32, inbox.shape, 0)
-    lane = lax.broadcasted_iota(jnp.int32, inbox.shape, 2)
-    ahead = lax.rem(peer_id - me + peers, peers)
-    real = (lane < FAR) & (ahead >= 2) & (ahead <= peers - 2)
-    beyond = rows * base
-    keys = jnp.where(real, inbox[...] * base + (ahead - 2) * FAR + lane, beyond)
-
-    def next_key(i, last):
-        key = jnp.min(jnp.where(keys > last, keys, beyond))
-        arr_key[i] = key
-        return key
-
-    lax.fori_loop(0, others * FAR, next_key, jnp.int32(-1))
-
-    def count(p, _):
-        arr_count[p] = jnp.sum((keys < p * base).astype(jnp.int32))
-        return 0
-
-    lax.fori_loop(0, rows + 1, count, 0)
+
+    def order_arrivals():
+        for q in range(peers):
+            packed[q, :] = inbox[q, 0, :]
+        peer_id = lax.broadcasted_iota(jnp.int32, packed.shape, 0)
+        lane = lax.broadcasted_iota(jnp.int32, packed.shape, 1)
+        ahead = lax.rem(peer_id - me + peers, peers)
+        real = (lane < FAR) & (ahead >= 2) & (ahead <= peers - 2)
+        beyond = rows * base
+        keys = jnp.where(real, packed[...] * base + (ahead - 2) * FAR + lane, beyond)
+
+        def next_key(i, last):
+            key = jnp.min(jnp.where(keys > last, keys, beyond))
+            arr_key[i] = key
+            return key
+
+        lax.fori_loop(0, others * FAR, next_key, jnp.int32(-1))
+        arr_count[0] = 0
+
+        def count(i, _):
+            for g in range(4):
+                p = i * 4 + g + 1
+                arr_count[p] = jnp.sum((keys < p * base).astype(jnp.int32))
+            return 0
+
+        lax.fori_loop(0, rows // 4, count, 0)
 
     def sweep(s, _):
-        mu_copy.start()
         nu_copy.start()
 
         @pl.when(s == 0)
         def _():
+            mix_copy.wait()
+            mu_copy.wait()
+            for i in range(states):
+                for j in range(states):
+                    a, b = slice(i * size, (i + 1) * size), slice(j * size, (j + 1) * size)
+                    mix_t[a, b] = mix[b, a].T
+
+            def turn_mu(t, _):
+                for i in range(2):
+                    mu_t[t, :, i * size : (i + 1) * size] = u_ref[2 * t + i].T
+                return 0
+
+            lax.fori_loop(0, per // 2, turn_mu, 0)
             kern_copy.wait()
-            mix_copy.wait()
-            mix_t_copy.wait()
-
-        mu_copy.wait()
+
         nu_copy.wait()
 
         def turn_nu(p, _):
@@ -433,8 +460,13 @@
 
         receive_forward(0)
         lax.fori_loop(0, per, lambda sub, _: (apply_rows(0, sub), 0)[1], 0)
+
+        @pl.when(s == 0)
+        def _():
+            order_arrivals()
+
         receive_forward(1)
-        lax.fori_loop(0, per + 2 * LAG, chain, 0)
+        lax.fori_loop(0, per // 2 + 2 * LAG, chain, 0)
         for h in range(2):
             forward_sent(h)
         sum_products(0)
@@ -448,10 +480,19 @@
                 for j in range(1, states):
                     a_copy(h, j, sub).wait_send()
                     b_copy(h, j, sub).wait_send()
-            u_ref[pl.ds(pl.multiple_of(sub * size, size), size), :] = u_t[sub].T
             return 0
 
         lax.fori_loop(0, per, settle, 0)
+
+        @pl.when(s == sweeps - 1)
+        def _():
+            def turn_u(t, _):
+                for i in range(2):
+                    u_ref[2 * t + i] = u_t[t, :, i * size : (i + 1) * size].T
+                return 0
+
+            lax.fori_loop(0, per // 2, turn_u, 0)
+
         for h in range(2):
             receive_back(h)
             finish_all(h)
@@ -493,16 +534,17 @@
     potential_u, values = pl.pallas_call(
         functools.partial(solve_kernel, ITERS, peers, states),
         out_shape=(
-            jax.ShapeDtypeStruct((local_rows // states, nodes), F32),
+            jax.ShapeDtypeStruct((per, size, nodes), F32),
             jax.ShapeDtypeStruct((rows, size, cols), F32),
         ),
-        in_specs=[vmem()] + [smem()] * 3 + [hbm()] * 6,
+        in_specs=[vmem()] + [smem()] * 3 + [hbm()] * 5,
         out_specs=(vmem(), vmem()),
         scratch_shapes=[
             pltpu.VMEM((rows, degree, size, size), BF16),
             pltpu.VMEM((nodes, nodes), BF16),
             pltpu.VMEM((nodes, nodes), BF16),
-            pltpu.VMEM((per, nodes, size), F32),
+            pltpu.VMEM((per // 2, nodes, 2 * size), F32),
+            pltpu.VMEM((per // 2, nodes, 2 * size), F32),
             scratch(table_size),
             scratch(table_size),
             scratch(rows),
@@ -514,6 +556,7 @@
             scratch(2 * NEAR + nfar),
             scratch(nfar, dtype=F32),
             pltpu.VMEM((peers, 1, cols), jnp.int32),
+            pltpu.VMEM((peers, cols), jnp.int32),
             pltpu.SMEM((peers, 1, cols), jnp.int32),
             pltpu.SMEM((nfar,), jnp.int32),
             pltpu.SMEM((rows + 1,), jnp.int32),
@@ -534,10 +577,14 @@
         name="solve",
     )(
         want, sources, pair_perm, pair_last,
-        start_v.reshape(rows, size, cols), kern_blocks, state_kernel, state_kernel.T, mu,
+        start_v.reshape(rows, size, cols), kern_blocks, state_kernel,
+        mu.reshape(per, size, nodes),
         nu.reshape(rows, size, cols),
     )
-    return (potential_u, values.reshape(local_rows, cols))
+    return (
+        potential_u.reshape(local_rows // states, nodes),
+        values.reshape(local_rows, cols),
+    )
 
 
 def solution(mesh):

time: 194 us -> 193 us (level)
  local copies, waits for them, and re-layouts: 7.84 us -> 5.8 us
    unnamed x8 -> x7, local copies, waits for them, and re-layouts: 6.75 us -> 4.71 us
where the time goes in v6:
time: 193 us; the launch traced here: 192 us
  Pallas kernels  183 us (95%)
  local copies, waits for them, and re-layouts  5.8 us (3%)
  other arithmetic  2.66 us (1%)
    pallas_call x1, Pallas kernels, per_device(): pl.pallas_call(functools.partial(solve_kernel, ITERS, peers, states), out...  183 us
    unnamed x7, local copies, waits for them, and re-layouts  4.71 us

profile of v6, /device:TPU:1, one launch (start us, length us, event | category | flops | bytes accessed | tf_op | source)
XLA Modules:
  0.0 192.4 jit_solution(16798213332025330637)
XLA Ops:
  0.6 0.8 copy.15
  1.4 0.1 eq.112
  1.5 0.3 convert_reduce_fusion
  1.8 0.1 mul.83
  1.9 0.1 copy.16
  2.0 0.2 multiply_reduce_fusion
  2.1 0.1 copy.20
  2.2 0.1 mul.94
  2.3 0.4 select_reduce_fusion
  2.8 0.0 copy-start.1
  2.8 0.2 convert_reduce_fusion.1
  3.0 0.7 select_reduce_fusion.1.pair_perm
  3.7 0.1 fusion.1
  3.9 0.1 convert_reduce_fusion.2
  4.0 0.5 add_select_fusion.3.pair_last
  4.5 0.1 copy.19
  4.6 0.6 pad.4
  5.2 0.0 copy-done.1
  5.2 183.2 %solve.1 = (f32[6,128,512]{2,1,0:T(8,128)}, f32[24,128,128]{2,1,0:T(8,128)}) custom-call(s32[32,1,128]{2,1,0:T(1,128)} %bitcast.13, s32[384]{0:T(512)} %copy-done.1, s32[384]{0:T(512)} %select_reduce_fusion.1.pair_perm, s32[94]{0:T(128)} %add_select_fusion.3.pair_last, f32[24,128,128]{2,1,0:T(8,128)} %bitcast.8, bf16[24,16,128,128]{3,2,1,0:T(8,128)(2,1)} %kern_hbm.1, ...), custom_call_target="tpu_custom_call" | custom-call | tf_op jit(solution)/shard_map/solve/pallas_call | solution.py:534
  188.4 0.0 copy-start
  188.4 2.8 %copy.23 = f32[768,512]{1,0:T(8,128)} copy(f32[768,512]{1,0:T(8,128)} %bitcast.12) | data formatting | bytes 3145728
  191.2 0.0 copy-done
  191.2 1.1 copy.24
  (5 shorter events, 0.1 us)
Async XLA Ops:
  2.8 2.4 %copy-start.1 = (s32[384]{0:T(512)}, s32[384]{0:T(512)S(1)}, u32[]{:S(2)}) copy-start(s32[384]{0:T(512)S(1)} %get-tuple-element.9.src_ref) | copy-start | bytes 4612
  188.4 2.8 %copy-start = (f32[24,128,128]{2,1,0:T(8,128)S(1)}, f32[24,128,128]{2,1,0:T(8,128)}, u32[]{:S(2)}) copy-start(f32[24,128,128]{2,1,0:T(8,128)} %get-tuple-element.5) | copy-start | bytes 4718596

commit v7 on v6

--- a/solution.py
+++ b/solution.py
@@ -116,9 +116,9 @@
         q = lax.rem(me + o, peers)
         return pltpu.make_async_remote_copy(
             src_ref=want_ref.at[q],
-            dst_ref=inbox.at[me],
+            dst_ref=inbox.at[peers - o - 1],
             send_sem=ask_send.at[o],
-            recv_sem=ask_recv.at[o],
+            recv_sem=ask_recv,
             device_id={"mesh": q},
         )
 
@@ -126,12 +126,10 @@
         ask(o).start()
         return 0
 
-    def ask_wait(o, _):
-        ask(o).wait_recv()
+    def ask_sent(o, _):
         ask(o).wait_send()
         return 0
 
-    inbox[me] = want_ref[me]
     pl.semaphore_wait(barrier, peers - 1 + states - 1)
     lax.fori_loop(1, peers, ask_start, 0)
     start_copy.wait()
@@ -147,7 +145,13 @@
         return 0
 
     lax.fori_loop(0, rows, cast, 0)
-    lax.fori_loop(1, peers, ask_wait, 0)
+    pltpu.make_async_remote_copy(
+        src_ref=inbox,
+        dst_ref=inbox,
+        send_sem=ask_send.at[0],
+        recv_sem=ask_recv,
+        device_id={"mesh": right},
+    ).wait_recv()
     asked_copy = pltpu.make_async_copy(inbox, asked, local_sem.at[6])
     asked_copy.start()
     asked_copy.wait()
@@ -173,8 +177,8 @@
         return pltpu.make_async_remote_copy(
             src_ref=outbox.at[h, pl.ds(2 * NEAR + (o - 2) * FAR, FAR)],
             dst_ref=table[h].at[pl.ds(far0 + (at - 2) * FAR, FAR)],
-            send_sem=far_send.at[h, o],
-            recv_sem=far_recv.at[h, at],
+            send_sem=far_send.at[h],
+            recv_sem=far_recv.at[h],
             device_id={"mesh": lax.rem(me + o, peers)},
         )
 
@@ -192,8 +196,8 @@
         return pltpu.make_async_remote_copy(
             src_ref=outbox.at[h, pl.ds(2 * NEAR + (o - 2) * FAR, FAR)],
             dst_ref=arrived[h].at[pl.ds(2 * NEAR + (at - 2) * FAR, FAR)],
-            send_sem=back_far_send.at[h, o],
-            recv_sem=back_far_recv.at[h, at],
+            send_sem=back_far_send.at[h],
+            recv_sem=back_far_recv.at[h],
             device_id={"mesh": lax.rem(me + o, peers)},
         )
 
@@ -217,14 +221,31 @@
             device_id={"state": to},
         )
 
+    def all_far(h):
+        return pltpu.make_async_remote_copy(
+            src_ref=outbox.at[h, pl.ds(2 * NEAR, others * FAR)],
+            dst_ref=table[h].at[pl.ds(far0, others * FAR)],
+            send_sem=far_send.at[h],
+            recv_sem=far_recv.at[h],
+            device_id={"mesh": right},
+        )
+
+    def all_back(h):
+        return pltpu.make_async_remote_copy(
+            src_ref=outbox.at[h, pl.ds(2 * NEAR, others * FAR)],
+            dst_ref=arrived[h].at[pl.ds(2 * NEAR, others * FAR)],
+            send_sem=back_far_send.at[h],
+            recv_sem=back_far_recv.at[h],
+            device_id={"mesh": right},
+        )
+
     def send_forward(h):
         for k in range(2):
             fwd_near(h, k).start()
 
         def send(o):
-            q = lax.rem(me + o, peers)
             for f in range(FAR):
-                outbox[h, 2 * NEAR + (o - 2) * FAR + f] = blocks[h][asked[q, 0, f]]
+                outbox[h, 2 * NEAR + (o - 2) * FAR + f] = blocks[h][asked[o - 1, 0, f]]
             fwd_far(h, o).start()
 
         every(send)
@@ -232,12 +253,12 @@
     def receive_forward(h):
         for k in range(2):
             fwd_near(h, k).wait_recv()
-        every(lambda o: fwd_far(h, o).wait_recv())
+        all_far(h).wait_recv()
 
     def forward_sent(h):
         for k in range(2):
             fwd_near(h, k).wait_send()
-        every(lambda o: fwd_far(h, o).wait_send())
+        all_far(h).wait_send()
 
     def apply_rows(h, sub):
         for j in list(range(1, states)) + [0]:
@@ -346,7 +367,8 @@
     def send_back(h):
         def load(i):
             at = pair_last[rows + i]
-            outbox[h, i] = pick(sums[h, jnp.maximum(at, 0)], at).astype(BF16)
+            got = sums[h, jnp.maximum(at, 0)]
+            outbox[h, i] = jnp.where(at >= 0, got, jnp.zeros_like(got))
 
         def pack_near(i, _):
             load(i)
@@ -366,10 +388,10 @@
     def receive_back(h):
         for k in range(2):
             back_near(h, k).wait_recv()
-        every(lambda o: back_far(h, o).wait_recv())
+        all_back(h).wait_recv()
         for k in range(2):
             back_near(h, k).wait_send()
-        every(lambda o: back_far(h, o).wait_send())
+        all_back(h).wait_send()
 
     def finish_all(h):
         def add(i, carry):
@@ -401,15 +423,16 @@
 
     for h in range(2):
         send_forward(h)
+    lax.fori_loop(1, peers, ask_sent, 0)
 
     base = peers * FAR
 
     def order_arrivals():
-        for q in range(peers):
+        for q in range(peers - 1):
             packed[q, :] = inbox[q, 0, :]
-        peer_id = lax.broadcasted_iota(jnp.int32, packed.shape, 0)
+        packed[peers - 1, :] = jnp.zeros((packed.shape[1],), jnp.int32)
         lane = lax.broadcasted_iota(jnp.int32, packed.shape, 1)
-        ahead = lax.rem(peer_id - me + peers, peers)
+        ahead = lax.broadcasted_iota(jnp.int32, packed.shape, 0) + 1
         real = (lane < FAR) & (ahead >= 2) & (ahead <= peers - 2)
         beyond = rows * base
         keys = jnp.where(real, packed[...] * base + (ahead - 2) * FAR + lane, beyond)
@@ -555,9 +578,9 @@
             scratch(2 * NEAR + nfar),
             scratch(2 * NEAR + nfar),
             scratch(nfar, dtype=F32),
-            pltpu.VMEM((peers, 1, cols), jnp.int32),
+            pltpu.VMEM((peers - 1, 1, cols), jnp.int32),
             pltpu.VMEM((peers, cols), jnp.int32),
-            pltpu.SMEM((peers, 1, cols), jnp.int32),
+            pltpu.SMEM((peers - 1, 1, cols), jnp.int32),
             pltpu.SMEM((nfar,), jnp.int32),
             pltpu.SMEM((rows + 1,), jnp.int32),
             scratch(2, states, per),
@@ -565,11 +588,11 @@
             scratch(2, states, per),
             scratch(2, states, per),
             dma((7,)),
-            dma((2, 2)), dma((2, 2)), dma((2, peers)), dma((2, peers)),
-            dma((2, 2)), dma((2, 2)), dma((2, peers)), dma((2, peers)),
+            dma((2, 2)), dma((2, 2)), dma((2,)), dma((2,)),
+            dma((2, 2)), dma((2, 2)), dma((2,)), dma((2,)),
             dma((2, states, per)), dma((2, states, per)),
             dma((2, states, per)), dma((2, states, per)),
-            dma((peers,)), dma((peers,)),
+            dma((peers,)), dma,
         ],
         compiler_params=pltpu.CompilerParams(
             vmem_limit_bytes=VMEM_LIMIT, collective_id=0, has_side_effects=True

time: 193 us -> 187 us (0.969)
  Pallas kernels: 183 us -> 178 us
    pallas_call x1, Pallas kernels: 183 us -> 178 us  [per_device(): pl.pallas_call(functools.partial(solve_kernel, ITERS, peers, states), out...]
where the time goes in v7:
time: 187 us
  Pallas kernels  178 us (95%)
  local copies, waits for them, and re-layouts  5.8 us (3%)
  other arithmetic  2.66 us (1%)
    pallas_call x1, Pallas kernels, per_device(): pl.pallas_call(functools.partial(solve_kernel, ITERS, peers, states), out...  178 us
    unnamed x7, local copies, waits for them, and re-layouts  4.71 us

profile of v7, /device:TPU:1, one launch (start us, length us, event | category | flops | bytes accessed | tf_op | source)
XLA Modules:
  0.0 187.1 jit_solution(410065921693143219)
XLA Ops:
  0.6 0.8 copy.15
  1.4 0.1 eq.112
  1.5 0.3 convert_reduce_fusion
  1.8 0.1 mul.83
  1.9 0.1 copy.16
  2.0 0.2 multiply_reduce_fusion
  2.1 0.1 copy.20
  2.2 0.1 mul.94
  2.3 0.4 select_reduce_fusion
  2.8 0.0 copy-start.1
  2.8 0.2 convert_reduce_fusion.1
  3.0 0.7 select_reduce_fusion.1.pair_perm
  3.7 0.1 fusion.1
  3.9 0.1 convert_reduce_fusion.2
  4.0 0.5 add_select_fusion.3.pair_last
  4.5 0.1 copy.19
  4.6 0.6 pad.4
  5.2 0.0 copy-done.1
  5.2 177.9 %solve.1 = (f32[6,128,512]{2,1,0:T(8,128)}, f32[24,128,128]{2,1,0:T(8,128)}) custom-call(s32[32,1,128]{2,1,0:T(1,128)} %bitcast.13, s32[384]{0:T(512)} %copy-done.1, s32[384]{0:T(512)} %select_reduce_fusion.1.pair_perm, s32[94]{0:T(128)} %add_select_fusion.3.pair_last, f32[24,128,128]{2,1,0:T(8,128)} %bitcast.8, bf16[24,16,128,128]{3,2,1,0:T(8,128)(2,1)} %kern_hbm.1, ...), custom_call_target="tpu_custom_call" | custom-call | tf_op jit(solution)/shard_map/solve/pallas_call | solution.py:557
  183.1 0.0 copy-start
  183.2 2.8 %copy.23 = f32[768,512]{1,0:T(8,128)} copy(f32[768,512]{1,0:T(8,128)} %bitcast.12) | data formatting | bytes 3145728
  185.9 0.0 copy-done
  185.9 1.1 copy.24
  (5 shorter events, 0.1 us)
Async XLA Ops:
  2.8 2.4 %copy-start.1 = (s32[384]{0:T(512)}, s32[384]{0:T(512)S(1)}, u32[]{:S(2)}) copy-start(s32[384]{0:T(512)S(1)} %get-tuple-element.9.src_ref) | copy-start | bytes 4612
  183.1 2.8 %copy-start = (f32[24,128,128]{2,1,0:T(8,128)S(1)}, f32[24,128,128]{2,1,0:T(8,128)}, u32[]{:S(2)}) copy-start(f32[24,128,128]{2,1,0:T(8,128)} %get-tuple-element.5) | copy-start | bytes 4718596

commit v8 on v7

v8 whole, which is shorter than its diff:
```python
import functools
import jax
import jax.numpy as jnp
from jax import lax
from jax.experimental import pallas as pl
from jax.experimental.pallas import tpu as pltpu
from jax.sharding import PartitionSpec as P

ITERS = 2
NEAR = 6
FAR = 2
LAG = 1
VMEM_LIMIT = 60 * 1024 * 1024
F32 = jnp.float32
BF16 = jnp.bfloat16


def vmem():
    return pl.BlockSpec(memory_space=pltpu.VMEM)


def smem():
    return pl.BlockSpec(memory_space=pltpu.SMEM)


def hbm():
    return pl.BlockSpec(memory_space=pl.ANY)


def far_plan(flat_cols, me, peers, rows):
    owners = flat_cols // rows
    places = flat_cols % rows
    delta = (owners - me + peers) % peers
    is_own = delta == 0
    is_left = delta == peers - 1
    is_right = delta == 1
    is_far = ~(is_own | is_left | is_right)
    ids = jnp.arange(peers * rows, dtype=jnp.int32)
    hits = (flat_cols[:, None] == ids[None, :]) & is_far[:, None]
    needed = jnp.max(hits.astype(jnp.int32), axis=0).reshape(peers, rows)
    before = jnp.arange(rows)[:, None] < jnp.arange(rows)[None, :]
    ranks = jnp.sum(needed[:, :, None] * before[None].astype(jnp.int32), axis=1)
    place_ids = jnp.arange(rows, dtype=jnp.int32)
    requests = jnp.stack(
        [jnp.sum(needed * (ranks == s) * place_ids[None, :], axis=1) for s in range(FAR)],
        axis=1,
    )
    slots = jnp.sum(hits.astype(jnp.int32) * ranks.reshape(1, -1), axis=1)
    far_at = rows + 2 * NEAR + (delta - 2) * FAR + slots
    sources = jnp.where(
        is_own,
        places,
        jnp.where(
            is_left,
            rows + places - (rows - NEAR),
            jnp.where(is_right, rows + NEAR + places, far_at),
        ),
    )
    return sources.astype(jnp.int32), requests.astype(jnp.int32)


def ordered_sums(keys, bins):
    count = keys.shape[0]
    ids = jnp.arange(count, dtype=jnp.int32)
    full = keys * count + ids
    rank = jnp.sum((full[None, :] < full[:, None]).astype(jnp.int32), axis=1)
    here = (rank[:, None] == ids[None, :]).astype(jnp.int32)
    perm = jnp.sum(here * ids[:, None], axis=0)
    bin_ids = jnp.arange(bins, dtype=jnp.int32)[:, None]
    upto = jnp.sum((keys[None, :] <= bin_ids).astype(jnp.int32), axis=1)
    some = jnp.any(keys[None, :] == bin_ids, axis=1)
    return perm, jnp.where(some, upto - 1, -1)


def solve_kernel(
    sweeps, peers, states,
    want_ref, src_ref, pair_perm, pair_last,
    start_hbm, kern_hbm, mix_hbm, mu_hbm, nu_hbm,
    u_ref, v_ref,
    kern, mix, mix_t, mu_t, nu_t, u_t, table_0, table_1, blocks_0, blocks_1, outbox, products, sums,
    arrived_0, arrived_1, running, inbox, packed, asked, arr_key, arr_count,
    a_out, a_in, b_out, b_in,
    local_sem, near_send, near_recv, far_send, far_recv,
    back_near_send, back_near_recv, back_far_send, back_far_recv,
    a_send, a_recv, b_send, b_recv, c_send, c_recv, ask_send, ask_recv,
):
    me = lax.axis_index("mesh")
    mz = lax.axis_index("state")
    rows, degree, size, _ = kern.shape
    table, blocks, arrived = (table_0, table_1), (blocks_0, blocks_1), (arrived_0, arrived_1)
    half = table_0.shape[1]
    per = rows // states
    far0 = rows + 2 * NEAR
    others = peers - 3
    right = lax.rem(me + 1, peers)
    left = lax.rem(me + peers - 1, peers)

    kern_copy = pltpu.make_async_copy(kern_hbm, kern, local_sem.at[0])
    mix_copy = pltpu.make_async_copy(mix_hbm, mix, local_sem.at[1])
    mu_copy = pltpu.make_async_copy(mu_hbm, u_ref, local_sem.at[3])
    nu_copy = pltpu.make_async_copy(nu_hbm, v_ref, local_sem.at[4])
    start_copy = pltpu.make_async_copy(start_hbm, v_ref, local_sem.at[5])
    start_copy.start()

    barrier = pltpu.get_barrier_semaphore()

    def greet(o, _):
        pl.semaphore_signal(barrier, inc=1, device_id={"mesh": lax.rem(me + o, peers)})
        return 0

    lax.fori_loop(1, peers, greet, 0)
    for j in range(1, states):
        pl.semaphore_signal(barrier, inc=1, device_id={"state": lax.rem(mz + j, states)})

    def ask(o):
        q = lax.rem(me + o, peers)
        return pltpu.make_async_remote_copy(
            src_ref=want_ref.at[q],
            dst_ref=inbox.at[peers - o - 1],
            send_sem=ask_send.at[o],
            recv_sem=ask_recv,
            device_id={"mesh": q},
        )

    def ask_start(o, _):
        ask(o).start()
        return 0

    def ask_sent(o, _):
        ask(o).wait_send()
        return 0

    pl.semaphore_wait(barrier, peers - 1 + states - 1)
    lax.fori_loop(1, peers, ask_start, 0)
    start_copy.wait()
    kern_copy.start()
    mix_copy.start()
    mu_copy.start()

    def cast(p, _):
        v = v_ref[p].astype(BF16).T
        for h in range(2):
            table[h][p] = v[h * half : (h + 1) * half]
            blocks[h][p] = v[h * half : (h + 1) * half]
        return 0

    lax.fori_loop(0, rows, cast, 0)
    def every(body):
        def one(i, _):
            body(2 + lax.rem(i * 12, others))
            return 0

        lax.fori_loop(0, others, one, 0)

    def fwd_near(h, k):
        return pltpu.make_async_remote_copy(
            src_ref=blocks[h].at[pl.ds((rows - NEAR, 0)[k], NEAR)],
            dst_ref=table[h].at[pl.ds(rows + k * NEAR, NEAR)],
            send_sem=near_send.at[h, k],
            recv_sem=near_recv.at[h, k],
            device_id={"mesh": (right, left)[k]},
        )

    def fwd_far(h, o):
        at = peers - o
        return pltpu.make_async_remote_copy(
            src_ref=outbox.at[h, pl.ds(2 * NEAR + (o - 2) * FAR, FAR)],
            dst_ref=table[h].at[pl.ds(far0 + (at - 2) * FAR, FAR)],
            send_sem=far_send.at[h],
            recv_sem=far_recv.at[h],
            device_id={"mesh": lax.rem(me + o, peers)},
        )

    def back_near(h, k):
        return pltpu.make_async_remote_copy(
            src_ref=outbox.at[h, pl.ds(k * NEAR, NEAR)],
            dst_ref=arrived[h].at[pl.ds(k * NEAR, NEAR)],
            send_sem=back_near_send.at[h, k],
            recv_sem=back_near_recv.at[h, k],
            device_id={"mesh": (left, right)[k]},
        )

    def back_far(h, o):
        at = peers - o
        return pltpu.make_async_remote_copy(
            src_ref=outbox.at[h, pl.ds(2 * NEAR + (o - 2) * FAR, FAR)],
            dst_ref=arrived[h].at[pl.ds(2 * NEAR + (at - 2) * FAR, FAR)],
            send_sem=back_far_send.at[h],
            recv_sem=back_far_recv.at[h],
            device_id={"mesh": lax.rem(me + o, peers)},
        )

    def a_copy(h, j, t):
        to = lax.rem(mz + j, states)
        return pltpu.make_async_remote_copy(
            src_ref=a_out.at[h, to, pl.ds(2 * t, 2)],
            dst_ref=a_in.at[h, mz, pl.ds(2 * t, 2)],
            send_sem=a_send.at[h, j, t],
            recv_sem=a_recv.at[h, j, t],
            device_id={"state": to},
        )

    def b_copy(j, t):
        to = lax.rem(mz + j, states)
        return pltpu.make_async_remote_copy(
            src_ref=b_out.at[0, to, pl.ds(2 * t, 2)],
            dst_ref=b_in.at[0, mz, pl.ds(2 * t, 2)],
            send_sem=b_send.at[j, t],
            recv_sem=b_recv.at[j, t],
            device_id={"state": to},
        )

    def b_rest(j):
        to = lax.rem(mz + j, states)
        return pltpu.make_async_remote_copy(
            src_ref=b_out.at[1, to],
            dst_ref=b_in.at[1, mz],
            send_sem=c_send.at[j],
            recv_sem=c_recv.at[j],
            device_id={"state": to},
        )

    def all_far(h):
        return pltpu.make_async_remote_copy(
            src_ref=outbox.at[h, pl.ds(2 * NEAR, others * FAR)],
            dst_ref=table[h].at[pl.ds(far0, others * FAR)],
            send_sem=far_send.at[h],
            recv_sem=far_recv.at[h],
            device_id={"mesh": right},
        )

    def all_back(h):
        return pltpu.make_async_remote_copy(
            src_ref=outbox.at[h, pl.ds(2 * NEAR, others * FAR)],
            dst_ref=arrived[h].at[pl.ds(2 * NEAR, others * FAR)],
            send_sem=back_far_send.at[h],
            recv_sem=back_far_recv.at[h],
            device_id={"mesh": right},
        )

    def send_near(h):
        for k in range(2):
            fwd_near(h, k).start()

    def send_far(h):
        def send(o):
            for f in range(FAR):
                outbox[h, 2 * NEAR + (o - 2) * FAR + f] = blocks[h][asked[o - 1, 0, f]]
            fwd_far(h, o).start()

        every(send)

    def receive_forward(h):
        for k in range(2):
            fwd_near(h, k).wait_recv()
        all_far(h).wait_recv()

    def forward_sent(h):
        for k in range(2):
            fwd_near(h, k).wait_send()
        all_far(h).wait_send()

    def apply_rows(h, t):
        for j in list(range(1, states)) + [0]:
            to = lax.rem(mz + j, states)
            for i in range(2):
                sub = 2 * t + i
                r = to * per + sub
                lhs = jnp.concatenate(
                    [table[h][src_ref[r * degree + k]] for k in range(degree)], axis=1
                )
                rhs = jnp.concatenate([kern[r, k] for k in range(degree)], axis=1)
                out = lax.dot_general(
                    lhs, rhs, (((1,), (1,)), ((), ())), preferred_element_type=F32
                ).astype(BF16)
                if j == 0:
                    a_in[h, mz, sub] = out
                else:
                    a_out[h, to, sub] = out
            if j > 0:
                a_copy(h, j, t).start()

    def mix_rows(t):
        for h in range(2):
            for j in range(1, states):
                a_copy(h, j, t).wait_recv()
        a = jnp.concatenate(
            [
                jnp.concatenate([a_in[h, z, 2 * t + i] for i in range(2)], axis=1)
                for z in range(states)
                for h in range(2)
            ],
            axis=0,
        )
        kv = jnp.dot(mix[...], a, preferred_element_type=F32)
        u = mu_t[t] / kv
        u_t[t] = u
        b = jnp.dot(mix_t[...], u.astype(BF16), preferred_element_type=F32).astype(BF16)
        for i in range(2):
            for z in range(states):
                for h in range(2):
                    b_out[h, z, 2 * t + i] = b[
                        (2 * z + h) * half : (2 * z + h + 1) * half, i * size : (i + 1) * size
                    ]
        for j in range(1, states):
            b_copy(j, t).start()
        for i in range(2):
            for h in range(2):
                b_in[h, mz, 2 * t + i] = b_out[h, mz, 2 * t + i]

    def product_rows(h, sub):
        for z in range(states):
            r = z * per + sub
            b = b_in[h, z, sub]
            for k in range(0, degree, 2):
                rhs = jnp.concatenate([kern[r, k], kern[r, k + 1]], axis=1)
                both = jnp.dot(b, rhs, preferred_element_type=F32)
                products[r * degree + k] = both[:, :size]
                products[r * degree + k + 1] = both[:, size:]

    def chain(t, _):
        steps = per // 2

        @pl.when(t < steps)
        def _():
            apply_rows(1, t)

        @pl.when((t >= LAG) & (t < steps + LAG))
        def _():
            mix_rows(t - LAG)

        @pl.when(t == steps + LAG - 1)
        def _():
            for j in range(1, states):
                b_rest(j).start()

        @pl.when(t >= 2 * LAG)
        def _():
            for j in range(1, states):
                b_copy(j, t - 2 * LAG).wait_recv()
            for i in range(2):
                product_rows(0, 2 * (t - 2 * LAG) + i)

        return 0

    def zeros():
        return jnp.zeros((half, size), F32)

    def pick(got, at):
        return jnp.where(at >= 0, got.astype(F32), zeros())

    def sum_products(h):
        def add(i, carry):
            acc, before = carry
            for g in range(8):
                p = pair_perm[i * 8 + g]
                now = src_ref[p]
                acc = jnp.where(now == before, acc, zeros()) + products[p]
                sums[h, i * 8 + g] = acc.astype(BF16)
                before = now
            return acc, before

        lax.fori_loop(0, rows * degree // 8, add, (zeros(), jnp.int32(-1)))

    def send_back(h):
        def load(i):
            at = pair_last[rows + i]
            got = sums[h, jnp.maximum(at, 0)]
            outbox[h, i] = jnp.where(at >= 0, got, jnp.zeros_like(got))

        def pack_near(i, _):
            load(i)
            return 0

        lax.fori_loop(0, 2 * NEAR, pack_near, 0)
        for k in range(2):
            back_near(h, k).start()

        def give(o):
            for f in range(FAR):
                load(2 * NEAR + (o - 2) * FAR + f)
            back_far(h, o).start()

        every(give)

    def receive_back(h):
        for k in range(2):
            back_near(h, k).wait_recv()
        all_back(h).wait_recv()
        for k in range(2):
            back_near(h, k).wait_send()
        all_back(h).wait_send()

    def finish_all(h, ending):
        def add(i, carry):
            acc, before = carry
            e = lax.rem(arr_key[i], base)
            now = arr_key[i] // base
            acc = jnp.where(now == before, acc, zeros()) + arrived[h][2 * NEAR + e].astype(F32)
            running[i] = acc
            return acc, now

        lax.fori_loop(0, others * FAR, add, (zeros(), jnp.int32(-1)))

        def finish(p, near):
            at = pair_last[p]
            far = jnp.where(arr_count[p + 1] > arr_count[p], arr_count[p + 1] - 1, -1)
            total = pick(sums[h, jnp.maximum(at, 0)], at) + pick(running[jnp.maximum(far, 0)], far)
            if near is not None:
                total = total + arrived[h][near].astype(F32)
            v = nu_t[p, h * half : (h + 1) * half] / total
            if ending:
                v_ref[p, :, h * half : (h + 1) * half] = v.T
            else:
                rounded = v.astype(BF16)
                table[h][p] = rounded
                blocks[h][p] = rounded
            return 0

        lax.fori_loop(0, NEAR, lambda p, _: finish(p, NEAR + p), 0)
        lax.fori_loop(NEAR, rows - NEAR, lambda p, _: finish(p, None), 0)
        lax.fori_loop(rows - NEAR, rows, lambda p, _: finish(p, p - (rows - NEAR)), 0)

    for h in range(2):
        send_near(h)
    pltpu.make_async_remote_copy(
        src_ref=inbox,
        dst_ref=inbox,
        send_sem=ask_send.at[0],
        recv_sem=ask_recv,
        device_id={"mesh": right},
    ).wait_recv()
    asked_copy = pltpu.make_async_copy(inbox, asked, local_sem.at[6])
    asked_copy.start()
    asked_copy.wait()
    for h in range(2):
        send_far(h)
    lax.fori_loop(1, peers, ask_sent, 0)

    base = peers * FAR

    def order_arrivals():
        for q in range(peers - 1):
            packed[q, :] = inbox[q, 0, :]
        packed[peers - 1, :] = jnp.zeros((packed.shape[1],), jnp.int32)
        lane = lax.broadcasted_iota(jnp.int32, packed.shape, 1)
        ahead = lax.broadcasted_iota(jnp.int32, packed.shape, 0) + 1
        real = (lane < FAR) & (ahead >= 2) & (ahead <= peers - 2)
        beyond = rows * base
        keys = jnp.where(real, packed[...] * base + (ahead - 2) * FAR + lane, beyond)

        def next_key(i, last):
            key = jnp.min(jnp.where(keys > last, keys, beyond))
            arr_key[i] = key
            return key

        lax.fori_loop(0, others * FAR, next_key, jnp.int32(-1))
        arr_count[0] = 0

        def count(i, _):
            for g in range(4):
                p = i * 4 + g + 1
                arr_count[p] = jnp.sum((keys < p * base).astype(jnp.int32))
            return 0

        lax.fori_loop(0, rows // 4, count, 0)

    def sweep(s, _):
        @pl.when(s == 0)
        def _():
            nu_copy.start()
            mix_copy.wait()
            mu_copy.wait()
            for i in range(states):
                for j in range(states):
                    a, b = slice(i * size, (i + 1) * size), slice(j * size, (j + 1) * size)
                    mix_t[a, b] = mix[b, a].T

            def turn_mu(t, _):
                for i in range(2):
                    mu_t[t, :, i * size : (i + 1) * size] = u_ref[2 * t + i].T
                return 0

            lax.fori_loop(0, per // 2, turn_mu, 0)
            nu_copy.wait()

            def turn_nu(p, _):
                nu_t[p] = v_ref[p].T
                return 0

            lax.fori_loop(0, rows, turn_nu, 0)
            kern_copy.wait()

        receive_forward(0)
        lax.fori_loop(0, per // 2, lambda t, _: (apply_rows(0, t), 0)[1], 0)

        @pl.when(s == 0)
        def _():
            order_arrivals()

        receive_forward(1)
        lax.fori_loop(0, per // 2 + 2 * LAG, chain, 0)
        for h in range(2):
            forward_sent(h)
        sum_products(0)
        send_back(0)
        for j in range(1, states):
            b_rest(j).wait_recv()
        lax.fori_loop(0, per, lambda sub, _: (product_rows(1, sub), 0)[1], 0)
        sum_products(1)
        send_back(1)

        for j in range(1, states):
            for t in range(per // 2):
                for h in range(2):
                    a_copy(h, j, t).wait_send()
                b_copy(j, t).wait_send()
            b_rest(j).wait_send()

        @pl.when(s == sweeps - 1)
        def _():
            def turn_u(t, _):
                for i in range(2):
                    u_ref[2 * t + i] = u_t[t, :, i * size : (i + 1) * size].T
                return 0

            lax.fori_loop(0, per // 2, turn_u, 0)

        for h in range(2):
            receive_back(h)

            @pl.when(s == sweeps - 1)
            def _():
                finish_all(h, True)

            @pl.when(s < sweeps - 1)
            def _():
                finish_all(h, False)
                send_near(h)
                send_far(h)

        return 0

    lax.fori_loop(0, sweeps, sweep, 0)


def per_device(kern_blocks, kern_cols, state_kernel, start_v, mu, nu):
    rows, degree, size, _ = kern_blocks.shape
    local_rows, cols = start_v.shape
    peers = lax.axis_size("mesh")
    states = lax.axis_size("state")
    me = lax.axis_index("mesh")
    per = rows // states
    nfar = (peers - 3) * FAR
    table_size = rows + 2 * NEAR + nfar
    nodes = states * cols
    dma = pltpu.SemaphoreType.DMA
    sources, requests = far_plan(kern_cols.reshape(-1), me, peers, rows)
    want = jnp.pad(requests, ((0, 0), (0, cols - FAR))).reshape(peers, 1, cols)
    pair_perm, pair_last = ordered_sums(sources, table_size)
    half = cols // 2

    def scratch(*dims, dtype=BF16):
        return pltpu.VMEM(dims + (half, size), dtype)

    potential_u, values = pl.pallas_call(
        functools.partial(solve_kernel, ITERS, peers, states),
        out_shape=(
            jax.ShapeDtypeStruct((per, size, nodes), F32),
            jax.ShapeDtypeStruct((rows, size, cols), F32),
        ),
        in_specs=[vmem()] + [smem()] * 3 + [hbm()] * 5,
        out_specs=(vmem(), vmem()),
        scratch_shapes=[
            pltpu.VMEM((rows, degree, size, size), BF16),
            pltpu.VMEM((nodes, nodes), BF16),
            pltpu.VMEM((nodes, nodes), BF16),
            pltpu.VMEM((per // 2, nodes, 2 * size), F32),
            pltpu.VMEM((rows, cols, size), F32),
            pltpu.VMEM((per // 2, nodes, 2 * size), F32),
            scratch(table_size),
            scratch(table_size),
            scratch(rows),
            scratch(rows),
            scratch(2, 2 * NEAR + nfar),
            scratch(rows * degree, dtype=F32),
            scratch(2, rows * degree),
            scratch(2 * NEAR + nfar),
            scratch(2 * NEAR + nfar),
            scratch(nfar, dtype=F32),
            pltpu.VMEM((peers - 1, 1, cols), jnp.int32),
            pltpu.VMEM((peers, cols), jnp.int32),
            pltpu.SMEM((peers - 1, 1, cols), jnp.int32),
            pltpu.SMEM((nfar,), jnp.int32),
            pltpu.SMEM((rows + 1,), jnp.int32),
            scratch(2, states, per),
            scratch(2, states, per),
            scratch(2, states, per),
            scratch(2, states, per),
            dma((7,)),
            dma((2, 2)), dma((2, 2)), dma((2,)), dma((2,)),
            dma((2, 2)), dma((2, 2)), dma((2,)), dma((2,)),
            dma((2, states, per // 2)), dma((2, states, per // 2)),
            dma((states, per // 2)), dma((states, per // 2)),
            dma((states,)), dma((states,)),
            dma((peers,)), dma,
        ],
        compiler_params=pltpu.CompilerParams(
            vmem_limit_bytes=VMEM_LIMIT, collective_id=0, has_side_effects=True
        ),
        name="solve",
    )(
        want, sources, pair_perm, pair_last,
        start_v.reshape(rows, size, cols), kern_blocks, state_kernel,
        mu.reshape(per, size, nodes),
        nu.reshape(rows, size, cols),
    )
    return (
        potential_u.reshape(local_rows // states, nodes),
        values.reshape(local_rows, cols),
    )


def solution(mesh):
    placed = (
        P("mesh", None, None, None),
        P("mesh", None),
        P(),
        P("mesh", "state"),
        P(("mesh", "state"), None),
        P("mesh", "state"),
    )
    return jax.shard_map(
        per_device,
        mesh=mesh,
        in_specs=placed,
        out_specs=(P(("mesh", "state"), None), P("mesh", "state")),
        check_vma=False,
    )
```

time: 187 us -> 178 us (0.952)
  Pallas kernels: 178 us -> 167 us
    pallas_call x1, Pallas kernels: 178 us -> 167 us  [per_device(): pl.pallas_call(functools.partial(solve_kernel, ITERS, peers, states), out...]
where the time goes in v8:
time: 178 us; the launch traced here: 176 us
  Pallas kernels  167 us (94%)
  local copies, waits for them, and re-layouts  5.8 us (3%)
  other arithmetic  2.66 us (1%)
    pallas_call x1, Pallas kernels, per_device(): pl.pallas_call(functools.partial(solve_kernel, ITERS, peers, states), out...  167 us
    unnamed x7, local copies, waits for them, and re-layouts  4.71 us

profile of v8, /device:TPU:1, one launch (start us, length us, event | category | flops | bytes accessed | tf_op | source)
XLA Modules:
  0.0 176.5 jit_solution(1258854370396291179)
XLA Ops:
  0.6 0.8 copy.15
  1.4 0.1 eq.112
  1.5 0.3 convert_reduce_fusion
  1.8 0.1 mul.83
  1.9 0.1 copy.16
  2.0 0.2 multiply_reduce_fusion
  2.1 0.1 copy.20
  2.2 0.1 mul.94
  2.3 0.4 select_reduce_fusion
  2.8 0.0 copy-start.1
  2.8 0.2 convert_reduce_fusion.1
  3.0 0.7 select_reduce_fusion.1.pair_perm
  3.7 0.1 fusion.1
  3.9 0.1 convert_reduce_fusion.2
  4.0 0.5 add_select_fusion.3.pair_last
  4.5 0.1 copy.19
  4.6 0.6 pad.4
  5.2 0.0 copy-done.1
  5.2 167.3 %solve.1 = (f32[6,128,512]{2,1,0:T(8,128)}, f32[24,128,128]{2,1,0:T(8,128)}) custom-call(s32[32,1,128]{2,1,0:T(1,128)} %bitcast.13, s32[384]{0:T(512)} %copy-done.1, s32[384]{0:T(512)} %select_reduce_fusion.1.pair_perm, s32[94]{0:T(128)} %add_select_fusion.3.pair_last, f32[24,128,128]{2,1,0:T(8,128)} %bitcast.8, bf16[24,16,128,128]{3,2,1,0:T(8,128)(2,1)} %kern_hbm.1, ...), custom_call_target="tpu_custom_call" | custom-call | tf_op jit(solution)/shard_map/solve/pallas_call | solution.py:566
  172.5 0.0 copy-start
  172.5 2.8 %copy.23 = f32[768,512]{1,0:T(8,128)} copy(f32[768,512]{1,0:T(8,128)} %bitcast.12) | data formatting | bytes 3145728
  175.3 0.0 copy-done
  175.3 1.1 copy.24
  (5 shorter events, 0.1 us)
Async XLA Ops:
  2.8 2.4 %copy-start.1 = (s32[384]{0:T(512)}, s32[384]{0:T(512)S(1)}, u32[]{:S(2)}) copy-start(s32[384]{0:T(512)S(1)} %get-tuple-element.9.src_ref) | copy-start | bytes 4612
  172.5 2.8 %copy-start = (f32[24,128,128]{2,1,0:T(8,128)S(1)}, f32[24,128,128]{2,1,0:T(8,128)}, u32[]{:S(2)}) copy-start(f32[24,128,128]{2,1,0:T(8,128)} %get-tuple-element.5) | copy-start | bytes 4718596

commit v9 on v8

--- a/solution.py
+++ b/solution.py
@@ -280,19 +280,25 @@
             if j > 0:
                 a_copy(h, j, t).start()
 
-    def mix_rows(t):
-        for h in range(2):
-            for j in range(1, states):
-                a_copy(h, j, t).wait_recv()
+    def mix_half(h, t):
+        for j in range(1, states):
+            a_copy(h, j, t).wait_recv()
         a = jnp.concatenate(
             [
                 jnp.concatenate([a_in[h, z, 2 * t + i] for i in range(2)], axis=1)
                 for z in range(states)
-                for h in range(2)
             ],
             axis=0,
         )
-        kv = jnp.dot(mix[...], a, preferred_element_type=F32)
+        wide = states * half
+        return jnp.dot(mix[:, h * wide : (h + 1) * wide], a, preferred_element_type=F32)
+
+    def mix_first(t, _):
+        u_t[t] = mix_half(0, t)
+        return 0
+
+    def mix_rows(t):
+        kv = u_t[t] + mix_half(1, t)
         u = mu_t[t] / kv
         u_t[t] = u
         b = jnp.dot(mix_t[...], u.astype(BF16), preferred_element_type=F32).astype(BF16)
@@ -352,15 +358,15 @@
     def sum_products(h):
         def add(i, carry):
             acc, before = carry
-            for g in range(8):
-                p = pair_perm[i * 8 + g]
+            for g in range(16):
+                p = pair_perm[i * 16 + g]
                 now = src_ref[p]
                 acc = jnp.where(now == before, acc, zeros()) + products[p]
-                sums[h, i * 8 + g] = acc.astype(BF16)
+                sums[h, i * 16 + g] = acc.astype(BF16)
                 before = now
             return acc, before
 
-        lax.fori_loop(0, rows * degree // 8, add, (zeros(), jnp.int32(-1)))
+        lax.fori_loop(0, rows * degree // 16, add, (zeros(), jnp.int32(-1)))
 
     def send_back(h):
         def load(i):
@@ -475,6 +481,11 @@
                 for j in range(states):
                     a, b = slice(i * size, (i + 1) * size), slice(j * size, (j + 1) * size)
                     mix_t[a, b] = mix[b, a].T
+            for h in range(2):
+                for z in range(0, states, 2):
+                    two = [mix_t[(2 * (z + i) + h) * half : (2 * (z + i) + h + 1) * half] for i in range(2)]
+                    at = (h * states + z) * half
+                    mix[:, at : at + 2 * half] = jnp.concatenate(two, axis=0).T
 
             def turn_mu(t, _):
                 for i in range(2):
@@ -498,6 +509,7 @@
         def _():
             order_arrivals()
 
+        lax.fori_loop(0, per // 2, mix_first, 0)
         receive_forward(1)
         lax.fori_loop(0, per // 2 + 2 * LAG, chain, 0)
         for h in range(2):

time: 178 us -> 180 us (1.011)
  the two profiles are of different devices: /device:TPU:1 before, /device:TPU:4 now
where the time goes in v9:
time: 180 us
  Pallas kernels  171 us (95%)
  local copies, waits for them, and re-layouts  5.8 us (3%)
  other arithmetic  2.66 us (1%)
    pallas_call x1, Pallas kernels, per_device(): pl.pallas_call(functools.partial(solve_kernel, ITERS, peers, states), out...  171 us
    unnamed x7, local copies, waits for them, and re-layouts  4.71 us

profile of v9, /device:TPU:4, one launch (start us, length us, event | category | flops | bytes accessed | tf_op | source)
XLA Modules:
  0.0 179.8 jit_solution(10496334487274132719)
XLA Ops:
  0.6 0.8 copy.15
  1.4 0.1 eq.112
  1.5 0.3 convert_reduce_fusion
  1.8 0.1 mul.83
  1.9 0.1 copy.16
  2.0 0.2 multiply_reduce_fusion
  2.1 0.1 copy.20
  2.2 0.1 mul.94
  2.3 0.4 select_reduce_fusion
  2.8 0.0 copy-start.1
  2.8 0.2 convert_reduce_fusion.1
  3.0 0.7 select_reduce_fusion.1.pair_perm
  3.7 0.1 fusion.1
  3.9 0.1 convert_reduce_fusion.2
  4.0 0.5 add_select_fusion.3.pair_last
  4.5 0.1 copy.19
  4.6 0.6 pad.4
  5.2 0.0 copy-done.1
  5.2 170.6 %solve.1 = (f32[6,128,512]{2,1,0:T(8,128)}, f32[24,128,128]{2,1,0:T(8,128)}) custom-call(s32[32,1,128]{2,1,0:T(1,128)} %bitcast.13, s32[384]{0:T(512)} %copy-done.1, s32[384]{0:T(512)} %select_reduce_fusion.1.pair_perm, s32[94]{0:T(128)} %add_select_fusion.3.pair_last, f32[24,128,128]{2,1,0:T(8,128)} %bitcast.8, bf16[24,16,128,128]{3,2,1,0:T(8,128)(2,1)} %kern_hbm.1, ...), custom_call_target="tpu_custom_call" | custom-call | tf_op jit(solution)/shard_map/solve/pallas_call | solution.py:578
  175.8 0.0 copy-start
  175.9 2.8 %copy.23 = f32[768,512]{1,0:T(8,128)} copy(f32[768,512]{1,0:T(8,128)} %bitcast.12) | data formatting | bytes 3145728
  178.6 0.0 copy-done
  178.6 1.1 copy.24
  (5 shorter events, 0.1 us)
Async XLA Ops:
  2.8 2.4 %copy-start.1 = (s32[384]{0:T(512)}, s32[384]{0:T(512)S(1)}, u32[]{:S(2)}) copy-start(s32[384]{0:T(512)S(1)} %get-tuple-element.9.src_ref) | copy-start | bytes 4612
  175.8 2.8 %copy-start = (f32[24,128,128]{2,1,0:T(8,128)S(1)}, f32[24,128,128]{2,1,0:T(8,128)}, u32[]{:S(2)}) copy-start(f32[24,128,128]{2,1,0:T(8,128)} %get-tuple-element.5) | copy-start | bytes 4718596
